TPU v7x, 32 devices: a whole 2x2x4 slice. The times are simulated.
32 devices in a mesh: rows: 16 (over z, x, core), mlp: 2 (over y).
Axes of the slice: x: 2, y: 2, z: 4, core: 2. Of those that a mesh axis runs over, the one named last changes fastest.
Arguments:
- tokens: bfloat16 [65536, 512], P(('rows', 'mlp')), may hold values from -6 to 6
- segment_ids: int32 [512, 128], P(('rows', 'mlp')), may hold values from 0 to 7, never falling along the last dimension, each value on 1 to 64 neighbouring positions
- ln1_gain: bfloat16 [512], replicated, may hold values from 0.099609375 to 1.8984375
- ln1_bias: bfloat16 [512], replicated, may hold values from -3 to 3
- qkv_weight: bfloat16 [512, 1536], replicated, may hold values from -0.25 to 0.25
- qv_bias: bfloat16 [2, 512], replicated, may hold values from -3 to 3
- out_weight: bfloat16 [512, 512], replicated, may hold values from -1 to 1
- out_bias: bfloat16 [512], replicated, may hold values from -3 to 3
- ln2_gain: bfloat16 [512], replicated, may hold values from 0.099609375 to 1.8984375
- ln2_bias: bfloat16 [512], replicated, may hold values from -3 to 3
- up_weight: bfloat16 [512, 2048], P(None, 'mlp'), may hold values from -0.25 to 0.25
- up_bias: bfloat16 [2048], P('mlp'), may hold values from -3 to 3
- down_weight: bfloat16 [2048, 512], P('mlp'), may hold values from -0.125 to 0.125
- down_bias: bfloat16 [512], replicated, may hold values from -3 to 3
- out_grad: bfloat16 [65536, 512], P(('rows', 'mlp')), may hold values from -6 to 6
Outputs:
- layer_out: bfloat16 [65536, 512], P(('rows', 'mlp'))
- in_grad: bfloat16 [65536, 512], P(('rows', 'mlp'))
- grad_ln1_gain: float32 [512], replicated
- grad_ln1_bias: float32 [512], replicated
- grad_qkv_weight: float32 [512, 1536], replicated
- grad_qv_bias: float32 [2, 512], replicated
- grad_out_weight: float32 [512, 512], replicated
- grad_out_bias: float32 [512], replicated
- grad_ln2_gain: float32 [512], replicated
- grad_ln2_bias: float32 [512], replicated
- grad_up_weight: float32 [512, 2048], P(None, 'mlp')
- grad_up_bias: float32 [2048], P('mlp')
- grad_down_weight: float32 [2048, 512], P('mlp')
- grad_down_bias: float32 [512], replicated
Inputs may be any that keep to these rules, and one draw needn't show every extreme that they name: `segment_ids`: within each packed row the ids never fall; each episode fragment holds 1 to 64 tokens, and some fragment holds exactly 64.
All inputs are finite; a program needn't handle non-finite values.
Results may differ from a plain program's by a relative error of at most 0.011.
Values may be sent and summed in bfloat16 or wider, within the bound.
No kernel may reach another device: no remote copies, remote signals or barrier semaphores. Data moves between devices by JAX's collectives and lax.ppermute only.
A program may use at most 192 MiB of HBM per device.

v0:
```python
import math

import jax
import jax.numpy as jnp
from jax import lax
from jax.sharding import PartitionSpec as P

HEAD_DIM = 64
FRAME = 4


norm_eps = 1e-05


def smooth_gate(value):
    return jax.nn.gelu(value, approximate=True)


def normalize(value):
    center = value - jnp.mean(value, axis=-1, keepdims=True)
    spread = jnp.mean(center * center, axis=-1, keepdims=True)
    inv_std = lax.rsqrt(spread + norm_eps)
    return (center * inv_std, inv_std)


def norm_back(grad, normed, inv_std, gain):
    scaled = grad * gain
    return inv_std * (
        scaled
        - jnp.mean(scaled, axis=-1, keepdims=True)
        - normed * jnp.mean(scaled * normed, axis=-1, keepdims=True)
    )


def times_t(left, right):
    return lax.dot_general(
        left, right, (((1,), (1,)), ((), ())), preferred_element_type=jnp.float32
    )


def t_times(left, right):
    return lax.dot_general(
        left, right, (((0,), (0,)), ((), ())), preferred_element_type=jnp.float32
    )


def local(
    tokens,
    segment_ids,
    ln1_gain,
    ln1_bias,
    qkv_weight,
    qv_bias,
    out_weight,
    out_bias,
    ln2_gain,
    ln2_bias,
    up_weight,
    up_bias,
    down_weight,
    down_bias,
    out_grad,
):
    rows_here, width = tokens.shape
    nseq_here, seq_len = segment_ids.shape
    head_dim = HEAD_DIM
    heads = width // head_dim
    scale = 1.0 / math.sqrt(head_dim)
    group = math.gcd(nseq_here, max(1, 512 // seq_len))
    nblocks = nseq_here // group
    frames = jnp.arange(seq_len) // FRAME
    causal = frames[:, None] >= frames[None, :]

    def split(value):
        return value.reshape(nblocks, group, seq_len, heads, head_dim)

    def allowed(seg):
        return ((seg[:, :, None] == seg[:, None, :]) & causal[None])[:, None]

    def block_scores(query_blk, key_blk, seg):
        scores = (
            jnp.einsum("gqhd,gkhd->ghqk", query_blk, key_blk, preferred_element_type=jnp.float32)
            * scale
        )
        return jnp.where(allowed(seg), scores, -1000000000.0)

    def forward_block(items):
        query_blk, key_blk, value_blk, seg = items
        scores = block_scores(query_blk, key_blk, seg)
        peak = jnp.max(scores, axis=-1, keepdims=True)
        expo = jnp.exp(scores - peak)
        total = jnp.sum(expo, axis=-1, keepdims=True)
        probs = (expo / total).astype(jnp.bfloat16)
        context_blk = jnp.einsum(
            "ghqk,gkhd->gqhd", probs, value_blk, preferred_element_type=jnp.float32
        )
        return (context_blk.astype(jnp.bfloat16), (peak + jnp.log(total))[..., 0])

    def backward_block(items):
        query_blk, key_blk, value_blk, seg, log_total, grad_ctx = items
        scores = block_scores(query_blk, key_blk, seg)
        probs = jnp.where(allowed(seg), jnp.exp(scores - log_total[..., None]), 0.0)
        probs_low = probs.astype(jnp.bfloat16)
        grad_value = jnp.einsum(
            "ghqk,gqhd->gkhd", probs_low, grad_ctx, preferred_element_type=jnp.float32
        )
        grad_prob = jnp.einsum(
            "gqhd,gkhd->ghqk", grad_ctx, value_blk, preferred_element_type=jnp.float32
        )
        weighted = jnp.sum(probs * grad_prob, axis=-1, keepdims=True)
        grad_score = (probs * (grad_prob - weighted)).astype(jnp.bfloat16)
        grad_query = (
            jnp.einsum("ghqk,gkhd->gqhd", grad_score, key_blk, preferred_element_type=jnp.float32)
            * scale
        )
        grad_key = (
            jnp.einsum("ghqk,gqhd->gkhd", grad_score, query_blk, preferred_element_type=jnp.float32)
            * scale
        )
        return (
            grad_query.astype(jnp.bfloat16),
            grad_key.astype(jnp.bfloat16),
            grad_value.astype(jnp.bfloat16),
        )

    inputs = tokens.astype(jnp.float32)
    normed_one, inv_one = normalize(inputs)
    first_in = (normed_one * ln1_gain + ln1_bias).astype(jnp.bfloat16)
    joined = jnp.dot(first_in, qkv_weight, preferred_element_type=jnp.float32)
    query = (joined[:, :width] + qv_bias[0]).astype(jnp.bfloat16)
    keys = joined[:, width : 2 * width].astype(jnp.bfloat16)
    values = (joined[:, 2 * width :] + qv_bias[1]).astype(jnp.bfloat16)
    seg_blocks = segment_ids.reshape(nblocks, group, seq_len)
    context_four, log_totals = lax.map(
        forward_block, (split(query), split(keys), split(values), seg_blocks)
    )
    context = context_four.reshape(rows_here, width)
    resid = inputs + jnp.dot(context, out_weight, preferred_element_type=jnp.float32) + out_bias
    normed_two, inv_two = normalize(resid)
    second_in = (normed_two * ln2_gain + ln2_bias).astype(jnp.bfloat16)
    second_all = lax.all_gather(second_in, "mlp", axis=0, tiled=True)
    up_all, up_bias_all, down_all = (up_weight, up_bias, down_weight)
    hidden = jnp.dot(second_all, up_all, preferred_element_type=jnp.float32) + up_bias_all
    gated_value, gate_pull = jax.vjp(smooth_gate, hidden)
    gated = gated_value.astype(jnp.bfloat16)
    ffn_out = lax.psum_scatter(
        jnp.dot(gated, down_all, preferred_element_type=jnp.float32).astype(jnp.bfloat16),
        "mlp",
        scatter_dimension=0,
        tiled=True,
    ).astype(jnp.float32)
    cotan_all = lax.all_gather(out_grad, "mlp", axis=0, tiled=True)
    layer_out = (resid + ffn_out + down_bias).astype(jnp.bfloat16)
    cotan = out_grad.astype(jnp.float32)
    grad_gated = times_t(cotan_all, down_all)
    grad_hidden = gate_pull(grad_gated)[0].astype(jnp.bfloat16)
    down_part = t_times(gated, cotan_all)
    up_part = t_times(second_all, grad_hidden)
    up_bias_part = jnp.sum(grad_hidden.astype(jnp.float32), axis=0)
    grad_second = lax.psum_scatter(
        times_t(grad_hidden, up_all), "mlp", scatter_dimension=0, tiled=True
    )
    gain_two_part = jnp.sum(grad_second * normed_two, axis=0)
    bias_two_part = jnp.sum(grad_second, axis=0)
    down_bias_part = jnp.sum(cotan, axis=0)
    grad_resid = cotan + norm_back(grad_second, normed_two, inv_two, ln2_gain)
    grad_attn = grad_resid.astype(jnp.bfloat16)
    out_weight_part = t_times(context, grad_attn)
    out_bias_part = jnp.sum(grad_attn.astype(jnp.float32), axis=0)
    grad_context = times_t(grad_attn, out_weight).astype(jnp.bfloat16)
    grad_query, grad_key, grad_value = lax.map(
        backward_block,
        (split(query), split(keys), split(values), seg_blocks, log_totals, split(grad_context)),
    )
    grad_query = grad_query.reshape(rows_here, width)
    grad_key = grad_key.reshape(rows_here, width)
    grad_value = grad_value.reshape(rows_here, width)
    grad_joined = jnp.concatenate([grad_query, grad_key, grad_value], axis=1)
    qkv_part = t_times(first_in, grad_joined)
    qv_part = jnp.stack(
        [
            jnp.sum(grad_query.astype(jnp.float32), axis=0),
            jnp.sum(grad_value.astype(jnp.float32), axis=0),
        ]
    )
    grad_first = times_t(grad_joined, qkv_weight)
    gain_one_part = jnp.sum(grad_first * normed_one, axis=0)
    bias_one_part = jnp.sum(grad_first, axis=0)
    in_grad = (grad_resid + norm_back(grad_first, normed_one, inv_one, ln1_gain)).astype(
        jnp.bfloat16
    )
    grad_up, grad_up_bias, grad_down = lax.psum((up_part, up_bias_part, down_part), "rows")
    grad_g1, grad_c1, grad_qkv, grad_qv, grad_wo, grad_bo, grad_g2, grad_c2, grad_b2 = lax.psum(
        (
            gain_one_part,
            bias_one_part,
            qkv_part,
            qv_part,
            out_weight_part,
            out_bias_part,
            gain_two_part,
            bias_two_part,
            down_bias_part,
        ),
        ("rows", "mlp"),
    )
    return (
        layer_out,
        in_grad,
        grad_g1,
        grad_c1,
        grad_qkv,
        grad_qv,
        grad_wo,
        grad_bo,
        grad_g2,
        grad_c2,
        grad_up,
        grad_up_bias,
        grad_down,
        grad_b2,
    )


def solution(mesh):
    placed = (
        P(("rows", "mlp"), None),
        P(("rows", "mlp"), None),
        P(),
        P(),
        P(),
        P(),
        P(),
        P(),
        P(),
        P(),
        P(None, "mlp"),
        P("mlp"),
        P("mlp", None),
        P(),
        P(("rows", "mlp"), None),
    )
    return jax.shard_map(
        local,
        mesh=mesh,
        in_specs=placed,
        out_specs=(
            P(("rows", "mlp"), None),
            P(("rows", "mlp"), None),
            P(),
            P(),
            P(),
            P(),
            P(),
            P(),
            P(),
            P(),
            P(None, "mlp"),
            P("mlp"),
            P("mlp", None),
            P(),
        ),
        check_vma=False,
    )
```

profile of v0, /device:TPU:0, one launch (start us, length us, event | category | flops | bytes accessed | tf_op | source)
XLA Modules:
  0.0 677.8 jit_solution(10362449141556910316)
XLA Ops:
  24.4 6.2 reshape.187
  30.5 5.1 copy.56
  35.6 6.2 reshape.188
  41.8 5.1 copy.57
  46.8 6.2 reshape.189
  53.0 5.1 copy.58
  60.0 22.5 %while.28 = (s32[]{:T(128)}, bf16[4,4,128,8,64]{2,1,0,4,3:T(4,128)(2,1)}, f32[4,4,8,128]{3,2,1,0:T(8,128)S(1)}, bf16[4,4,128,8,64]{2,4,3,1,0:T(8,128)(2,1)}, s32...) while((s32[]{:T(128)}, ...), condition=%wide.region_5.6_spmd.clone, body=%wide.region_2.5_spmd.clone.sunk | while | flops 140914688 | bytes 9871973 | solution.py:134
  82.5 4.5 reshape.179
  95.6 58.8 %all-gather.3.cloned.1.call-done = bf16[4096,512]{0,1:T(8,128)(2,1)} async-done(((bf16[2048,512]{0,1:T(8,128)(2,1)}), bf16[4096,512]{0,1:T(8,128)(2,1)}) %all-gather.3.cloned.1.call-update) | async-done | bytes 4194320 | tf_op jit(solution)/shard_map/all_gather | solution.py:141
  154.4 11.3 %fusion.83 = f32[4096,1024]{1,0:T(8,128)} fusion(bf16[4096,512]{0,1:T(8,128)(2,1)} %all-gather.3.cloned.1.call-done, bf16[512,1024]{1,0:T(8,128)(2,1)S(1)} %copy-done.32), kind=kOutput, calls=%fused_computation.141 | convolution fusion | flops 4294967296 | bytes 22020096 | tf_op jit(solution)/shard_map/dot_general | solution.py:143
  165.7 47.0 %all-gather.5.cloned.1.call-done = bf16[4096,512]{1,0:T(8,128)(2,1)} async-done(((bf16[2048,512]{1,0:T(8,128)(2,1)}), bf16[4096,512]{1,0:T(8,128)(2,1)}) %all-gather.5.cloned.1.call-update) | async-done | bytes 4194320 | tf_op jit(solution)/shard_map/all_gather | solution.py:152
  212.7 20.5 %convert_reduce_fusion = (f32[1024]{0:T(1024)S(1)}, bf16[4096,1024]{1,0:T(8,128)(2,1)S(1)}, bf16[4096,1024]{1,0:T(8,128)(2,1)}) fusion(f32[4096,1024]{1,0:T(8,128)} %fusion.83, f32[1024]{0:T(1024)S(1)} %convert_element_type.127, bf16[4096,512]{1,0:T(8,128)(2,1)} %all-gather.5.cloned.1.call-done, bf16[1024,512]{1,0:T(8,128)(2,1)} %param.31), kind=kOutput, calls=%fused_computation.75 | convolution fusion | flops 4399823872 | bytes 38805504 | tf_op jit(solution)/shard_map/dot_general | solution.py:36
  236.4 6.8 %fusion.84 = f32[4096,512]{0,1:T(8,128)} fusion(bf16[4096,1024]{1,0:T(8,128)(2,1)S(1)} %get-tuple-element.288, bf16[512,1024]{1,0:T(8,128)(2,1)S(1)} %copy-done.32), kind=kOutput, calls=%fused_computation.142 | convolution fusion | flops 4294967296 | bytes 17825792 | tf_op jit(solution)/shard_map/dot_general | solution.py:36
  244.4 9.5 %convolution_convert_fusion.2 = bf16[4096,512]{0,1:T(8,128)(2,1)} fusion(bf16[4096,1024]{1,0:T(8,128)(2,1)} %get-tuple-element.295, bf16[1024,512]{1,0:T(8,128)(2,1)S(1)} %copy-done.33), kind=kOutput, calls=%fused_computation.80 | convolution fusion | flops 4297064448 | bytes 13631488 | tf_op jit(solution)/shard_map/dot_general | solution.py:147
  254.0 15.2 %copy.61 = bf16[2048,512]{0,1:T(8,128)(2,1)} copy(bf16[2048,512]{1,0:T(8,128)(2,1)} %param.33) | data formatting | bytes 4194304 | tf_op args[14]
  269.3 33.7 %psum.93 = f32[1024]{0:T(1024)} all-reduce(f32[1024]{0:T(1024)S(1)} %get-tuple-element.287), channel_id=1, replica_groups=mesh['rows'=16,'mlp'=2] {'rows'}, use_global_device_ids=true, to_apply=%region_34.35 | all-reduce | flops 1024 | bytes 8192 | tf_op jit(solution)/shard_map/psum | solution.py:192
  303.0 10.7 %fusion.86 = f32[1024,512]{1,0:T(8,128)} fusion(bf16[4096,1024]{1,0:T(8,128)(2,1)} %get-tuple-element.295, bf16[4096,512]{1,0:T(8,128)(2,1)} %all-gather.5.cloned.1.call-done), kind=kOutput, calls=%fused_computation.144 | convolution fusion | flops 4294967296 | bytes 14680064 | tf_op jit(solution)/shard_map/dot_general | solution.py:42
  313.7 8.5 %fusion.85 = f32[512,1024]{1,0:T(8,128)} fusion(bf16[4096,512]{0,1:T(8,128)(2,1)S(1)} %copy-done.31, bf16[4096,1024]{1,0:T(8,128)(2,1)} %copy-done.34), kind=kOutput, calls=%fused_computation.143 | convolution fusion | flops 4294967296 | bytes 14680064 | tf_op jit(solution)/shard_map/dot_general | solution.py:42
  322.3 20.4 %reduce-scatter.5.cloned.1.call-done = f32[2048,512]{0,1:T(8,128)} async-done(((f32[4096,512]{0,1:T(8,128)}), f32[2048,512]{0,1:T(8,128)}) %reduce-scatter.5.cloned.1.call-update) | async-done | bytes 4194320 | tf_op jit(solution)/shard_map/reduce_scatter | solution.py:160
  347.2 52.0 %reduce-scatter.3.cloned.1.call-done = bf16[2048,512]{0,1:T(8,128)(2,1)} async-done(((bf16[4096,512]{0,1:T(8,128)(2,1)}), bf16[2048,512]{0,1:T(8,128)(2,1)}) %reduce-scatter.3.cloned.1.call-update) | async-done | bytes 2097168 | tf_op jit(solution)/shard_map/reduce_scatter | solution.py:146
  399.2 6.9 %convert_reduce_fusion.3 = (f32[512]{0:T(512)S(1)}, f32[2048,512]{0,1:T(8,128)S(1)}, bf16[2048,512]{0,1:T(8,128)(2,1)}, f32[512]{0:T(512)S(1)}) fusion(f32[2048]{0:T(1024)S(1)} %get-tuple-element.306, f32[2048,512]{0,1:T(8,128)} %copy-done.1, f32[2048]{0:T(1024)S(1)} %broadcast_multiply_fusion.4, f32[2048]{0:T(1024)S(1)} %get-tuple-element.307, ...), kind=kLoop, calls=%fused_computation.105 | loop fusion | flops 17824768 | bytes 18915328 | tf_op jit(solution)/shard_map/reduce_sum | solution.py:169
  411.6 6.2 reshape.186
  417.8 5.1 copy.66
  424.7 50.8 %while.29 = (s32[]{:T(128)}, bf16[4,4,128,8,64]{2,4,3,1,0:T(8,128)(2,1)}, bf16[4,4,128,8,64]{2,1,0,4,3:T(4,128)(2,1)}, bf16[4,4,128,8,64]{2,4,3,1,0:T(8,128)(2,1...) while((s32[]{:T(128)}, ...), condition=%wide.region_14.15_spmd.clone, body=%wide.region_12.14_spmd.clone.sunk | while | flops 342241280 | bytes 22277756 | solution.py:171
  492.4 4.5 copy.70
  506.2 8.2 %fusion.82 = (f32[512]{0:T(512)S(1)}, f32[2048,512]{1,0:T(8,128)}) fusion(bf16[2048,1536]{0,1:T(8,128)(2,1)} %constant_dynamic-update-slice_fusion, bf16[512,1536]{1,0:T(8,128)(2,1)S(1)} %copy-done), kind=kOutput, calls=%fused_computation.140 | convolution fusion | flops 3222273536 | bytes 12060672 | tf_op jit(solution)/shard_map/dot_general | solution.py:36
  514.5 5.2 fusion.76
  523.8 5.7 copy.71
  529.5 4.6 fusion.68
  534.4 5.0 fusion.67
  547.3 39.8 %all-reduce = (f32[512]{0:T(512)}, f32[512]{0:T(512)}, f32[2,512]{1,0:T(2,128)}, f32[512]{0:T(512)}, f32[512]{0:T(512)}, /*index=5*/f32[512]{0:T(512)}, f32[512]{0:T(512)}) all-reduce(f32[512]{0:T(512)S(1)} %get-tuple-element.233, f32[512]{0:T(512)S(1)} %get-tuple-element.304, ...), channel_id=1, replica_groups=mesh['rows'=16,'mlp'=2] {'rows','mlp'}, use_global_device_ids=true, to_apply=%region_18.19 | all-reduce | flops 4096 | bytes 32768 | tf_op jit(solution)/shard_map/psum | solution.py:193
  587.2 75.8 %all-reduce.6.cloned.1.call-done = (f32[512,1536]{1,0:T(8,128)}, f32[512,512]{1,0:T(8,128)}) async-done(((f32[512,1536]{1,0:T(8,128)}, f32[512,512]{1,0:T(8,128)}), (f32[512,1536]{1,0:T(8,128)}, f32[512,512]{1,0:T(8,128)})) %all-reduce.6.cloned.1.call-update) | async-done | bytes 4194320 | tf_op jit(solution)/shard_map/psum | solution.py:193
  (210 shorter events, 162.1 us)
Async XLA Ops:
  7.2 8.5 %copy-start = (bf16[512,1536]{1,0:T(8,128)(2,1)S(1)}, bf16[512,1536]{1,0:T(8,128)(2,1)}, u32[]{:S(2)}) copy-start(bf16[512,1536]{1,0:T(8,128)(2,1)} %param.23) | copy-start | bytes 4718596
  7.2 147.2 %all-gather.3.cloned.1.call-start = ((), (), s32[]{:S(2)}) async-start(), calls=%async_computation.2 | async-start | bytes 6291456 | tf_op jit(solution)/shard_map/all_gather | solution.py:141
  7.3 8.4 %copy-start.25 = (bf16[512]{0:T(512)(128)(2,1)S(1)}, bf16[512]{0:T(512)(128)(2,1)}, u32[]{:S(2)}) copy-start(bf16[512]{0:T(512)(128)(2,1)} %param.21) | copy-start | bytes 3076
  7.3 8.4 %copy-start.26 = (bf16[512]{0:T(512)(128)(2,1)S(1)}, bf16[512]{0:T(512)(128)(2,1)}, u32[]{:S(2)}) copy-start(bf16[512]{0:T(512)(128)(2,1)} %param.22) | copy-start | bytes 3076
  7.3 8.4 %copy-start.21 = (bf16[2,512]{1,0:T(2,128)(2,1)S(1)}, bf16[2,512]{1,0:T(2,128)(2,1)}, u32[]{:S(2)}) copy-start(bf16[2,512]{1,0:T(2,128)(2,1)} %param.24) | copy-start | bytes 6148
  11.3 4.4 copy-start.4
  13.4 6.1 copy-start.14
  15.6 3.9 copy-start.16
  15.7 3.9 copy-start.19
  15.7 3.9 copy-start.23
  53.0 6.9 %copy-start.18 = (s32[16,128]{1,0:T(8,128)S(1)}, s32[16,128]{1,0:T(8,128)}, u32[]{:S(2)}) copy-start(s32[16,128]{1,0:T(8,128)} %param.20) | copy-start | bytes 24580
  82.4 4.6 copy-start.27
  82.4 4.6 copy-start.13
  92.7 61.6 %copy-start.32 = (bf16[512,1024]{1,0:T(8,128)(2,1)S(1)}, bf16[512,1024]{1,0:T(8,128)(2,1)}, u32[]{:S(2)}) copy-start(bf16[512,1024]{1,0:T(8,128)(2,1)} %param.29) | copy-start | bytes 3145732
  94.7 117.9 %all-gather.5.cloned.1.call-start = ((), (), s32[]{:S(2)}) async-start(), calls=%async_computation.4 | async-start | bytes 6291456 | tf_op jit(solution)/shard_map/all_gather | solution.py:152
  95.5 247.2 %reduce-scatter.5.cloned.1.call-start = ((), (), s32[]{:S(2)}) async-start(), calls=%async_computation.5 | async-start | bytes 12582912 | tf_op jit(solution)/shard_map/reduce_scatter | solution.py:160
  243.2 156.0 %reduce-scatter.3.cloned.1.call-start = ((), (), s32[]{:S(2)}) async-start(), calls=%async_computation.3 | async-start | bytes 6291456 | tf_op jit(solution)/shard_map/reduce_scatter | solution.py:146
  253.9 15.3 %copy-start.30 = (bf16[512]{0:T(512)(128)(2,1)S(1)}, bf16[512]{0:T(512)(128)(2,1)}, u32[]{:S(2)}) copy-start(bf16[512]{0:T(512)(128)(2,1)} %param.32) | copy-start | bytes 3076
  254.0 333.2 %all-reduce.8.cloned.1.call-start = ((), (), s32[]{:S(2)}) async-start(), calls=%async_computation.7 | async-start | bytes 8388608 | tf_op jit(solution)/shard_map/psum | solution.py:192
  303.0 10.7 %copy-start.31 = (bf16[4096,512]{0,1:T(8,128)(2,1)S(1)}, bf16[4096,512]{0,1:T(8,128)(2,1)}, u32[]{:S(2)}) copy-start(bf16[4096,512]{0,1:T(8,128)(2,1)} %all-gather.3.cloned.1.call-done) | copy-start | bytes 12582916
  322.2 340.7 %all-reduce.6.cloned.1.call-start = ((), (), s32[]{:S(2)}) async-start(), calls=%async_computation.6 | async-start | bytes 8388608 | tf_op jit(solution)/shard_map/psum | solution.py:193
  501.4 3.3 copy-start.7
  506.2 8.3 %copy-start.5 = (bf16[2048,512]{0,1:T(8,128)(2,1)S(1)}, bf16[2048,512]{0,1:T(8,128)(2,1)}, u32[]{:S(2)}) copy-start(bf16[2048,512]{0,1:T(8,128)(2,1)} %copy.52) | copy-start | bytes 6291460
  506.2 8.3 %copy-start.12 = (bf16[2048,1536]{0,1:T(8,128)(2,1)S(1)}, bf16[2048,1536]{0,1:T(8,128)(2,1)}, u32[]{:S(2)}) copy-start(bf16[2048,1536]{0,1:T(8,128)(2,1)} %constant_dynamic-update-slice_fusion) | copy-start | bytes 18874372
  506.2 8.3 %copy-start.15 = (f32[2048]{0:T(1024)S(1)}, f32[2048]{0:T(1024)}, u32[]{:S(2)}) copy-start(f32[2048]{0:T(1024)} %copy-done.14) | copy-start | bytes 24580
  506.2 8.3 %copy-start.17 = (f32[2048]{0:T(1024)S(1)}, f32[2048]{0:T(1024)}, u32[]{:S(2)}) copy-start(f32[2048]{0:T(1024)} %copy-done.16) | copy-start | bytes 24580
  506.2 8.3 %copy-start.20 = (f32[512]{0:T(512)S(1)}, f32[512]{0:T(512)}, u32[]{:S(2)}) copy-start(f32[512]{0:T(512)} %copy-done.19) | copy-start | bytes 6148
  506.2 8.3 %copy-start.24 = (f32[512]{0:T(512)S(1)}, f32[512]{0:T(512)}, u32[]{:S(2)}) copy-start(f32[512]{0:T(512)} %copy-done.23) | copy-start | bytes 6148
  529.5 4.6 copy-start.3
  529.5 5.0 copy-start.6
  663.0 3.9 copy-start.11
  663.0 4.9 copy-start.9
  (9 other events, 19.1 us)
Sparse Core Ops, SparseCore 0:
  94.9 59.4 all-gather.2
  155.9 56.7 all-gather.4
  243.4 99.2 reduce-scatter.4
  344.9 54.2 reduce-scatter.2
  402.8 111.5 all-reduce.7
  521.5 141.4 all-reduce.5
where the time goes:
time: 689 us; the launch traced here: 678 us
  waiting for transfers between devices  255 us (37%)
  matrix products  150 us (22%)
  local copies, waits for them, and re-layouts  143 us (21%)
  blocking collectives  73.6 us (11%)
  other arithmetic  40.5 us (6%)
  between operations  15 us (2%)
    psum x1, waiting for transfers between devices, local(): lax.psum((gain_one_part, bias_one_part, qkv_part, qv_part, out_weight_par...  75.8 us
    unnamed x84, local copies, waits for them, and re-layouts  68.3 us
    all_gather x1, waiting for transfers between devices, local(): second_all = lax.all_gather(second_in, 'mlp', axis=0, tiled=True)  58.8 us
    reduce_scatter x1, waiting for transfers between devices, local(): lax.psum_scatter(jnp.dot(gated, down_all, preferred_element_type=jnp.floa...  52 us
    all_gather x1, waiting for transfers between devices, local(): cotan_all = lax.all_gather(out_grad, 'mlp', axis=0, tiled=True)  47 us
    psum x1, blocking collectives, local(): lax.psum((gain_one_part, bias_one_part, qkv_part, qv_part, out_weight_par...  39.8 us
    dot_general x4, matrix products, times_t(): lax.dot_general(left, right, (((1,), (1,)), ((), ())), preferred_element_...  38.2 us
    psum x1, blocking collectives, local(): lax.psum((up_part, up_bias_part, down_part), 'rows')  33.7 us
  transfers between devices with their start and end apart: 6, of which 5 were waited for; matrix products, arithmetic and copies ran while one was open for 30% of the time, Pallas kernels for 0%

commit v1 on v0

v1 whole, which is shorter than its diff:
```python
import functools
import math

import jax
import jax.numpy as jnp
from jax import lax
from jax.experimental import pallas as pl
from jax.experimental.pallas import tpu as pltpu
from jax.sharding import PartitionSpec as P

BF, F32 = jnp.bfloat16, jnp.float32
SEQ, HD, FRAME = 128, 64, 4
EPS = 1e-5
C0 = math.sqrt(2.0 / math.pi)
C1 = C0 * 0.044715
LIMIT = 56 * 1024 * 1024
BOTH = ("rows", "mlp")


def mm(a, b, ca=1, cb=0):
    return lax.dot_general(a, b, (((ca,), (cb,)), ((), ())), preferred_element_type=F32)


def layer_norm(x):
    c = x - jnp.mean(x, axis=-1, keepdims=True)
    inv = lax.rsqrt(jnp.mean(c * c, axis=-1, keepdims=True) + EPS)
    return c * inv, inv


def norm_back(grad, normed, inv, gain):
    s = grad * gain
    return inv * (
        s
        - jnp.mean(s, axis=-1, keepdims=True)
        - normed * jnp.mean(s * normed, axis=-1, keepdims=True)
    )


def fold(v):
    return jnp.sum(v.reshape(-1, 8, v.shape[-1]), axis=0)


def stack_heads(v):
    low = lax.broadcasted_iota(jnp.int32, v.shape, 1) < HD
    zero = jnp.zeros_like(v)
    return jnp.concatenate([jnp.where(low, v, zero), jnp.where(low, zero, v)], axis=0)


def allowed_of(seg_row, transposed):
    wide = jnp.broadcast_to(seg_row.astype(F32), (SEQ, SEQ))
    same = wide == wide.T
    a = lax.broadcasted_iota(jnp.int32, (SEQ, SEQ), 1 if transposed else 0)
    b = lax.broadcasted_iota(jnp.int32, (SEQ, SEQ), 0 if transposed else 1)
    return same & (a // FRAME >= b // FRAME)


def whole(a):
    zeros = (0,) * len(a.shape)
    return pl.BlockSpec(a.shape, lambda i, *_: zeros)


def rows_spec(r, w):
    return pl.BlockSpec((r, w), lambda i, *_: (i, 0))


def shape(s, dtype):
    return jax.ShapeDtypeStruct(s, dtype)


def cost(macs, nbytes=0):
    return pl.CostEstimate(flops=2 * macs, bytes_accessed=nbytes, transcendentals=0)


def attn_fwd_body(tok, seg, g1, b1, wqkv, bqkv, wo, bo, g2, b2, joined_o, ctx_o, resid_o, h2_o):
    rows, width = tok.shape
    x = tok[...].astype(F32)
    n1, _ = layer_norm(x)
    h1 = (n1 * g1[...].astype(F32) + b1[...].astype(F32)).astype(BF)
    joined = (mm(h1, wqkv[...]) + bqkv[...].astype(F32)).astype(BF)
    joined_o[...] = joined
    parts = []
    for s in range(rows // SEQ):
        ok = allowed_of(seg[0, s : s + 1, :], False)
        r = slice(s * SEQ, (s + 1) * SEQ)
        outs = []
        for p in range(width // 128):
            q = joined[r, p * 128 : (p + 1) * 128] * BF(0.125)
            k = joined[r, width + p * 128 : width + (p + 1) * 128]
            v = joined[r, 2 * width + p * 128 : 2 * width + (p + 1) * 128]
            sc = mm(q, stack_heads(k), 1, 1)
            pr = []
            for h in range(2):
                t = jnp.where(ok, sc[:, h * 128 : (h + 1) * 128], -1e9)
                e = jnp.exp(t - jnp.max(t, axis=1, keepdims=True))
                pr.append((e * (1.0 / jnp.sum(e, axis=1, keepdims=True))).astype(BF))
            outs.append(mm(jnp.concatenate(pr, axis=1), stack_heads(v)).astype(BF))
        parts.append(jnp.concatenate(outs, axis=1))
    ctx = jnp.concatenate(parts, axis=0)
    ctx_o[...] = ctx
    resid = x + mm(ctx, wo[...]) + bo[...].astype(F32)
    resid_o[...] = resid
    n2, _ = layer_norm(resid)
    h2_o[...] = (n2 * g2[...].astype(F32) + b2[...].astype(F32)).astype(BF)


def attn_fwd(tok, seg, g1, b1, wqkv, bqkv, wo, bo, g2, b2, rows):
    t, d = tok.shape
    small = (g1, b1, wqkv, bqkv, wo, bo, g2, b2)
    return pl.pallas_call(
        attn_fwd_body,
        grid=(t // rows,),
        in_specs=[rows_spec(rows, d), pl.BlockSpec((1, rows // SEQ, SEQ), lambda i: (i, 0, 0))]
        + [whole(a) for a in small],
        out_specs=[rows_spec(rows, w) for w in (3 * d, d, d, d)],
        out_shape=[shape((t, 3 * d), BF), shape((t, d), BF), shape((t, d), F32), shape((t, d), BF)],
        compiler_params=pltpu.CompilerParams(vmem_limit_bytes=LIMIT),
        cost_estimate=cost(2 * t * d * 4 * d),
        name="attn_fwd",
    )(tok, seg.reshape(t // rows, rows // SEQ, SEQ), *small)


def ffn_chunk(hv, gv, h2t, gt, up, ub, dn):
    v = mm(hv, up) + ub
    v2 = v * v
    a = 0.5 + 0.5 * jnp.tanh(v * (C0 + C1 * v2))
    act = v * a
    slope = a + 2.0 * act * (1.0 - a) * (C0 + 3.0 * C1 * v2)
    gated = act.astype(BF)
    dhid = (mm(gv, dn, 1, 1) * slope).astype(BF)
    return mm(gated, dn), mm(dhid, up, 1, 1), mm(h2t, dhid), mm(gt, gated), fold(dhid.astype(F32))


def ffn_own_body(core, h2, g, up, ub, down, out_o, dh2_o, keep_o, send_o, gub_o, gup, gdn, gub):
    i = pl.program_id(0)
    d, f = up.shape
    half = f // 2

    @pl.when(i == 0)
    def _():
        gup[...] = jnp.zeros_like(gup)
        gdn[...] = jnp.zeros_like(gdn)
        gub[...] = jnp.zeros_like(gub)

    hv, gv = h2[...], g[...]
    h2t, gt = hv.T, gv.T
    out = dh2 = 0.0
    for c in range(2):
        s = slice(c * half, (c + 1) * half)
        o, dh, u, w, b = ffn_chunk(hv, gv, h2t, gt, up[:, s], ub[:, s].astype(F32), down[s, :])
        out, dh2 = out + o, dh2 + dh
        gup[c] += u
        gdn[c] += w
        gub[c] += b
    out_o[...] = out
    dh2_o[...] = dh2

    @pl.when(i == pl.num_programs(0) - 1)
    def _():
        c = core[0]
        keep_o[0] = gup[c].astype(BF)
        keep_o[1] = gdn[c].astype(BF)
        send_o[0] = gup[1 - c].astype(BF)
        send_o[1] = gdn[1 - c].astype(BF)
        gub_o[0:1] = jnp.sum(gub[0], axis=0, keepdims=True)
        gub_o[1:2] = jnp.sum(gub[1], axis=0, keepdims=True)


def ffn_own(core, h2, g, up, ub, down, rows):
    t, d = h2.shape
    f = up.shape[1]
    half = f // 2
    outs = [shape((t, d), F32), shape((t, d), F32), shape((2, d, half), BF), shape((2, d, half), BF), shape((2, half), F32)]
    return pl.pallas_call(
        ffn_own_body,
        grid_spec=pltpu.PrefetchScalarGridSpec(
            num_scalar_prefetch=1,
            grid=(t // rows,),
            in_specs=[rows_spec(rows, d), rows_spec(rows, d), whole(up), whole(ub), whole(down)],
            out_specs=[rows_spec(rows, d), rows_spec(rows, d)] + [whole(o) for o in outs[2:]],
            scratch_shapes=[pltpu.VMEM((2, d, half), F32), pltpu.VMEM((2, d, half), F32), pltpu.VMEM((2, 8, half), F32)],
        ),
        out_shape=outs,
        compiler_params=pltpu.CompilerParams(vmem_limit_bytes=LIMIT),
        cost_estimate=cost(2 * 6 * t * d * f),
        name="ffn_own",
    )(core, h2, g, up, ub, down)


def ffn_other_body(
    h2, g, w_send, w_keep, out_p, dh2_p, resid, ctx, wo, g2, b2,
    layer_o, dattn_o, dctx_o, keep_o, send_o, gub_o, gout_o, vec_o, gup, gdn, gub, gout, vec,
):
    i = pl.program_id(0)
    d = h2.shape[1]

    @pl.when(i == 0)
    def _():
        for a in (gup, gdn, gub, gout, vec):
            a[...] = jnp.zeros_like(a)

    hv, gv = h2[...], g[...]
    h2t, gt = hv.T, gv.T
    out, dh2 = out_p[...], dh2_p[...]
    for c, w in enumerate((w_send, w_keep)):
        ub = w[2 * d : 2 * d + 8, :].astype(F32)[0:1]
        o, dh, u, wd, b = ffn_chunk(hv, gv, h2t, gt, w[0:d, :], ub, w[d : 2 * d, :])
        out, dh2 = out + o, dh2 + dh
        gup[c] += u
        gdn[c] += wd
        gub[c] += b
    res = resid[...]
    layer_o[...] = (res + out + b2[...].astype(F32)).astype(BF)
    n2, inv2 = layer_norm(res)
    gf = gv.astype(F32)
    dattn = (gf + norm_back(dh2, n2, inv2, g2[...].astype(F32))).astype(BF)
    dattn_o[...] = dattn
    dctx_o[...] = mm(dattn, wo[...], 1, 1).astype(BF)
    gout[...] += mm(ctx[...].T, dattn)
    vec[0] += fold(dattn.astype(F32))
    vec[1] += fold(dh2 * n2)
    vec[2] += fold(dh2)
    vec[3] += fold(gf)

    @pl.when(i == pl.num_programs(0) - 1)
    def _():
        send_o[0] = gup[0].astype(BF)
        send_o[1] = gdn[0].astype(BF)
        keep_o[0] = gup[1].astype(BF)
        keep_o[1] = gdn[1].astype(BF)
        for c in range(2):
            gub_o[c : c + 1] = jnp.sum(gub[c], axis=0, keepdims=True)
        gout_o[...] = gout[...].astype(BF)
        for c in range(4):
            vec_o[c : c + 1] = jnp.sum(vec[c], axis=0, keepdims=True)


def ffn_other(h2, g, w_send, w_keep, out_p, dh2_p, resid, ctx, wo, g2, b2, rows):
    t, d = h2.shape
    half = d
    outs = [shape((t, d), BF)] * 3 + [
        shape((2, d, half), BF), shape((2, d, half), BF), shape((2, half), F32), shape((d, d), BF), shape((4, d), F32),
    ]
    return pl.pallas_call(
        ffn_other_body,
        grid=(t // rows,),
        in_specs=[rows_spec(rows, d), rows_spec(rows, d), whole(w_send), whole(w_keep)]
        + [rows_spec(rows, d)] * 4
        + [whole(wo), whole(g2), whole(b2)],
        out_specs=[rows_spec(rows, d)] * 3 + [whole(o) for o in outs[3:]],
        out_shape=outs,
        scratch_shapes=[
            pltpu.VMEM((2, d, half), F32), pltpu.VMEM((2, d, half), F32), pltpu.VMEM((2, 8, half), F32),
            pltpu.VMEM((d, d), F32), pltpu.VMEM((4, 8, d), F32),
        ],
        compiler_params=pltpu.CompilerParams(vmem_limit_bytes=LIMIT),
        cost_estimate=cost(2 * (6 * t * d * 2 * half + 2 * t * d * d)),
        name="ffn_other",
    )(h2, g, w_send, w_keep, out_p, dh2_p, resid, ctx, wo, g2, b2)


def attn_bwd_body(place, joined, dctx, seg, tok, wqkv, gout, gub_own, gub_other, vec, dj_o, pay_o, acc, cs, small):
    i = pl.program_id(0)
    rows, width = tok.shape

    @pl.when(i == 0)
    def _():
        acc[...] = jnp.zeros_like(acc)
        cs[...] = jnp.zeros_like(cs)

    n1, _ = layer_norm(tok[...].astype(F32))
    n1t = n1.astype(BF).T
    seqs = []
    for s in range(rows // SEQ):
        ok = allowed_of(seg[0, s : s + 1, :], True)
        r = slice(s * SEQ, (s + 1) * SEQ)
        dq, dk, dv = [], [], []
        for p in range(width // 128):
            q = joined[r, p * 128 : (p + 1) * 128] * BF(0.125)
            k = joined[r, width + p * 128 : width + (p + 1) * 128]
            v = joined[r, 2 * width + p * 128 : 2 * width + (p + 1) * 128]
            qs = stack_heads(q)
            dc = stack_heads(dctx[r, p * 128 : (p + 1) * 128])
            sc = mm(k, qs, 1, 1)
            dp = mm(v, dc, 1, 1)
            pb, ds = [], []
            for h in range(2):
                hs = slice(h * 128, (h + 1) * 128)
                t = jnp.where(ok, sc[:, hs], -1e9)
                e = jnp.exp(t - jnp.max(t, axis=0, keepdims=True))
                pr = e * (1.0 / jnp.sum(e, axis=0, keepdims=True))
                dph = dp[:, hs]
                ds.append((pr * (dph - jnp.sum(pr * dph, axis=0, keepdims=True))).astype(BF))
                pb.append(pr.astype(BF))
            dv.append(mm(jnp.concatenate(pb, axis=1), dc).astype(BF))
            dk.append(mm(jnp.concatenate(ds, axis=1), qs).astype(BF))
            dq.append((mm(jnp.concatenate(ds, axis=0), stack_heads(k), 0, 0) * 0.125).astype(BF))
        seqs.append(jnp.concatenate(dq + dk + dv, axis=1))
    dj = jnp.concatenate(seqs, axis=0)
    dj_o[...] = dj
    acc[...] += mm(n1t, dj)
    cs[...] += fold(dj.astype(F32))

    @pl.when(i == pl.num_programs(0) - 1)
    def _():
        w = wqkv[...]
        weighted = (acc[...] * w.astype(F32)).astype(BF)
        ones = jnp.ones((8, 3 * width), BF)
        total = jnp.sum(cs[...], axis=0, keepdims=True)
        part = cs[...]
        hi = part.astype(BF)
        lo = (part - hi.astype(F32)).astype(BF)
        small[...] = jnp.zeros_like(small)
        small[0:1] = mm(ones, weighted, 1, 1)[0:1]
        small[1:2] = jnp.sum(mm(hi, w, 1, 1) + mm(lo, w, 1, 1), axis=0, keepdims=True)
        for j in range(3):
            small[2 + j : 3 + j] = total[:, j * width : (j + 1) * width]
        for j in range(4):
            small[5 + j : 6 + j] = vec[j : j + 1, :]
        y, c = place[0], place[1]
        for j in range(2):
            small[pl.ds(16 + 2 * y + j, 1)] = gub_own[j : j + 1, :]
        small[pl.ds(16 + 2 * (1 - y) + 1 - c, 1)] = gub_other[0:1, :]
        small[pl.ds(16 + 2 * (1 - y) + c, 1)] = gub_other[1:2, :]
        pay_o[0, 0:width] = acc[:, 0:width].astype(BF)
        pay_o[0, width : 2 * width] = acc[:, width : 2 * width].astype(BF)
        pay_o[0, 2 * width :] = small[...].astype(BF)
        pay_o[1, 0:width] = acc[:, 2 * width :].astype(BF)
        pay_o[1, width : 2 * width] = gout[...]
        pay_o[1, 2 * width :] = jnp.zeros((32, width), BF)


def attn_bwd(place, joined, dctx, seg, tok, wqkv, gout, gub_own, gub_other, vec, rows):
    t, d = tok.shape
    outs = [shape((t, 3 * d), BF), shape((2, 2 * d + 32, d), BF)]
    rest = (wqkv, gout, gub_own, gub_other, vec)
    return pl.pallas_call(
        attn_bwd_body,
        grid_spec=pltpu.PrefetchScalarGridSpec(
            num_scalar_prefetch=1,
            grid=(t // rows,),
            in_specs=[
                rows_spec(rows, 3 * d),
                rows_spec(rows, d),
                pl.BlockSpec((1, rows // SEQ, SEQ), lambda i, *_: (i, 0, 0)),
                rows_spec(rows, d),
            ]
            + [whole(a) for a in rest],
            out_specs=[rows_spec(rows, 3 * d), whole(outs[1])],
            scratch_shapes=[pltpu.VMEM((d, 3 * d), F32), pltpu.VMEM((8, 3 * d), F32), pltpu.VMEM((32, d), F32)],
        ),
        out_shape=outs,
        compiler_params=pltpu.CompilerParams(vmem_limit_bytes=LIMIT),
        cost_estimate=cost(2 * t * d * 5 * d),
        name="attn_bwd",
    )(place, joined, dctx, seg.reshape(t // rows, rows // SEQ, SEQ), tok, *rest)


def in_grad_body(dj, tok, dattn, wqkv, g1, out_o):
    dh1 = mm(dj[...], wqkv[...], 1, 1)
    n1, inv1 = layer_norm(tok[...].astype(F32))
    out_o[...] = (dattn[...].astype(F32) + norm_back(dh1, n1, inv1, g1[...].astype(F32))).astype(BF)


def in_grad_of(dj, tok, dattn, wqkv, g1, rows):
    t, d = tok.shape
    return pl.pallas_call(
        in_grad_body,
        grid=(t // rows,),
        in_specs=[rows_spec(rows, 3 * d), rows_spec(rows, d), rows_spec(rows, d), whole(wqkv), whole(g1)],
        out_specs=rows_spec(rows, d),
        out_shape=shape((t, d), BF),
        compiler_params=pltpu.CompilerParams(vmem_limit_bytes=LIMIT),
        cost_estimate=cost(2 * t * d * 3 * d),
        name="in_grad",
    )(dj, tok, dattn, wqkv, g1)


def gray(u):
    return u ^ (u >> 1)


def gray_back(g):
    u = 0
    while g:
        u, g = u ^ g, g >> 1
    return u


def local(
    n_rows,
    tokens,
    segment_ids,
    ln1_gain,
    ln1_bias,
    qkv_weight,
    qv_bias,
    out_weight,
    out_bias,
    ln2_gain,
    ln2_bias,
    up_weight,
    up_bias,
    down_weight,
    down_bias,
    out_grad,
):
    t, d = tokens.shape
    half = up_weight.shape[1] // 2
    r, y = lax.axis_index("rows"), lax.axis_index("mlp")
    core = r & 1
    up_dims = n_rows.bit_length() - 2

    def flip(dim, row, m):
        if dim == "core":
            return row ^ 1, m
        if dim == "y":
            return row, m ^ 1
        if dim == 0:
            return row ^ 2, m
        return (gray_back(gray(row >> 2) ^ (1 << (dim - 1))) << 2) | (row & 3), m

    def bit(dim):
        if dim == "y":
            return y
        if dim == 0:
            return (r >> 1) & 1
        return (gray(r >> 2) >> (dim - 1)) & 1

    def swap(value, *dims):
        pairs = []
        for row in range(n_rows):
            for m in range(2):
                row2, m2 = flip(dims[0] if row & 1 == 0 else dims[-1], row, m)
                pairs.append((row * 2 + m, row2 * 2 + m2))
        return lax.ppermute(value, BOTH, pairs)

    def by_core(first, second):
        return jnp.where(core == 0, first, second)

    def pick(value, index):
        return lax.dynamic_index_in_dim(value, index, 0, keepdims=False)

    def add(a, b):
        return (a.astype(F32) + b.astype(F32)).astype(BF)

    def in_order(mine, other, v):
        return jnp.stack([jnp.where(v == 0, mine, other), jnp.where(v == 0, other, mine)])

    first = 1 - core
    bias_rows = jnp.broadcast_to(lax.dynamic_slice(up_bias, (first * half,), (half,))[None], (16, half))
    w_mine = jnp.concatenate(
        [
            lax.dynamic_slice(up_weight, (0, first * half), (d, half)),
            lax.dynamic_slice(down_weight, (first * half, 0), (half, d)),
            bias_rows,
        ],
        axis=0,
    )
    w_send = swap(w_mine, "y")
    w_keep = swap(w_send, "core")

    row = lambda a: a.reshape(1, -1)
    bqkv = jnp.concatenate([qv_bias[0], jnp.zeros((d,), BF), qv_bias[1]]).reshape(1, -1)
    joined, ctx, resid, h2 = attn_fwd(
        tokens, segment_ids, row(ln1_gain), row(ln1_bias), qkv_weight, bqkv, out_weight, row(out_bias),
        row(ln2_gain), row(ln2_bias), rows=512,
    )
    core_s = core.reshape(1).astype(jnp.int32)
    out_p, dh2_p, own_keep, own_send, gub_own = ffn_own(
        core_s, h2, out_grad, up_weight, row(up_bias), down_weight, rows=512
    )
    own = add(own_keep, swap(own_send, "core"))
    layer_out, dattn, dctx, oth_keep, oth_send, gub_oth, gout, vec = ffn_other(
        h2, out_grad, w_send, w_keep, out_p, dh2_p, resid, ctx, out_weight, row(ln2_gain), row(down_bias), rows=512
    )
    oth = add(oth_keep, swap(oth_send, "core"))
    place = jnp.stack([y, core]).astype(jnp.int32)
    dj, pay = attn_bwd(place, joined, dctx, segment_ids, tokens, qkv_weight, gout, gub_own, gub_oth, vec, rows=512)

    order0 = [0, "y"] + list(range(1, up_dims))
    order1 = ["y"] + list(range(1, up_dims)) + [0]
    v0 = bit(0)
    four = jnp.concatenate([own, oth], axis=0)
    k0, k1 = by_core(v0, 0), by_core(2 + v0, 1)
    s0, s1 = by_core(1 - v0, 2), by_core(3 - v0, 3)
    two = jnp.stack([pick(four, k0), pick(four, k1)])
    two = add(two, swap(jnp.stack([pick(four, s0), pick(four, s1)]), order0[0], order1[0]))
    v1 = by_core(0, bit(order1[1]))
    one = add(pick(two, v1), swap(pick(two, 1 - v1), order0[1], order1[1]))
    for a, b in zip(order0[2:], order1[2:]):
        one = add(one, swap(one, a, b))
    v2 = by_core(v0, bit(order1[1]))
    mine = in_order(one, swap(one, order0[0], order1[1]), v2)
    theirs = swap(mine, "core")
    both = in_order(mine, theirs, core)
    grad_up = jnp.concatenate([both[0, 0], both[1, 0]], axis=1).astype(F32)
    grad_down = jnp.concatenate([both[0, 1].T, both[1, 1].T], axis=0).astype(F32)

    part = add(pick(pay, core), swap(pick(pay, 1 - core), "core"))
    hr = part.shape[0] // 2
    part = part.reshape(2, hr, d)
    va = by_core(bit(order0[0]), bit(order1[0]))
    piece = add(pick(part, va), swap(pick(part, 1 - va), order0[0], order1[0]))
    for a, b in zip(order0[1:], order1[1:]):
        piece = add(piece, swap(piece, a, b))
    part = in_order(piece, swap(piece, order0[0], order1[0]), va).reshape(2 * hr, d)
    full = in_order(part, swap(part, "core"), core).astype(F32)

    in_grad = in_grad_of(dj, tokens, dattn, qkv_weight, row(ln1_gain), rows=512)

    small = full[0, 2 * d :]
    raw = jnp.concatenate([full[0, :d], full[0, d : 2 * d], full[1, :d]], axis=1)
    csum = small[2:5].reshape(1, 3 * d)
    grad_qkv = raw * ln1_gain.astype(F32)[:, None] + ln1_bias.astype(F32)[:, None] * csum
    gub = lax.dynamic_slice(small, (16 + 2 * y, 0), (2, d)).reshape(-1)
    return (
        layer_out,
        in_grad,
        small[0],
        small[1],
        grad_qkv,
        jnp.stack([small[2], small[4]]),
        full[1, d : 2 * d],
        small[5],
        small[6],
        small[7],
        grad_up,
        gub,
        grad_down,
        small[8],
    )


def solution(mesh):
    placed = (
        P(BOTH, None), P(BOTH, None), P(), P(), P(), P(), P(), P(), P(), P(),
        P(None, "mlp"), P("mlp"), P("mlp", None), P(), P(BOTH, None),
    )
    return jax.shard_map(
        functools.partial(local, mesh.shape["rows"]),
        mesh=mesh,
        in_specs=placed,
        out_specs=(
            P(BOTH, None), P(BOTH, None), P(), P(), P(), P(), P(), P(), P(), P(),
            P(None, "mlp"), P("mlp"), P("mlp", None), P(),
        ),
        check_vma=False,
    )
```

time: 689 us -> 222 us (0.32); the launches traced: 678 us -> 221 us
  waiting for transfers between devices: 255 us -> 52.2 us
  matrix products: 150 us -> 0 us
  local copies, waits for them, and re-layouts: 143 us -> 16.4 us
  Pallas kernels: 0 us -> 103 us
  blocking collectives: 73.6 us -> 0 us
  starting transfers between devices: 0.24 us -> 28.7 us
  other arithmetic: 40.5 us -> 20.1 us
  between operations: 15 us -> 0.93 us
    dot_general x40 -> x0, matrix products: 150 us -> none  [the longest x4 38.2 us: times_t(): lax.dot_general(left, right, (((1,), (1,)), ((), ())), preferred_element_...]
    all_gather x2 -> x0, waiting for transfers between devices: 106 us -> none  [the longest x1 58.8 us: local(): second_all = lax.all_gather(second_in, 'mlp', axis=0, tiled=True)]
    pallas_call x0 -> x5, Pallas kernels: none -> 103 us  [the longest x1 28.9 us: attn_bwd(): pl.pallas_call(attn_bwd_body, grid_spec=pltpu.PrefetchScalarGridSpec(num_...]
    psum x2 -> x0, waiting for transfers between devices: 75.8 us -> none  [the longest x1 75.8 us: local(): lax.psum((gain_one_part, bias_one_part, qkv_part, qv_part, out_weight_par...]
    psum x2 -> x0, blocking collectives: 73.6 us -> none  [the longest x1 39.8 us: local(): lax.psum((gain_one_part, bias_one_part, qkv_part, qv_part, out_weight_par...]
    reduce_scatter x2 -> x0, waiting for transfers between devices: 72.4 us -> none  [the longest x1 52 us: local(): lax.psum_scatter(jnp.dot(gated, down_all, preferred_element_type=jnp.floa...]
    unnamed x84 -> x28, local copies, waits for them, and re-layouts: 68.3 us -> 4.45 us
    ppermute x0 -> x17, waiting for transfers between devices: none -> 52.2 us  [swap(): return lax.ppermute(value, BOTH, pairs)]
  transfers between devices with their start and end apart: 6 -> 17, of which waited for: 5 -> 9; matrix products, arithmetic and copies ran while one was open for 30% -> 13% of each run, Pallas kernels for 0% -> 46%
where the time goes in v1:
time: 222 us; the launch traced here: 221 us
  Pallas kernels  103 us (46%)
  waiting for transfers between devices  52.2 us (24%)
  starting transfers between devices  28.7 us (13%)
  other arithmetic  20.1 us (9%)
  local copies, waits for them, and re-layouts  16.4 us (7%)
    ppermute x17, waiting for transfers between devices, swap(): return lax.ppermute(value, BOTH, pairs)  52.2 us
    pallas_call x1, Pallas kernels, attn_bwd(): pl.pallas_call(attn_bwd_body, grid_spec=pltpu.PrefetchScalarGridSpec(num_...  28.9 us
    ppermute x17, starting transfers between devices, swap(): return lax.ppermute(value, BOTH, pairs)  28.7 us
    pallas_call x1, Pallas kernels, ffn_other(): pl.pallas_call(ffn_other_body, grid=(t // rows,), in_specs=[rows_spec(row...  26.8 us
    pallas_call x1, Pallas kernels, ffn_own(): pl.pallas_call(ffn_own_body, grid_spec=pltpu.PrefetchScalarGridSpec(num_s...  22 us
    pallas_call x1, Pallas kernels, attn_fwd(): pl.pallas_call(attn_fwd_body, grid=(t // rows,), in_specs=[rows_spec(rows...  15.9 us
    convert_element_type x11, other arithmetic, add(): return (a.astype(F32) + b.astype(F32)).astype(BF)  9.51 us
    pallas_call x1, Pallas kernels, in_grad_of(): pl.pallas_call(in_grad_body, grid=(t // rows,), in_specs=[rows_spec(rows,...  9.17 us
  transfers between devices with their start and end apart: 17, of which 9 were waited for; matrix products, arithmetic and copies ran while one was open for 13% of the time, Pallas kernels for 46%

profile of v1, /device:TPU:0, one launch (start us, length us, event | category | flops | bytes accessed | tf_op | source)
XLA Modules:
  0.0 221.1 jit_solution(11089147352940555309)
XLA Ops:
  2.9 3.0 %collective-permute-start = (bf16[1040,512]{1,0:T(8,128)(2,1)S(1)}, bf16[1040,512]{1,0:T(8,128)(2,1)S(1)}, u32[]{:S(2)}, u32[]{:S(2)}) collective-permute-start(bf16[1040,512]{1,0:T(8,128)(2,1)S(1)} %pad_maximum_fusion.1), channel_id=1, source_target_pairs={{0,1},{1,0},{2,3},{3,2},{4,5},{5,4},{6,7},{7,6},{8,9},{9,8},{10,11... | collective-permute-start | bytes 3194888 | tf_op jit(solution)/shard_map/ppermute | solution.py:435
  10.1 15.9 %attn_fwd.1 = (bf16[2048,1536]{1,0:T(8,128)(2,1)}, bf16[2048,512]{1,0:T(8,128)(2,1)}, f32[2048,512]{1,0:T(8,128)}, bf16[2048,512]{1,0:T(8,128)(2,1)}) custom-call(bf16[2048,512]{1,0:T(8,128)(2,1)} %tok.5, s32[4,4,128]{2,1,0:T(4,128)} %bitcast.81, bf16[1,512]{1,0:T(2,128)(2,1)} %reshape.100.g1, bf16[1,512]{1,0:T(2,128)(2,1)} %reshape.101.b1, ...), custom_call_target="tpu_custom_call" | custom-call | flops 8589934592 | tf_op jit(solution)/shard_map/attn_fwd/pallas_call | solution.py:109
  25.9 3.5 %collective-permute-done.w_send = bf16[1040,512]{1,0:T(8,128)(2,1)S(1)} collective-permute-done((bf16[1040,512]{1,0:T(8,128)(2,1)S(1)}, bf16[1040,512]{1,0:T(8,128)(2,1)S(1)}, u32[]{:S(2)}, u32[]{:S(2)}) %collective-permute-start) | collective-permute-done | bytes 1064992 | tf_op jit(solution)/shard_map/ppermute | solution.py:435
  29.4 22.0 %ffn_own.1 = (f32[2048,512]{1,0:T(8,128)}, f32[2048,512]{1,0:T(8,128)}, bf16[2,512,512]{2,1,0:T(8,128)(2,1)}, bf16[2,512,512]{2,1,0:T(8,128)(2,1)}, f32[2,512]{1,0:T(2,128)}) custom-call(s32[1]{0:T(128)} %bitcast.1.core, bf16[2048,512]{1,0:T(8,128)(2,1)} %get-tuple-element.33.h2, bf16[2048,512]{1,0:T(8,128)(2,1)} %g.3, bf16[512,1024]{1,0:T(8,128)(2,1)} %up.1, ...), custom_call_target="tpu_custom_call" | custom-call | flops 25769803776 | tf_op jit(solution)/shard_map/ffn_own/pallas_call | solution.py:173
  53.9 26.8 %ffn_other.1 = (bf16[2048,512]{1,0:T(8,128)(2,1)}, bf16[2048,512]{1,0:T(8,128)(2,1)}, bf16[2048,512]{1,0:T(8,128)(2,1)}, bf16[2,512,512]{2,1,0:T(8,128)(2,1)}, b...) custom-call(bf16[2048,512]{1,0:T(8,128)(2,1)} %get-tuple-element.33.h2, ...), custom_call_target="tpu_custom_call" | custom-call | flops 30064771072 | tf_op jit(solution)/shard_map/ffn_other/pallas_call | solution.py:243
  80.7 28.9 %attn_bwd.1 = (bf16[2048,1536]{1,0:T(8,128)(2,1)}, bf16[2,1056,512]{2,1,0:T(8,128)(2,1)}) custom-call(s32[2]{0:T(128)} %pad_add_fusion.place, bf16[2048,1536]{1,0:T(8,128)(2,1)} %get-tuple-element.39.joined, bf16[2048,512]{1,0:T(8,128)(2,1)} %get-tuple-element.40.dctx, s32[4,4,128]{2,1,0:T(4,128)} %bitcast.82, bf16[2048,512]{1,0:T(8,128)(2,1)} %tok.5, ...), custom_call_target="tpu_custom_call" | custom-call | flops 10737418240 | tf_op jit(solution)/shard_map/attn_bwd/pallas_call | solution.py:336
  111.5 1.9 add_convert_fusion.2
  113.9 1.5 fusion.1
  115.5 2.1 collective-permute-start.3
  117.7 1.5 add_convert_fusion.1
  121.1 3.9 %collective-permute-done.3 = bf16[528,512]{1,0:T(8,128)(2,1)S(1)} collective-permute-done((bf16[528,512]{1,0:T(8,128)(2,1)S(1)}, bf16[528,512]{1,0:T(8,128)(2,1)S(1)}, u32[]{:S(2)}, u32[]{:S(2)}) %collective-permute-start.3) | collective-permute-done | bytes 540704 | tf_op jit(solution)/shard_map/ppermute | solution.py:435
  125.1 1.8 collective-permute-start.4
  127.0 13.4 %collective-permute-done.4 = bf16[528,512]{1,0:T(8,128)(2,1)S(1)} collective-permute-done((bf16[528,512]{1,0:T(8,128)(2,1)S(1)}, bf16[528,512]{1,0:T(8,128)(2,1)S(1)}, u32[]{:S(2)}, u32[]{:S(2)}) %collective-permute-start.4) | collective-permute-done | bytes 540704 | tf_op jit(solution)/shard_map/ppermute | solution.py:435
  140.6 1.9 collective-permute-start.5
  143.4 1.5 add_convert_fusion
  145.0 1.6 collective-permute-start.12
  146.6 6.9 %collective-permute-done.5 = bf16[528,512]{1,0:T(8,128)(2,1)} collective-permute-done((bf16[528,512]{1,0:T(8,128)(2,1)S(1)}, bf16[528,512]{1,0:T(8,128)(2,1)}, u32[]{:S(2)}, u32[]{:S(2)}) %collective-permute-start.5) | collective-permute-done | bytes 540704 | tf_op jit(solution)/shard_map/ppermute | solution.py:435
  154.7 3.8 %collective-permute-start.6 = (bf16[528,512]{1,0:T(8,128)(2,1)S(1)}, bf16[528,512]{1,0:T(8,128)(2,1)}, u32[]{:S(2)}, u32[]{:S(2)}) collective-permute-start(bf16[528,512]{1,0:T(8,128)(2,1)S(1)} %add_convert_fusion.4), channel_id=1, source_target_pairs={{0,24},{1,25},{2,6},{3,7},{4,28},{5,29},{6,2},{7,3},{8,16},{9,17},... | collective-permute-start | bytes 1622024 | tf_op jit(solution)/shard_map/ppermute | solution.py:435
  158.7 13.1 %collective-permute-done.6 = bf16[528,512]{1,0:T(8,128)(2,1)} collective-permute-done((bf16[528,512]{1,0:T(8,128)(2,1)S(1)}, bf16[528,512]{1,0:T(8,128)(2,1)}, u32[]{:S(2)}, u32[]{:S(2)}) %collective-permute-start.6) | collective-permute-done | bytes 540704 | tf_op jit(solution)/shard_map/ppermute | solution.py:435
  173.0 2.0 collective-permute-start.7
  175.0 2.2 collective-permute-done.13
  177.4 2.2 collective-permute-start.14
  179.6 6.4 %collective-permute-done.7 = bf16[528,512]{1,0:T(8,128)(2,1)S(1)} collective-permute-done((bf16[528,512]{1,0:T(8,128)(2,1)S(1)}, bf16[528,512]{1,0:T(8,128)(2,1)S(1)}, u32[]{:S(2)}, u32[]{:S(2)}) %collective-permute-start.7) | collective-permute-done | bytes 540704 | tf_op jit(solution)/shard_map/ppermute | solution.py:435
  186.2 2.2 %collective-permute-done.14 = bf16[512,512]{1,0:T(8,128)(2,1)S(1)} collective-permute-done((bf16[512,512]{1,0:T(8,128)(2,1)S(1)}, bf16[512,512]{1,0:T(8,128)(2,1)S(1)}, u32[]{:S(2)}, u32[]{:S(2)}) %collective-permute-start.14) | collective-permute-done | bytes 524320 | tf_op jit(solution)/shard_map/ppermute | solution.py:435
  188.6 2.1 collective-permute-start.15
  190.7 9.2 %in_grad.1 = bf16[2048,512]{1,0:T(8,128)(2,1)} custom-call(bf16[2048,1536]{1,0:T(8,128)(2,1)} %get-tuple-element.45.dj, bf16[2048,512]{1,0:T(8,128)(2,1)} %tok.5, bf16[2048,512]{1,0:T(8,128)(2,1)} %get-tuple-element.46.dattn, bf16[512,1536]{1,0:T(8,128)(2,1)} %wqkv.5, bf16[1,512]{1,0:T(2,128)(2,1)} %reshape.100.g1), custom_call_target="tpu_custom_call" | custom-call | flops 6442450944 | tf_op jit(solution)/shard_map/in_grad/pallas_call | solution.py:366
  200.0 7.1 %collective-permute-start.16 = (bf16[2,512,512]{2,1,0:T(8,128)(2,1)S(1)}, bf16[2,512,512]{2,1,0:T(8,128)(2,1)S(1)}, u32[]{:S(2)}, u32[]{:S(2)}) collective-permute-start(bf16[2,512,512]{2,1,0:T(8,128)(2,1)S(1)} %pad_maximum_fusion.3), channel_id=1, source_target_pairs={{0,2},{1,3},{2,0},{3,1},{4,6},{5,7},{6,4},{7,5},{8,10},{9,11},{10,... | collective-permute-start | bytes 3145736 | tf_op jit(solution)/shard_map/ppermute | solution.py:435
  207.9 2.3 %maximum_convert_fusion = f32[2,1056,512]{2,1,0:T(8,128)} fusion(bf16[1,1056,512]{2,1,0:T(8,128)(2,1)S(1)} %get-tuple-element.95, bf16[1,1056,512]{2,1,0:T(8,128)(2,1)S(1)} %get-tuple-element.94), kind=kLoop, calls=%fused_computation.10 | loop fusion | flops 2162688 | bytes 6488064 | tf_op jit(solution)/shard_map/convert_element_type | solution.py:507
  211.4 3.6 %slice_bitcast_fusion = (f32[512,512]{1,0:T(8,128)}, f32[512,512]{1,0:T(8,128)S(1)}, f32[512,512]{1,0:T(8,128)S(1)}, f32[512,512]{1,0:T(8,128)S(1)}) fusion(f32[2,1056,512]{2,1,0:T(8,128)} %maximum_convert_fusion), kind=kLoop, calls=%fused_computation.26 | loop fusion | bytes 8388608 | tf_op jit(solution)/shard_map/squeeze | solution.py:523
  215.0 2.1 fusion
  217.7 1.8 copy.30
  219.5 1.6 maximum_convert_fusion.1
  (87 shorter events, 20.2 us)
Async XLA Ops:
  1.4 4.5 %copy-start.4 = (bf16[1024]{0:T(1024)(128)(2,1)S(1)}, bf16[1024]{0:T(1024)(128)(2,1)}, u32[]{:S(2)}) copy-start(bf16[1024]{0:T(1024)(128)(2,1)} %param.26) | copy-start | bytes 6148
  1.4 5.1 %copy-start.3 = (bf16[2,512]{1,0:T(2,128)(2,1)S(1)}, bf16[2,512]{1,0:T(2,128)(2,1)}, u32[]{:S(2)}) copy-start(bf16[2,512]{1,0:T(2,128)(2,1)} %param.20) | copy-start | bytes 6148
  1.4 5.8 %copy-start.5 = (bf16[512]{0:T(512)(128)(2,1)S(1)}, bf16[512]{0:T(512)(128)(2,1)}, u32[]{:S(2)}) copy-start(bf16[512]{0:T(512)(128)(2,1)} %param.17) | copy-start | bytes 3076
  1.4 6.3 %copy-start.7 = (bf16[512]{0:T(512)(128)(2,1)S(1)}, bf16[512]{0:T(512)(128)(2,1)}, u32[]{:S(2)}) copy-start(bf16[512]{0:T(512)(128)(2,1)} %param.23) | copy-start | bytes 3076
  1.4 6.9 %copy-start.6 = (bf16[512]{0:T(512)(128)(2,1)S(1)}, bf16[512]{0:T(512)(128)(2,1)}, u32[]{:S(2)}) copy-start(bf16[512]{0:T(512)(128)(2,1)} %param.18) | copy-start | bytes 3076
  1.4 7.5 %copy-start.8 = (bf16[512]{0:T(512)(128)(2,1)S(1)}, bf16[512]{0:T(512)(128)(2,1)}, u32[]{:S(2)}) copy-start(bf16[512]{0:T(512)(128)(2,1)} %param.22) | copy-start | bytes 3076
  1.4 8.1 %copy-start.9 = (bf16[512]{0:T(512)(128)(2,1)S(1)}, bf16[512]{0:T(512)(128)(2,1)}, u32[]{:S(2)}) copy-start(bf16[512]{0:T(512)(128)(2,1)} %param.24) | copy-start | bytes 3076
  2.9 26.5 %collective-permute-start = (bf16[1040,512]{1,0:T(8,128)(2,1)S(1)}, bf16[1040,512]{1,0:T(8,128)(2,1)S(1)}, u32[]{:S(2)}, u32[]{:S(2)}) collective-permute-start(bf16[1040,512]{1,0:T(8,128)(2,1)S(1)} %pad_maximum_fusion.1), channel_id=1, source_target_pairs={{0,1},{1,0},{2,3},{3,2},{4,5},{5,4},{6,7},{7,6},{8,9},{9,8},{10,11... | collective-permute-start | bytes 3194888 | tf_op jit(solution)/shard_map/ppermute | solution.py:435
  29.4 22.0 %copy-start.11 = (bf16[1040,512]{1,0:T(8,128)(2,1)}, bf16[1040,512]{1,0:T(8,128)(2,1)S(1)}, u32[]{:S(2)}) copy-start(bf16[1040,512]{1,0:T(8,128)(2,1)S(1)} %collective-permute-done.w_send) | copy-start | bytes 3194884
  29.4 23.4 %collective-permute-start.1 = (bf16[1040,512]{1,0:T(8,128)(2,1)S(1)}, bf16[1040,512]{1,0:T(8,128)(2,1)S(1)}, u32[]{:S(2)}, u32[]{:S(2)}) collective-permute-start(bf16[1040,512]{1,0:T(8,128)(2,1)S(1)} %collective-permute-done.w_send), channel_id=1, source_target_pairs={{0,2},{1,3},{2,0},{3,1},{4,6},{5,7},{6,4},{7,5},{8,10},{9,11},{10,... | collective-permute-start | bytes 3194888 | tf_op jit(solution)/shard_map/ppermute | solution.py:435
  29.4 22.3 %copy-start.10 = (bf16[512]{0:T(512)(128)(2,1)S(1)}, bf16[512]{0:T(512)(128)(2,1)}, u32[]{:S(2)}) copy-start(bf16[512]{0:T(512)(128)(2,1)} %param.28) | copy-start | bytes 3076
  51.5 60.0 %collective-permute-start.9 = (bf16[2,512,512]{2,1,0:T(8,128)(2,1)}, bf16[2,512,512]{2,1,0:T(8,128)(2,1)}, u32[]{:S(2)}, u32[]{:S(2)}) collective-permute-start(bf16[2,512,512]{2,1,0:T(8,128)(2,1)} %get-tuple-element.49), channel_id=1, source_target_pairs={{0,2},{1,3},{2,0},{3,1},{4,6},{5,7},{6,4},{7,5},{8,10},{9,11},{10,... | collective-permute-start | bytes 3145736 | tf_op jit(solution)/shard_map/ppermute | solution.py:435
  52.9 1.0 copy-start.12
  110.9 3.0 %copy-start = (bf16[2,1056,512]{2,1,0:T(8,128)(2,1)S(1)}, bf16[2,1056,512]{2,1,0:T(8,128)(2,1)}, u32[]{:S(2)}) copy-start(bf16[2,1056,512]{2,1,0:T(8,128)(2,1)} %get-tuple-element.47) | copy-start | bytes 6488068
  110.9 3.0 %collective-permute-start.2 = (bf16[1056,512]{1,0:T(8,128)(2,1)S(1)}, bf16[1056,512]{1,0:T(8,128)(2,1)}, u32[]{:S(2)}, u32[]{:S(2)}) collective-permute-start(bf16[1056,512]{1,0:T(8,128)(2,1)S(1)} %dynamic-slice_bitcast_fusion), channel_id=1, source_target_pairs={{0,2},{1,3},{2,0},{3,1},{4,6},{5,7},{6,4},{7,5},{8,10},{9,11},{10,... | collective-permute-start | bytes 3244040 | tf_op jit(solution)/shard_map/ppermute | solution.py:435
  111.4 6.3 %collective-permute-start.10 = (bf16[2,512,512]{2,1,0:T(8,128)(2,1)}, bf16[2,512,512]{2,1,0:T(8,128)(2,1)}, u32[]{:S(2)}, u32[]{:S(2)}) collective-permute-start(bf16[2,512,512]{2,1,0:T(8,128)(2,1)} %get-tuple-element.51), channel_id=1, source_target_pairs={{0,2},{1,3},{2,0},{3,1},{4,6},{5,7},{6,4},{7,5},{8,10},{9,11},{10,... | collective-permute-start | bytes 3145736 | tf_op jit(solution)/shard_map/ppermute | solution.py:435
  113.4 4.3 %copy-start.1 = (bf16[2,512,512]{2,1,0:T(8,128)(2,1)S(1)}, bf16[2,512,512]{2,1,0:T(8,128)(2,1)}, u32[]{:S(2)}) copy-start(bf16[2,512,512]{2,1,0:T(8,128)(2,1)} %get-tuple-element.50) | copy-start | bytes 3145732
  115.5 9.5 %collective-permute-start.3 = (bf16[528,512]{1,0:T(8,128)(2,1)S(1)}, bf16[528,512]{1,0:T(8,128)(2,1)S(1)}, u32[]{:S(2)}, u32[]{:S(2)}) collective-permute-start(bf16[528,512]{1,0:T(8,128)(2,1)S(1)} %dynamic-slice_bitcast_fusion.1), channel_id=1, source_target_pairs={{0,4},{1,5},{2,3},{3,2},{4,0},{5,1},{6,7},{7,6},{8,12},{9,13},{10,... | collective-permute-start | bytes 1622024 | tf_op jit(solution)/shard_map/ppermute | solution.py:435
  121.0 21.4 %collective-permute-start.11 = (bf16[2,512,512]{2,1,0:T(8,128)(2,1)}, bf16[2,512,512]{2,1,0:T(8,128)(2,1)S(1)}, u32[]{:S(2)}, u32[]{:S(2)}) collective-permute-start(bf16[2,512,512]{2,1,0:T(8,128)(2,1)} %pad_maximum_fusion.2), channel_id=1, source_target_pairs={{0,4},{1,5},{2,3},{3,2},{4,0},{5,1},{6,7},{7,6},{8,12},{9,13},{10,... | collective-permute-start | bytes 3145736 | tf_op jit(solution)/shard_map/ppermute | solution.py:435
  125.1 15.3 %collective-permute-start.4 = (bf16[528,512]{1,0:T(8,128)(2,1)S(1)}, bf16[528,512]{1,0:T(8,128)(2,1)S(1)}, u32[]{:S(2)}, u32[]{:S(2)}) collective-permute-start(bf16[528,512]{1,0:T(8,128)(2,1)S(1)} %fusion.2), channel_id=1, source_target_pairs={{0,1},{1,0},{2,10},{3,11},{4,5},{5,4},{6,14},{7,15},{8,9},{9,8},{1... | collective-permute-start | bytes 1622024 | tf_op jit(solution)/shard_map/ppermute | solution.py:435
  140.6 12.9 %collective-permute-start.5 = (bf16[528,512]{1,0:T(8,128)(2,1)S(1)}, bf16[528,512]{1,0:T(8,128)(2,1)}, u32[]{:S(2)}, u32[]{:S(2)}) collective-permute-start(bf16[528,512]{1,0:T(8,128)(2,1)S(1)} %add_convert_fusion.5), channel_id=1, source_target_pairs={{0,8},{1,9},{2,26},{3,27},{4,12},{5,13},{6,30},{7,31},{8,0},{9,1},... | collective-permute-start | bytes 1622024 | tf_op jit(solution)/shard_map/ppermute | solution.py:435
  142.5 1.0 copy-start.2
  145.0 13.5 %collective-permute-start.12 = (bf16[512,512]{1,0:T(8,128)(2,1)S(1)}, bf16[512,512]{1,0:T(8,128)(2,1)S(1)}, u32[]{:S(2)}, u32[]{:S(2)}) collective-permute-start(bf16[512,512]{1,0:T(8,128)(2,1)S(1)} %dynamic-slice_bitcast_fusion.2), channel_id=1, source_target_pairs={{0,1},{1,0},{2,10},{3,11},{4,5},{5,4},{6,14},{7,15},{8,9},{9,8},{1... | collective-permute-start | bytes 1572872 | tf_op jit(solution)/shard_map/ppermute | solution.py:435
  154.7 17.1 %collective-permute-start.6 = (bf16[528,512]{1,0:T(8,128)(2,1)S(1)}, bf16[528,512]{1,0:T(8,128)(2,1)}, u32[]{:S(2)}, u32[]{:S(2)}) collective-permute-start(bf16[528,512]{1,0:T(8,128)(2,1)S(1)} %add_convert_fusion.4), channel_id=1, source_target_pairs={{0,24},{1,25},{2,6},{3,7},{4,28},{5,29},{6,2},{7,3},{8,16},{9,17},... | collective-permute-start | bytes 1622024 | tf_op jit(solution)/shard_map/ppermute | solution.py:435
  158.7 18.6 %collective-permute-start.13 = (bf16[512,512]{1,0:T(8,128)(2,1)S(1)}, bf16[512,512]{1,0:T(8,128)(2,1)S(1)}, u32[]{:S(2)}, u32[]{:S(2)}) collective-permute-start(bf16[512,512]{1,0:T(8,128)(2,1)S(1)} %fusion.3), channel_id=1, source_target_pairs={{0,8},{1,9},{2,26},{3,27},{4,12},{5,13},{6,30},{7,31},{8,0},{9,1},... | collective-permute-start | bytes 1572872 | tf_op jit(solution)/shard_map/ppermute | solution.py:435
  173.0 12.9 %collective-permute-start.7 = (bf16[528,512]{1,0:T(8,128)(2,1)S(1)}, bf16[528,512]{1,0:T(8,128)(2,1)S(1)}, u32[]{:S(2)}, u32[]{:S(2)}) collective-permute-start(bf16[528,512]{1,0:T(8,128)(2,1)S(1)} %add_convert_fusion.3), channel_id=1, source_target_pairs={{0,4},{1,5},{2,3},{3,2},{4,0},{5,1},{6,7},{7,6},{8,12},{9,13},{10,... | collective-permute-start | bytes 1622024 | tf_op jit(solution)/shard_map/ppermute | solution.py:435
  177.4 11.0 %collective-permute-start.14 = (bf16[512,512]{1,0:T(8,128)(2,1)S(1)}, bf16[512,512]{1,0:T(8,128)(2,1)S(1)}, u32[]{:S(2)}, u32[]{:S(2)}) collective-permute-start(bf16[512,512]{1,0:T(8,128)(2,1)S(1)} %add_convert_fusion.7), channel_id=1, source_target_pairs={{0,24},{1,25},{2,6},{3,7},{4,28},{5,29},{6,2},{7,3},{8,16},{9,17},... | collective-permute-start | bytes 1572872 | tf_op jit(solution)/shard_map/ppermute | solution.py:435
  186.1 21.0 %collective-permute-start.8 = (bf16[1056,512]{1,0:T(8,128)(2,1)S(1)}, bf16[1056,512]{1,0:T(8,128)(2,1)S(1)}, u32[]{:S(2)}, u32[]{:S(2)}) collective-permute-start(bf16[1056,512]{1,0:T(8,128)(2,1)S(1)} %bitcast.71), channel_id=1, source_target_pairs={{0,2},{1,3},{2,0},{3,1},{4,6},{5,7},{6,4},{7,5},{8,10},{9,11},{10,... | collective-permute-start | bytes 3244040 | tf_op jit(solution)/shard_map/ppermute | solution.py:435
  188.6 11.3 %collective-permute-start.15 = (bf16[512,512]{1,0:T(8,128)(2,1)S(1)}, bf16[512,512]{1,0:T(8,128)(2,1)S(1)}, u32[]{:S(2)}, u32[]{:S(2)}) collective-permute-start(bf16[512,512]{1,0:T(8,128)(2,1)S(1)} %add_convert_fusion.6), channel_id=1, source_target_pairs={{0,4},{1,5},{2,10},{3,11},{4,0},{5,1},{6,14},{7,15},{8,12},{9,13},... | collective-permute-start | bytes 1572872 | tf_op jit(solution)/shard_map/ppermute | solution.py:435
  200.0 17.1 %collective-permute-start.16 = (bf16[2,512,512]{2,1,0:T(8,128)(2,1)S(1)}, bf16[2,512,512]{2,1,0:T(8,128)(2,1)S(1)}, u32[]{:S(2)}, u32[]{:S(2)}) collective-permute-start(bf16[2,512,512]{2,1,0:T(8,128)(2,1)S(1)} %pad_maximum_fusion.3), channel_id=1, source_target_pairs={{0,2},{1,3},{2,0},{3,1},{4,6},{5,7},{6,4},{7,5},{8,10},{9,11},{10,... | collective-permute-start | bytes 3145736 | tf_op jit(solution)/shard_map/ppermute | solution.py:435

commit v2 on v1

v2 whole, which is shorter than its diff:
```python
import functools
import math

import jax
import jax.numpy as jnp
from jax import lax
from jax.experimental import pallas as pl
from jax.experimental.pallas import tpu as pltpu
from jax.sharding import PartitionSpec as P

BF, F32 = jnp.bfloat16, jnp.float32
SEQ, HD, FRAME = 128, 64, 4
EPS = 1e-5
C0 = math.sqrt(2.0 / math.pi)
C1 = C0 * 0.044715
LIMIT = 20 * 1024 * 1024
BOTH = ("rows", "mlp")
SCALE = 8


def mm(a, b, ca=1, cb=0):
    return lax.dot_general(a, b, (((ca,), (cb,)), ((), ())), preferred_element_type=F32)


def layer_norm(x):
    c = x - jnp.mean(x, axis=-1, keepdims=True)
    inv = lax.rsqrt(jnp.mean(c * c, axis=-1, keepdims=True) + EPS)
    return c * inv, inv


def norm_back(grad, normed, inv, gain):
    s = grad * gain
    return inv * (
        s
        - jnp.mean(s, axis=-1, keepdims=True)
        - normed * jnp.mean(s * normed, axis=-1, keepdims=True)
    )


def fold(v):
    return jnp.sum(v.reshape(-1, 8, v.shape[-1]), axis=0)


def stack_heads(v):
    low = lax.broadcasted_iota(jnp.int32, v.shape, 1) < HD
    zero = jnp.zeros_like(v)
    return jnp.concatenate([jnp.where(low, v, zero), jnp.where(low, zero, v)], axis=0)


def allowed_of(seg_row, transposed):
    wide = jnp.broadcast_to(seg_row.astype(F32), (SEQ, SEQ))
    same = wide == wide.T
    a = lax.broadcasted_iota(jnp.int32, (SEQ, SEQ), 1 if transposed else 0)
    b = lax.broadcasted_iota(jnp.int32, (SEQ, SEQ), 0 if transposed else 1)
    return same & (a // FRAME >= b // FRAME)


def whole(a):
    zeros = (0,) * len(a.shape)
    return pl.BlockSpec(a.shape, lambda i, *_: zeros)


def rows_spec(r, w):
    return pl.BlockSpec((r, w), lambda i, *_: (i, 0))


def shape(s, dtype):
    return jax.ShapeDtypeStruct(s, dtype)


def in_hbm(s, dtype):
    return pltpu.HBM(s, dtype)


def cost(macs, nbytes=0):
    return pl.CostEstimate(flops=macs // SCALE, bytes_accessed=nbytes // SCALE, transcendentals=0)


def slab(ref, r, c):
    return ref[r, c * 128 : (c + 1) * 128]


def attn_fwd_body(tok, seg, vecs, wqkv, wo, joined_o, ctx_o, resid_o, h2_o, n1t_o):
    rows, width = tok.shape
    pairs = width // 128
    vec = vecs[...].astype(F32)
    g1, b1, bo, g2, b2, bq, bv = (vec[j : j + 1] for j in range(7))
    x = tok[...].astype(F32)
    n1, _ = layer_norm(x)
    n1t_o[...] = n1.astype(BF).T
    h1 = (n1 * g1 + b1).astype(BF)
    bias = jnp.concatenate([bq, jnp.zeros_like(bq), bv], axis=1)
    joined = (mm(h1, wqkv[...]) + bias).astype(BF)
    joined_o[...] = joined
    group = 2
    done = []
    for s0 in range(0, rows // SEQ, group):
        items = [(s, p) for s in range(s0, s0 + group) for p in range(pairs)]
        allow = {s: allowed_of(seg[0, s : s + 1, :], True) for s in range(s0, s0 + group)}

        def part(s, o, p):
            return joined[s * SEQ : (s + 1) * SEQ, o * width + p * 128 : o * width + (p + 1) * 128]

        scores = [mm(part(s, 1, p), stack_heads(part(s, 0, p) * BF(0.125)), 1, 1) for s, p in items]
        probs = []
        for (s, p), sc in zip(items, scores):
            two = []
            for h in range(2):
                v = jnp.where(allow[s], sc[:, h * SEQ : (h + 1) * SEQ], -1e9)
                e = jnp.exp(v - jnp.max(v, axis=0, keepdims=True))
                two.append((e * (1.0 / jnp.sum(e, axis=0, keepdims=True))).astype(BF))
            probs.append(jnp.concatenate(two, axis=0))
        outs = [mm(pr, stack_heads(part(s, 2, p)), 0, 0).astype(BF) for (s, p), pr in zip(items, probs)]
        for j in range(group):
            done.append(jnp.concatenate(outs[j * pairs : (j + 1) * pairs], axis=1))
    ctx = jnp.concatenate(done, axis=0)
    ctx_o[...] = ctx
    resid = x + mm(ctx, wo[...]) + bo
    resid_o[...] = resid
    n2, _ = layer_norm(resid)
    h2_o[...] = (n2 * g2 + b2).astype(BF)


def attn_fwd(tok, seg, vecs, wqkv, wo, rows):
    t, d = tok.shape
    return pl.pallas_call(
        attn_fwd_body,
        grid=(t // rows,),
        in_specs=[rows_spec(rows, d), pl.BlockSpec((1, rows // SEQ, SEQ), lambda i: (i, 0, 0))]
        + [whole(a) for a in (vecs, wqkv, wo)],
        out_specs=[rows_spec(rows, w) for w in (3 * d, d, d, d)] + [pl.BlockSpec((d, rows), lambda i: (0, i))],
        out_shape=[in_hbm((t, 3 * d), BF), in_hbm((t, d), BF), in_hbm((t, d), F32), shape((t, d), BF), in_hbm((d, t), BF)],
        compiler_params=pltpu.CompilerParams(vmem_limit_bytes=LIMIT),
        cost_estimate=cost(3 * t * d * 4 * d),
        name="attn_fwd",
    )(tok, seg.reshape(t // rows, rows // SEQ, SEQ), vecs, wqkv, wo)


def ffn_block(hv, gv, up, ub, down, chunk, gated_o, gup, gdn, gub):
    d, f = up.shape
    cuts = [slice(c * chunk, (c + 1) * chunk) for c in range(f // chunk)]
    ahead = [(mm(hv, up[:, s]), mm(gv, down[s, :], 1, 1)) for s in cuts]
    gates, slopes = [], []
    for s, (v, dg) in zip(cuts, ahead):
        v = v + ub[:, s]
        v2 = v * v
        a = 0.5 + 0.5 * jnp.tanh(v * (C0 + C1 * v2))
        act = v * a
        slope = a + act * (1.0 - a) * (2.0 * C0 + 6.0 * C1 * v2)
        dh = (dg * slope).astype(BF)
        gates.append(act.astype(BF))
        slopes.append(dh)
        gub[:, s] += fold(dh.astype(F32))
    gated, dhid = jnp.concatenate(gates, axis=1), jnp.concatenate(slopes, axis=1)
    gated_o[...] = gated
    gup[...] += mm(hv.T, dhid)
    gdn[...] += mm(gv.T, gated)
    return mm(dhid, up[...], 1, 1)


def ffn_own_body(core, h2, g, up, ub, down, gated_o, dh2_o, keep_o, send_o, gub_o, gup, gdn, gub):
    i = pl.program_id(0)
    half = up.shape[1] // 2

    @pl.when(i == 0)
    def _():
        for a in (gup, gdn, gub):
            a[...] = jnp.zeros_like(a)

    bias = jnp.concatenate([ub[j : j + 1] for j in range(2)], axis=1).astype(F32)
    dh2_o[...] = ffn_block(h2[...], g[...], up, bias, down, 256, gated_o, gup, gdn, gub)

    @pl.when(i == pl.num_programs(0) - 1)
    def _():
        mine = pl.ds(pl.multiple_of(core[0] * half, 128), half)
        theirs = pl.ds(pl.multiple_of((1 - core[0]) * half, 128), half)
        keep_o[0] = gup[:, mine].astype(BF)
        keep_o[1] = gdn[:, mine].astype(BF)
        send_o[0] = gup[:, theirs].astype(BF)
        send_o[1] = gdn[:, theirs].astype(BF)
        total = jnp.sum(gub[...], axis=0, keepdims=True)
        for j in range(2):
            gub_o[j : j + 1] = total[:, j * half : (j + 1) * half]


def ffn_outs(t, d, f):
    half = f // 2
    return [in_hbm((t, f), BF), pltpu.VMEM((t, d), F32), shape((2, d, half), BF), shape((2, d, half), BF), shape((2, half), F32)]


def ffn_scratch(d, f):
    return [pltpu.VMEM((d, f), F32), pltpu.VMEM((d, f), F32), pltpu.VMEM((8, f), F32)]


def ffn_own(core, h2, g, up, ub, down, rows):
    t, d = h2.shape
    f = up.shape[1]
    outs = ffn_outs(t, d, f)
    return pl.pallas_call(
        ffn_own_body,
        grid_spec=pltpu.PrefetchScalarGridSpec(
            num_scalar_prefetch=1,
            grid=(t // rows,),
            in_specs=[rows_spec(rows, d), rows_spec(rows, d), whole(up), whole(ub), whole(down)],
            out_specs=[rows_spec(rows, f), rows_spec(rows, d)] + [whole(o) for o in outs[2:]],
            scratch_shapes=ffn_scratch(d, f),
        ),
        out_shape=outs,
        compiler_params=pltpu.CompilerParams(vmem_limit_bytes=LIMIT),
        cost_estimate=cost(2 * 5 * t * d * f),
        name="ffn_own",
    )(core, h2, g, up, ub, down)


def ffn_other_body(h2, g, w_send, w_keep, dh2_p, gated_o, dh2_o, keep_o, send_o, gub_o, gup, gdn, gub, up, down, ub):
    i = pl.program_id(0)
    d = h2.shape[1]
    half = w_send.shape[1]

    @pl.when(i == 0)
    def _():
        for a in (gup, gdn, gub):
            a[...] = jnp.zeros_like(a)
        for c, w in enumerate((w_send, w_keep)):
            up[:, c * half : (c + 1) * half] = w[0:d, :]
            down[c * half : (c + 1) * half, :] = w[d : d + half, :]
            ub[:, c * half : (c + 1) * half] = w[d + half : d + half + 16, :].astype(F32)[0:8]

    dh2_o[...] = dh2_p[...] + ffn_block(h2[...], g[...], up, ub[0:1], down, 256, gated_o, gup, gdn, gub)

    @pl.when(i == pl.num_programs(0) - 1)
    def _():
        send_o[0] = gup[:, 0:half].astype(BF)
        send_o[1] = gdn[:, 0:half].astype(BF)
        keep_o[0] = gup[:, half:].astype(BF)
        keep_o[1] = gdn[:, half:].astype(BF)
        total = jnp.sum(gub[...], axis=0, keepdims=True)
        for j in range(2):
            gub_o[j : j + 1] = total[:, j * half : (j + 1) * half]


def ffn_other(h2, g, w_send, w_keep, dh2_p, rows):
    t, d = h2.shape
    f = 2 * w_send.shape[1]
    outs = ffn_outs(t, d, f)
    return pl.pallas_call(
        ffn_other_body,
        grid=(t // rows,),
        in_specs=[rows_spec(rows, d), rows_spec(rows, d), whole(w_send), whole(w_keep), rows_spec(rows, d)],
        out_specs=[rows_spec(rows, f), rows_spec(rows, d)] + [whole(o) for o in outs[2:]],
        out_shape=outs,
        scratch_shapes=ffn_scratch(d, f) + [pltpu.VMEM((d, f), BF), pltpu.VMEM((f, d), BF), pltpu.VMEM((8, f), F32)],
        compiler_params=pltpu.CompilerParams(vmem_limit_bytes=LIMIT),
        cost_estimate=cost(2 * 5 * t * d * f),
        name="ffn_other",
    )(h2, g, w_send, w_keep, dh2_p)


def mid_body(dh2, resid, g, ctx, wo, vecs, dattn_o, dctx_o, gout_o, vec_o, gout, vec):
    i = pl.program_id(0)

    @pl.when(i == 0)
    def _():
        gout[...] = jnp.zeros_like(gout)
        vec[...] = jnp.zeros_like(vec)

    dh = dh2[...]
    n2, inv2 = layer_norm(resid[...])
    gf = g[...].astype(F32)
    dattn = (gf + norm_back(dh, n2, inv2, vecs[...].astype(F32)[3:4])).astype(BF)
    dattn_o[...] = dattn
    dctx_o[...] = mm(dattn, wo[...], 1, 1).astype(BF)
    gout[...] += mm(ctx[...].T, dattn)
    for j, v in enumerate((dattn.astype(F32), dh * n2, dh, gf)):
        vec[j] += fold(v)

    @pl.when(i == pl.num_programs(0) - 1)
    def _():
        gout_o[...] = gout[...].astype(BF)
        for j in range(4):
            vec_o[j : j + 1] = jnp.sum(vec[j], axis=0, keepdims=True)


def mid(dh2, resid, g, ctx, wo, vecs, rows):
    t, d = dh2.shape
    outs = [pltpu.VMEM((t, d), BF), pltpu.VMEM((t, d), BF), shape((d, d), BF), shape((4, d), F32)]
    return pl.pallas_call(
        mid_body,
        grid=(t // rows,),
        in_specs=[rows_spec(rows, d)] * 4 + [whole(wo), whole(vecs)],
        out_specs=[rows_spec(rows, d)] * 2 + [whole(o) for o in outs[2:]],
        out_shape=outs,
        scratch_shapes=[pltpu.VMEM((d, d), F32), pltpu.VMEM((4, 8, d), F32)],
        compiler_params=pltpu.CompilerParams(vmem_limit_bytes=LIMIT),
        cost_estimate=cost(3 * 2 * t * d * d),
        name="mid",
    )(dh2, resid, g, ctx, wo, vecs)


def attn_bwd_block(q, k, v, dc, seg, dj_o):
    rows, width = q.shape
    pairs = width // 128
    group = 2
    for s0 in range(0, rows // SEQ, group):
        items = [(slice(s * SEQ, (s + 1) * SEQ), p) for s in range(s0, s0 + group) for p in range(pairs)]
        allow = [allowed_of(seg[0, s : s + 1, :], True) for s in range(s0, s0 + group) for p in range(pairs)]
        qs = [stack_heads(slab(q, r, p) * BF(0.125)) for r, p in items]
        dcs = [stack_heads(slab(dc, r, p)) for r, p in items]
        scores = [mm(slab(k, r, p), a, 1, 1) for (r, p), a in zip(items, qs)]
        dprobs = [mm(slab(v, r, p), a, 1, 1) for (r, p), a in zip(items, dcs)]
        probs, dscores = [], []
        for ok, sc, dp in zip(allow, scores, dprobs):
            pb, ds = [], []
            for h in range(2):
                cols = slice(h * SEQ, (h + 1) * SEQ)
                w = jnp.where(ok, sc[:, cols], -1e9)
                e = jnp.exp(w - jnp.max(w, axis=0, keepdims=True))
                pr = e * (1.0 / jnp.sum(e, axis=0, keepdims=True))
                ds.append((pr * (dp[:, cols] - jnp.sum(pr * dp[:, cols], axis=0, keepdims=True))).astype(BF))
                pb.append(pr.astype(BF))
            probs.append(pb)
            dscores.append(ds)
        for (r, p), pb, a in zip(items, probs, dcs):
            dj_o[r, 2 * width + p * 128 : 2 * width + (p + 1) * 128] = mm(jnp.concatenate(pb, axis=1), a).astype(BF)
        for (r, p), ds, a in zip(items, dscores, qs):
            dj_o[r, width + p * 128 : width + (p + 1) * 128] = mm(jnp.concatenate(ds, axis=1), a).astype(BF)
        for (r, p), ds in zip(items, dscores):
            dq = mm(jnp.concatenate(ds, axis=0), stack_heads(slab(k, r, p)), 0, 0) * 0.125
            dj_o[r, p * 128 : (p + 1) * 128] = dq.astype(BF)


def ln1_parts(acc, cs, w):
    ones = jnp.ones((8, w.shape[1]), BF)
    gain = mm(ones, (acc * w.astype(F32)).astype(BF), 1, 1)[0:1]
    hi = cs.astype(BF)
    lo = (cs - hi.astype(F32)).astype(BF)
    return gain, jnp.sum(mm(hi, w, 1, 1) + mm(lo, w, 1, 1), axis=0, keepdims=True)


def attn_bwd_body(place, joined, dc, seg, n1t, wqkv, gout, gub_own, gub_oth, vec, dj_o, keep_o, send_o, acc, cs, small):
    i = pl.program_id(0)
    d = n1t.shape[0]
    step = d // 16

    @pl.when(i == 0)
    def _():
        acc[...] = jnp.zeros_like(acc)
        cs[...] = jnp.zeros_like(cs)

    q, k, v = (joined.at[:, j * d : (j + 1) * d] for j in range(3))
    attn_bwd_block(q, k, v, dc, seg, dj_o)
    dj = dj_o[...]
    acc[...] += mm(n1t[...], dj)
    cs[...] += fold(dj.astype(F32))

    @pl.when(i == pl.num_programs(0) - 1)
    def _():
        gain, bias = ln1_parts(acc[...], cs[...], wqkv[...])
        csum = jnp.sum(cs[...], axis=0, keepdims=True)
        y, c = place[0], place[1]
        small[...] = jnp.zeros_like(small)

        def put(at, row):
            n = row.shape[1] // 128
            for j in range(n):
                small[pl.ds(at + j, 1)] = row[:, j * 128 : (j + 1) * 128]

        n = d // 128
        for j in range(4):
            put(j * n, vec[j : j + 1, :])
        for j in range(2):
            put(4 * n + (2 * y + j) * n, gub_own[j : j + 1, :])
        put(4 * n + (2 * (1 - y) + 1 - c) * n, gub_oth[0:1, :])
        put(4 * n + (2 * (1 - y) + c) * n, gub_oth[1:2, :])
        put(8 * n, csum)
        put(11 * n, gain)
        put(12 * n, bias)
        for o, core in ((keep_o, c), (send_o, 1 - c)):
            for b in range(8):
                where = pl.ds(pl.multiple_of((8 * core + b) * step, step), step)
                o[b, :, 0 : 3 * d] = acc[where, :].astype(BF)
                o[b, :, 3 * d : 4 * d] = gout[where, :]
                o[b, :, 4 * d :] = jnp.zeros((step, 128), BF)

        @pl.when(c == 0)
        def _():
            for b in range(2):
                keep_o[b, :, 4 * d :] = small[b * step : (b + 1) * step].astype(BF)

        @pl.when(c == 1)
        def _():
            for b in range(2):
                send_o[b, :, 4 * d :] = small[b * step : (b + 1) * step].astype(BF)


def attn_bwd(place, joined, dctx, seg, n1t, wqkv, gout, gub_own, gub_oth, vec, rows):
    d, t = n1t.shape
    outs = [pltpu.VMEM((t, 3 * d), BF)] + [shape((8, d // 16, 4 * d + 128), BF)] * 2
    rest = (wqkv, gout, gub_own, gub_oth, vec)
    return pl.pallas_call(
        attn_bwd_body,
        grid_spec=pltpu.PrefetchScalarGridSpec(
            num_scalar_prefetch=1,
            grid=(t // rows,),
            in_specs=[
                rows_spec(rows, 3 * d),
                rows_spec(rows, d),
                pl.BlockSpec((1, rows // SEQ, SEQ), lambda i, *_: (i, 0, 0)),
                pl.BlockSpec((d, rows), lambda i, *_: (0, i)),
            ]
            + [whole(a) for a in rest],
            out_specs=[rows_spec(rows, 3 * d)] + [whole(o) for o in outs[1:]],
            scratch_shapes=[pltpu.VMEM((d, 3 * d), F32), pltpu.VMEM((8, 3 * d), F32), pltpu.VMEM((64, 128), F32)],
        ),
        out_shape=outs,
        compiler_params=pltpu.CompilerParams(vmem_limit_bytes=LIMIT + 8 * 1024 * 1024),
        cost_estimate=cost(8 * t * d * 3 * d),
        name="attn_bwd",
    )(place, joined, dctx, seg.reshape(t // rows, rows // SEQ, SEQ), n1t, *rest)


def in_grad_body(dj, tok, dattn, wqkv, vecs, out_o):
    dh1 = mm(dj[...], wqkv[...], 1, 1)
    n1, inv1 = layer_norm(tok[...].astype(F32))
    gain = vecs[...].astype(F32)[0:1]
    out_o[...] = (dattn[...].astype(F32) + norm_back(dh1, n1, inv1, gain)).astype(BF)


def in_grad_of(dj, tok, dattn, wqkv, vecs, rows):
    t, d = tok.shape
    return pl.pallas_call(
        in_grad_body,
        grid=(t // rows,),
        in_specs=[rows_spec(rows, 3 * d), rows_spec(rows, d), rows_spec(rows, d), whole(wqkv), whole(vecs)],
        out_specs=rows_spec(rows, d),
        out_shape=shape((t, d), BF),
        compiler_params=pltpu.CompilerParams(vmem_limit_bytes=LIMIT),
        cost_estimate=cost(2 * t * d * 3 * d),
        name="in_grad",
    )(dj, tok, dattn, wqkv, vecs)


def layer_out_body(own, oth, resid, down, w_send, w_keep, vecs, out_o):
    d = resid.shape[1]
    half = w_send.shape[1]
    out = mm(own[...], down[...])
    out += mm(oth[:, 0:half], w_send[d : d + half, :]) + mm(oth[:, half:], w_keep[d : d + half, :])
    out_o[...] = (resid[...] + out + vecs[...].astype(F32)[7:8]).astype(BF)


def layer_out_of(own, oth, resid, down, w_send, w_keep, vecs, rows):
    t, d = resid.shape
    f = own.shape[1]
    return pl.pallas_call(
        layer_out_body,
        grid=(t // rows,),
        in_specs=[rows_spec(rows, f)] * 2 + [rows_spec(rows, d)] + [whole(a) for a in (down, w_send, w_keep, vecs)],
        out_specs=rows_spec(rows, d),
        out_shape=shape((t, d), BF),
        compiler_params=pltpu.CompilerParams(vmem_limit_bytes=LIMIT),
        cost_estimate=cost(2 * t * d * 2 * f),
        name="layer_out",
    )(own, oth, resid, down, w_send, w_keep, vecs)


def on_chip(body, outs, at, *args, name):
    return pl.pallas_call(
        body,
        in_specs=[pl.BlockSpec(memory_space=pltpu.SMEM)] + [pl.BlockSpec(memory_space=pltpu.VMEM)] * len(args),
        out_specs=[pl.BlockSpec(memory_space=pltpu.VMEM)] * len(outs),
        out_shape=outs,
        compiler_params=pltpu.CompilerParams(vmem_limit_bytes=24 * 1024 * 1024),
        cost_estimate=cost(0, 4 * 1024 * 1024),
        name=name,
    )(at, *args)


def plus(a, b):
    return (a.astype(F32) + b.astype(F32)).astype(BF)


def split_body(at, own_a, own_b, oth_a, oth_b, keep_o, send_o):
    def total(o, h):
        a, b = (own_a, own_b) if o == 0 else (oth_a, oth_b)
        return plus(a[h], b[h])

    @pl.when(at[0] == 0)
    def _():
        v = at[1]
        for o in range(2):
            keep_o[o] = total(o, v)
            send_o[o] = total(o, 1 - v)

    @pl.when(at[0] == 1)
    def _():
        for h in range(2):
            keep_o[h] = total(0, h)
            send_o[h] = total(1, h)


def halve(at, which, a, b):
    n = a.shape[0] // 2

    def body(at, a, b, keep_o, send_o):
        v = at[which]
        for j in range(n):
            keep_o[j] = plus(a[v * n + j], b[v * n + j])
            send_o[j] = plus(a[(1 - v) * n + j], b[(1 - v) * n + j])

    return on_chip(body, [shape((n, *a.shape[1:]), BF)] * 2, at, a, b, name="halve")


def finish_ffn_body(at, *refs):
    up_o, down_o = refs[4:]
    for c in range(2):
        chunk = at[0] if c == 0 else 1 - at[0]
        quarter, half = refs[0].shape[1:]
        units = pl.ds(pl.multiple_of(chunk * half, 128), half)
        for j in range(2):
            pair = refs[2 * c + j]
            which = at[3 + 2 * c] if j == 0 else 1 - at[3 + 2 * c]
            for i in range(2):
                part = at[4 + 2 * c] if i == 0 else 1 - at[4 + 2 * c]
                cols = pl.ds(pl.multiple_of(part * quarter, 128), quarter)

                @pl.when(which == 0)
                def _(pair=pair, i=i, cols=cols, units=units):
                    up_o[cols, units] = pair[i].astype(F32)

                @pl.when(which == 1)
                def _(pair=pair, i=i, cols=cols, units=units):
                    down_o[units, cols] = pair[i].astype(F32).T


def finish_rest_body(at, columns, *refs):
    qkv_o, qv_o, gout_o, gain1_o, bias1_o, bo_o, gain2_o, bias2_o, gub_o, b2_o, small = refs[4:]
    d = gout_o.shape[0]
    step, n = d // 16, d // 128
    pieces = []
    for c in range(2):
        core = at[0] if c == 0 else 1 - at[0]
        a0, b0, c0 = (at[7 + j] if c == 0 else at[11 + j] for j in range(3))
        for j in range(2):
            for i in range(4):
                bits = (a0 if j == 0 else 1 - a0, b0 if i < 2 else 1 - b0, c0 if i % 2 == 0 else 1 - c0)
                pieces.append((refs[2 * c + j], i, 8 * core + 4 * bits[0] + 2 * bits[1] + bits[2]))
    for ref, i, at_ in pieces:

        @pl.when(at_ < 2)
        def _(ref=ref, i=i, at_=at_):
            small[pl.ds(pl.multiple_of(at_ * step, step), step)] = ref[i, :, 4 * d :].astype(F32)

    def row(first, count):
        return jnp.concatenate([small[first + j : first + j + 1] for j in range(count)], axis=1)

    csum = row(8 * n, 3 * n)
    for ref, i, at_ in pieces:
        rows = pl.ds(pl.multiple_of(at_ * step, step), step)
        gain, bias = columns[rows, 0:1], columns[rows, 1:2]
        qkv_o[rows, :] = ref[i, :, 0 : 3 * d].astype(F32) * gain + bias * csum
        gout_o[rows, :] = ref[i, :, 3 * d : 4 * d].astype(F32)
    qv_o[0:1] = csum[:, 0:d]
    qv_o[1:2] = csum[:, 2 * d :]
    for o, j in ((bo_o, 0), (gain2_o, 1), (bias2_o, 2), (b2_o, 3)):
        o[...] = row(j * n, n)
    gain1_o[...] = row(11 * n, n)
    bias1_o[...] = row(12 * n, n)
    first = 4 * n + 2 * n * at[10]
    for j in range(2 * n):
        gub_o[:, j * 128 : (j + 1) * 128] = small[pl.ds(first + j, 1)]


def finish_rest(at, columns, *pieces):
    d = columns.shape[0]
    one = shape((1, d), F32)
    outs = [shape((d, 3 * d), F32), shape((2, d), F32), shape((d, d), F32)] + [one] * 5 + [shape((1, 2 * d), F32), one]
    args = (columns, *pieces)
    return pl.pallas_call(
        finish_rest_body,
        in_specs=[pl.BlockSpec(memory_space=pltpu.SMEM)] + [pl.BlockSpec(memory_space=pltpu.VMEM)] * len(args),
        out_specs=[pl.BlockSpec(memory_space=pltpu.VMEM)] * len(outs),
        out_shape=outs,
        scratch_shapes=[pltpu.VMEM((64, 128), F32)],
        compiler_params=pltpu.CompilerParams(vmem_limit_bytes=24 * 1024 * 1024),
        cost_estimate=cost(0, 8 * 1024 * 1024),
        name="finish_rest",
    )(at, *args)


def local(
    n_rows,
    tokens,
    segment_ids,
    ln1_gain,
    ln1_bias,
    qkv_weight,
    qv_bias,
    out_weight,
    out_bias,
    ln2_gain,
    ln2_bias,
    up_weight,
    up_bias,
    down_weight,
    down_bias,
    out_grad,
):
    t, d = tokens.shape
    half = up_weight.shape[1] // 2
    r, y = lax.axis_index("rows"), lax.axis_index("mlp")
    core = r & 1
    up_dims = n_rows.bit_length() - 2

    def flip(dim, row, m):
        if dim == "core":
            return row ^ 1, m
        if dim == "y":
            return row, m ^ 1
        return row ^ (2 << dim), m

    def bit(dim):
        return y if dim == "y" else (r >> (dim + 1)) & 1

    def swap(value, *dims):
        pairs = []
        for row in range(n_rows):
            for m in range(2):
                row2, m2 = flip(dims[0] if row & 1 == 0 else dims[-1], row, m)
                pairs.append((row * 2 + m, row2 * 2 + m2))
        return lax.ppermute(value, BOTH, pairs)

    def by_core(first, second):
        return jnp.where(core == 0, first, second)

    def after(value, *done):
        return lax.optimization_barrier((value, *done))[0]

    u0 = [0, "y"] + list(range(1, up_dims))
    u1 = ["y"] + list(range(1, up_dims)) + [0]
    q0 = [0, "y", 1, 2] + list(range(3, up_dims))
    q1 = ["y", 0, 2, 1] + list(range(3, up_dims))
    big, small = (by_core(bit(u0[0]), bit(u1[1])), by_core(bit(u1[1]), bit(u0[0]))), (
        by_core(bit(u0[2]), bit(u1[2])), by_core(bit(u1[2]), bit(u0[2])),
    )
    at = jnp.stack(
        [core, bit(0), by_core(0, bit(u1[1])), big[0], small[0], big[1], small[1]]
        + [by_core(bit(a), bit(b)) for a, b in zip(q0[:3], q1[:3])]
        + [y]
        + [by_core(bit(b), bit(a)) for a, b in zip(q0[:3], q1[:3])]
    ).astype(jnp.int32)
    place = jnp.stack([y, core]).astype(jnp.int32)
    core_s = core.reshape(1).astype(jnp.int32)
    vmem = lambda v: pltpu.with_memory_space_constraint(v, pltpu.VMEM)
    hbm = lambda v: pltpu.with_memory_space_constraint(v, pltpu.HBM)
    tokens, out_grad = hbm(tokens), hbm(out_grad)

    first = 1 - core
    bias_rows = jnp.broadcast_to(lax.dynamic_slice(up_bias, (first * half,), (half,))[None], (16, half))
    w_mine = jnp.concatenate(
        [
            lax.dynamic_slice(up_weight, (0, first * half), (d, half)),
            lax.dynamic_slice(down_weight, (first * half, 0), (half, d)),
            bias_rows,
        ],
        axis=0,
    )
    w_send = swap(w_mine, "y")
    vecs = jnp.concatenate(
        [
            jnp.stack([ln1_gain, ln1_bias, out_bias, ln2_gain, ln2_bias, qv_bias[0], qv_bias[1], down_bias]),
            up_bias.reshape(2, half),
            jnp.zeros((6, d), BF),
        ]
    )
    columns = jnp.stack([ln1_gain, ln1_bias], axis=1).astype(F32)
    joined, ctx, resid, h2, n1t = attn_fwd(tokens, segment_ids, vecs, qkv_weight, out_weight, rows=512)
    gated_own, dh2_own, own_keep, own_send, gub_own = ffn_own(
        core_s, h2, out_grad, up_weight, vecs[8:10], down_weight, rows=512
    )
    w_send = after(w_send, own_send)
    w_keep = swap(w_send, "core")
    own_recv = swap(own_send, "core")
    gated_oth, dh2, oth_keep, oth_send, gub_oth = ffn_other(h2, out_grad, w_send, w_keep, vmem(dh2_own), rows=512)
    oth_recv = swap(oth_send, "core")
    dattn, dctx, gout, vec = mid(vmem(dh2), hbm(resid), out_grad, hbm(ctx), out_weight, vecs, rows=512)

    block = shape((2, d, half), BF)
    oth_recv = after(oth_recv, vec)
    u_keep, u_send = on_chip(split_body, [block] * 2, at, own_keep, own_recv, oth_keep, oth_recv, name="split")
    u_recv = swap(u_send, u0[0], u1[0])
    dj, q_keep, q_send = attn_bwd(
        place, hbm(joined), after(dctx, u_keep), segment_ids, hbm(n1t), qkv_weight, gout, gub_own, gub_oth, vec, rows=512
    )
    q_recv = swap(q_send, "core")
    cut = lambda v: v.reshape(2, d // 2, half)
    u_keep, u_send = halve(at, 2, u_keep, after(u_recv, q_send))
    u_recv = swap(cut(u_send), u0[1], u1[1])
    in_grad = in_grad_of(dj, tokens, after(dattn, u_keep), qkv_weight, vecs, rows=512)
    q_keep, q_send = halve(at, 7, q_keep, after(q_recv, in_grad))
    q_recv = swap(q_send, q0[0], q1[0])
    layer_out = layer_out_of(
        hbm(gated_own), hbm(gated_oth), hbm(after(resid, q_keep)), down_weight, w_send, w_keep, vecs, rows=512
    )
    u_keep, u_send = halve(at, 4, cut(u_keep), after(u_recv, layer_out))
    u_recv = swap(u_send, u0[2], u1[2])
    q_keep, q_send = halve(at, 8, q_keep, after(q_recv, u_keep))
    q_recv = swap(q_send, q0[1], q1[1])
    u_one = plus(u_keep, after(u_recv, q_keep))
    for k in range(3, len(u0)):
        u_recv = swap(u_one, u0[k], u1[k])
        if k == 3:
            q_keep, q_send = halve(at, 9, q_keep, after(q_recv, u_one))
            q_recv = swap(q_send, q0[2], q1[2])
            u_recv = after(u_recv, q_keep)
        u_one = plus(u_one, u_recv)
    u_ag = swap(u_one, u0[2], u1[2])
    q_one = plus(q_keep, after(q_recv, u_one))
    for k in range(3, len(q0)):
        q_recv = swap(q_one, q0[k], q1[k])
        if k == 3:
            u_pair = jnp.concatenate([u_one, after(u_ag, q_one)], axis=0)
            u_far = swap(u_pair, u0[0], u1[1])
            u_pair_c = swap(u_pair, "core")
            q_recv = after(q_recv, u_pair)
        q_one = plus(q_one, q_recv)
    q_ag = swap(q_one, q0[2], q1[2])
    u_far = after(u_far, q_one)
    u_far_c = swap(u_far, "core")
    q_pair = jnp.concatenate([q_one, after(q_ag, u_far)], axis=0)
    q_ag = swap(q_pair, q0[1], q1[1])
    grad_up, grad_down = on_chip(
        finish_ffn_body, [shape((d, 2 * half), F32), shape((2 * half, d), F32)], at,
        u_pair, u_far, u_pair_c, after(u_far_c, q_pair), name="finish_ffn",
    )
    q_four = jnp.concatenate([q_pair, after(q_ag, grad_up)], axis=0)
    q_far = swap(q_four, q0[0], q1[0])
    grad_qkv, grad_qv, grad_wo, g1, c1, bo, g2, c2, gub, b2 = finish_rest(
        at, columns, q_four, q_far, swap(q_four, "core"), swap(q_far, "core")
    )
    flat = lambda v: v.reshape(-1)
    return (
        layer_out, in_grad, flat(g1), flat(c1), grad_qkv, grad_qv, grad_wo, flat(bo), flat(g2), flat(c2),
        grad_up, flat(gub), grad_down, flat(b2),
    )


def solution(mesh):
    placed = (
        P(BOTH, None), P(BOTH, None), P(), P(), P(), P(), P(), P(), P(), P(),
        P(None, "mlp"), P("mlp"), P("mlp", None), P(), P(BOTH, None),
    )
    return jax.shard_map(
        functools.partial(local, mesh.shape["rows"]),
        mesh=mesh,
        in_specs=placed,
        out_specs=(
            P(BOTH, None), P(BOTH, None), P(), P(), P(), P(), P(), P(), P(), P(),
            P(None, "mlp"), P("mlp"), P("mlp", None), P(),
        ),
        check_vma=False,
    )
```

time: 222 us -> 183 us (0.82)
  other arithmetic: 20.1 us -> 1.49 us
  waiting for transfers between devices: 52.2 us -> 43.2 us
  local copies, waits for them, and re-layouts: 16.4 us -> 7.81 us
  starting transfers between devices: 28.7 us -> 25.3 us
    pallas_call x0 -> x10, Pallas kernels: none -> 29.2 us  [the longest x1 9.67 us: layer_out_of(): pl.pallas_call(layer_out_body, grid=(t // rows,), in_specs=[rows_spec(row...]
    convert_element_type x16 -> x5, other arithmetic: 13.6 us -> 0.21 us  [the longest x4 0.2 us: plus(): return (a.astype(F32) + b.astype(F32)).astype(BF)]
    pallas_call x1, Pallas kernels: 28.9 us -> 16.4 us  [attn_bwd(): pl.pallas_call(attn_bwd_body, grid_spec=pltpu.PrefetchScalarGridSpec(num_...]
    ppermute x17 -> x22, waiting for transfers between devices: 52.2 us -> 43.2 us  [swap(): return lax.ppermute(value, BOTH, pairs)]
    pallas_call x1, Pallas kernels: 26.8 us -> 18.7 us  [ffn_other(): pl.pallas_call(ffn_other_body, grid=(t // rows,), in_specs=[rows_spec(row...]
    squeeze x4 -> x0, local copies, waits for them, and re-layouts: 5.01 us -> none  [the longest x1 3.6 us: local(): full[1, d:2 * d]]
    reshape x8 -> x1, local copies, waits for them, and re-layouts: 4.68 us -> 0.01 us  [local(): up_bias.reshape(2, half)]
    pallas_call x1, Pallas kernels: 22 us -> 17.8 us  [ffn_own(): pl.pallas_call(ffn_own_body, grid_spec=pltpu.PrefetchScalarGridSpec(num_s...]
  transfers between devices with their start and end apart: 17 -> 22, of which waited for: 9 -> 8; matrix products, arithmetic and copies ran while one was open for 13% -> 0% of each run, Pallas kernels for 46% -> 44%
where the time goes in v2:
time: 183 us; the launch traced here: 182 us
  Pallas kernels  103 us (56%)
  waiting for transfers between devices  43.2 us (24%)
  starting transfers between devices  25.3 us (14%)
  local copies, waits for them, and re-layouts  7.81 us (4%)
    ppermute x22, waiting for transfers between devices, swap(): return lax.ppermute(value, BOTH, pairs)  43.2 us
    ppermute x22, starting transfers between devices, swap(): return lax.ppermute(value, BOTH, pairs)  25.3 us
    pallas_call x1, Pallas kernels, ffn_other(): pl.pallas_call(ffn_other_body, grid=(t // rows,), in_specs=[rows_spec(row...  18.7 us
    pallas_call x1, Pallas kernels, ffn_own(): pl.pallas_call(ffn_own_body, grid_spec=pltpu.PrefetchScalarGridSpec(num_s...  17.8 us
    pallas_call x1, Pallas kernels, attn_bwd(): pl.pallas_call(attn_bwd_body, grid_spec=pltpu.PrefetchScalarGridSpec(num_...  16.4 us
    pallas_call x1, Pallas kernels, attn_fwd(): pl.pallas_call(attn_fwd_body, grid=(t // rows,), in_specs=[rows_spec(rows...  14 us
    pallas_call x1, Pallas kernels, layer_out_of(): pl.pallas_call(layer_out_body, grid=(t // rows,), in_specs=[rows_spec(row...  9.67 us
    pallas_call x7, Pallas kernels, on_chip(): pl.pallas_call(body, in_specs=[pl.BlockSpec(memory_space=pltpu.SMEM)] + [...  8.91 us
  transfers between devices with their start and end apart: 22, of which 8 were waited for; matrix products, arithmetic and copies ran while one was open for 0% of the time, Pallas kernels for 44%

profile of v2, /device:TPU:0, one launch (start us, length us, event | category | flops | bytes accessed | tf_op | source)
XLA Modules:
  0.0 182.3 jit_solution(16645558870563124380)
XLA Ops:
  1.5 1.4 constant_dynamic-slice_fusion
  2.9 1.0 pad_maximum_fusion
  4.0 3.0 %collective-permute-start = (bf16[1040,512]{1,0:T(8,128)(2,1)}, bf16[1040,512]{1,0:T(8,128)(2,1)}, u32[]{:S(2)}, u32[]{:S(2)}) collective-permute-start(bf16[1040,512]{1,0:T(8,128)(2,1)} %pad_maximum_fusion), channel_id=1, source_target_pairs={{0,1},{1,0},{2,3},{3,2},{4,5},{5,4},{6,7},{7,6},{8,9},{9,8},{10,11... | collective-permute-start | bytes 3194888 | tf_op jit(solution)/shard_map/ppermute | solution.py:630
  7.2 14.0 %attn_fwd.1 = (bf16[2048,1536]{1,0:T(8,128)(2,1)}, bf16[2048,512]{1,0:T(8,128)(2,1)}, f32[2048,512]{1,0:T(8,128)}, bf16[2048,512]{1,0:T(8,128)(2,1)S(1)}, bf16[512,2048]{1,0:T(8,128)(2,1)}) custom-call(bf16[2048,512]{1,0:T(8,128)(2,1)} %tok.3, s32[4,4,128]{2,1,0:T(4,128)S(1)} %bitcast.21, bf16[16,512]{1,0:T(8,128)(2,1)S(1)} %concatenate.16.vecs, ...), custom_call_target="tpu_custom_call" | custom-call | flops 805306368 | tf_op jit(solution)/shard_map/attn_fwd/pallas_call | solution.py:126
  21.2 17.8 %ffn_own.1 = (bf16[2048,1024]{1,0:T(8,128)(2,1)}, f32[2048,512]{1,0:T(8,128)S(1)}, bf16[2,512,512]{2,1,0:T(8,128)(2,1)S(1)}, bf16[2,512,512]{2,1,0:T(8,128)(2,1)}, f32[2,512]{1,0:T(2,128)S(1)}) custom-call(s32[1]{0:T(128)} %bitcast.core, bf16[2048,512]{1,0:T(8,128)(2,1)S(1)} %get-tuple-element.79.h2, bf16[2048,512]{1,0:T(8,128)(2,1)} %g.5, ...), custom_call_target="tpu_custom_call" | custom-call | flops 1342177280 | tf_op jit(solution)/shard_map/ffn_own/pallas_call | solution.py:199
  39.2 2.9 %collective-permute-done.1.w_keep = bf16[1040,512]{1,0:T(8,128)(2,1)S(1)} collective-permute-done((bf16[1040,512]{1,0:T(8,128)(2,1)}, bf16[1040,512]{1,0:T(8,128)(2,1)S(1)}, u32[]{:S(2)}, u32[]{:S(2)}) %collective-permute-start.1) | collective-permute-done | bytes 1064992 | tf_op jit(solution)/shard_map/ppermute | solution.py:630
  42.0 18.7 %ffn_other.1 = (bf16[2048,1024]{1,0:T(8,128)(2,1)}, f32[2048,512]{1,0:T(8,128)S(1)}, bf16[2,512,512]{2,1,0:T(8,128)(2,1)S(1)}, bf16[2,512,512]{2,1,0:T(8,128)(2,1)}, f32[2,512]{1,0:T(2,128)S(1)}) custom-call(bf16[2048,512]{1,0:T(8,128)(2,1)S(1)} %get-tuple-element.79.h2, bf16[2048,512]{1,0:T(8,128)(2,1)} %g.5, ...), custom_call_target="tpu_custom_call" | custom-call | flops 1342177280 | tf_op jit(solution)/shard_map/ffn_other/pallas_call | solution.py:246
  60.8 2.0 %copy-done.4 = f32[2048,512]{1,0:T(8,128)} copy-done((f32[2048,512]{1,0:T(8,128)}, f32[2048,512]{1,0:T(8,128)S(1)}, u32[]{:S(2)}) %copy-start.4) | copy-done | bytes 4194328
  64.4 2.2 %copy-done.5 = f32[2048,512]{1,0:T(8,128)S(1)} copy-done((f32[2048,512]{1,0:T(8,128)S(1)}, f32[2048,512]{1,0:T(8,128)}, u32[]{:S(2)}) %copy-start.5) | copy-done | bytes 4194328
  66.6 7.3 %mid.1 = (bf16[2048,512]{1,0:T(8,128)(2,1)S(1)}, bf16[2048,512]{1,0:T(8,128)(2,1)S(1)}, bf16[512,512]{1,0:T(8,128)(2,1)S(1)}, f32[4,512]{1,0:T(4,128)S(1)}) custom-call(f32[2048,512]{1,0:T(8,128)S(1)} %copy-done.5, f32[2048,512]{1,0:T(8,128)} %get-tuple-element.111.resid, bf16[2048,512]{1,0:T(8,128)(2,1)} %g.5, bf16[2048,512]{1,0:T(8,128)(2,1)} %get-tuple-element.88.ctx, ...), custom_call_target="tpu_custom_call" | custom-call | flops 402653184 | tf_op jit(solution)/shard_map/mid/pallas_call | solution.py:287
  74.0 2.0 %split.1 = (bf16[2,512,512]{2,1,0:T(8,128)(2,1)S(1)}, bf16[2,512,512]{2,1,0:T(8,128)(2,1)S(1)}) custom-call(s32[14]{0:T(128)S(1)} %stack.82.at, bf16[2,512,512]{2,1,0:T(8,128)(2,1)S(1)} %copy-done.9, bf16[2,512,512]{2,1,0:T(8,128)(2,1)} %collective-permute-done.2.own_b, bf16[2,512,512]{2,1,0:T(8,128)(2,1)S(1)} %copy-done.11, ...), custom_call_target="tpu_custom_call" | custom-call | bytes 524288 | tf_op jit(solution)/shard_map/split/pallas_call | solution.py:467
  76.0 1.6 collective-permute-start.5
  77.6 16.4 %attn_bwd.1 = (bf16[2048,1536]{1,0:T(8,128)(2,1)S(1)}, bf16[8,32,2176]{2,1,0:T(8,128)(2,1)S(1)}, bf16[8,32,2176]{2,1,0:T(8,128)(2,1)S(1)}) custom-call(s32[2]{0:T(128)S(1)} %pad_add_fusion.place, bf16[2048,1536]{1,0:T(8,128)(2,1)} %get-tuple-element.86.joined, bf16[2048,512]{1,0:T(8,128)(2,1)S(1)} %get-tuple-element.96.dc, s32[4,4,128]{2,1,0:T(4,128)S(1)} %bitcast.22, ...), custom_call_target="tpu_custom_call" | custom-call | flops 1610612736 | tf_op jit(solution)/shard_map/attn_bwd/pallas_call | solution.py:400
  95.5 7.3 %in_grad.1 = bf16[2048,512]{1,0:T(8,128)(2,1)} custom-call(bf16[2048,1536]{1,0:T(8,128)(2,1)S(1)} %get-tuple-element.103.dj, bf16[2048,512]{1,0:T(8,128)(2,1)} %tok.3, bf16[2048,512]{1,0:T(8,128)(2,1)S(1)} %get-tuple-element.108.dattn, bf16[512,1536]{1,0:T(8,128)(2,1)S(1)} %copy-done, bf16[16,512]{1,0:T(8,128)(2,1)S(1)} %concatenate.16.vecs), custom_call_target="tpu_custom_call" | custom-call | flops 402653184 | tf_op jit(solution)/shard_map/in_grad/pallas_call | solution.py:431
  103.7 1.5 collective-permute-start.6
  105.2 9.7 %layer_out.1 = bf16[2048,512]{1,0:T(8,128)(2,1)} custom-call(bf16[2048,1024]{1,0:T(8,128)(2,1)} %get-tuple-element.80.own, bf16[2048,1024]{1,0:T(8,128)(2,1)} %get-tuple-element.84.oth, f32[2048,512]{1,0:T(8,128)} %get-tuple-element.111.resid, bf16[1024,512]{1,0:T(8,128)(2,1)S(1)} %copy-done.1, bf16[1040,512]{1,0:T(8,128)(2,1)} %collective-permute-done.w_send, ...), custom_call_target="tpu_custom_call" | custom-call | flops 536870912 | tf_op jit(solution)/shard_map/layer_out/pallas_call | solution.py:454
  115.5 1.6 collective-permute-start.9
  118.6 4.9 %collective-permute-done.9 = bf16[1,256,512]{2,1,0:T(8,128)(2,1)S(1)} collective-permute-done((bf16[1,256,512]{2,1,0:T(8,128)(2,1)S(1)}, bf16[1,256,512]{2,1,0:T(8,128)(2,1)S(1)}, u32[]{:S(2)}, u32[]{:S(2)}) %collective-permute-start.9) | collective-permute-done | bytes 262176 | tf_op jit(solution)/shard_map/ppermute | solution.py:630
  123.6 2.0 %collective-permute-start.11 = (bf16[1,256,512]{2,1,0:T(8,128)(2,1)S(1)}, bf16[1,256,512]{2,1,0:T(8,128)(2,1)S(1)}, u32[]{:S(2)}, u32[]{:S(2)}) collective-permute-start(bf16[1,256,512]{2,1,0:T(8,128)(2,1)S(1)} %add_convert_fusion.1), channel_id=1, source_target_pairs={{0,16},{1,17},{2,6},{3,7},{4,20},{5,21},{6,2},{7,3},{8,24},{9,25},... | collective-permute-start | bytes 786440 | tf_op jit(solution)/shard_map/ppermute | solution.py:630
  126.2 2.5 %collective-permute-start.10 = (bf16[1,32,2176]{2,1,0:T(8,128)(2,1)S(1)}, bf16[1,32,2176]{2,1,0:T(8,128)(2,1)S(1)}, u32[]{:S(2)}, u32[]{:S(2)}) collective-permute-start(bf16[1,32,2176]{2,1,0:T(8,128)(2,1)S(1)} %get-tuple-element.123), channel_id=1, source_target_pairs={{0,8},{1,9},{2,18},{3,19},{4,12},{5,13},{6,22},{7,23},{8,0},{9,1},... | collective-permute-start | bytes 417800 | tf_op jit(solution)/shard_map/ppermute | solution.py:630
  128.8 11.4 %collective-permute-done.11 = bf16[1,256,512]{2,1,0:T(8,128)(2,1)S(1)} collective-permute-done((bf16[1,256,512]{2,1,0:T(8,128)(2,1)S(1)}, bf16[1,256,512]{2,1,0:T(8,128)(2,1)S(1)}, u32[]{:S(2)}, u32[]{:S(2)}) %collective-permute-start.11) | collective-permute-done | bytes 262176 | tf_op jit(solution)/shard_map/ppermute | solution.py:630
  141.1 3.4 %collective-permute-start.12 = (bf16[1,32,2176]{2,1,0:T(8,128)(2,1)S(1)}, bf16[1,32,2176]{2,1,0:T(8,128)(2,1)S(1)}, u32[]{:S(2)}, u32[]{:S(2)}) collective-permute-start(bf16[1,32,2176]{2,1,0:T(8,128)(2,1)S(1)} %add_convert_fusion.3), channel_id=1, source_target_pairs={{0,16},{1,17},{2,10},{3,11},{4,20},{5,21},{6,14},{7,15},{8,24},{9,... | collective-permute-start | bytes 417800 | tf_op jit(solution)/shard_map/ppermute | solution.py:630
  144.6 6.9 %collective-permute-done.13 = bf16[1,256,512]{2,1,0:T(8,128)(2,1)S(1)} collective-permute-done((bf16[1,256,512]{2,1,0:T(8,128)(2,1)S(1)}, bf16[1,256,512]{2,1,0:T(8,128)(2,1)S(1)}, u32[]{:S(2)}, u32[]{:S(2)}) %collective-permute-start.13) | collective-permute-done | bytes 262176 | tf_op jit(solution)/shard_map/ppermute | solution.py:630
  152.1 2.0 %collective-permute-start.14 = (bf16[1,32,2176]{2,1,0:T(8,128)(2,1)S(1)}, bf16[1,32,2176]{2,1,0:T(8,128)(2,1)S(1)}, u32[]{:S(2)}, u32[]{:S(2)}) collective-permute-start(bf16[1,32,2176]{2,1,0:T(8,128)(2,1)S(1)} %add_convert_fusion.2), channel_id=1, source_target_pairs={{0,8},{1,9},{2,18},{3,19},{4,12},{5,13},{6,22},{7,23},{8,0},{9,1},... | collective-permute-start | bytes 417800 | tf_op jit(solution)/shard_map/ppermute | solution.py:630
  154.2 6.6 %collective-permute-done.15.refs_1_ = bf16[2,256,512]{2,1,0:T(8,128)(2,1)S(1)} collective-permute-done((bf16[2,256,512]{2,1,0:T(8,128)(2,1)S(1)}, bf16[2,256,512]{2,1,0:T(8,128)(2,1)S(1)}, u32[]{:S(2)}, u32[]{:S(2)}) %collective-permute-start.15) | collective-permute-done | bytes 524320 | tf_op jit(solution)/shard_map/ppermute | solution.py:630
  160.8 2.1 %collective-permute-start.16 = (bf16[2,32,2176]{2,1,0:T(8,128)(2,1)S(1)}, bf16[2,32,2176]{2,1,0:T(8,128)(2,1)S(1)}, u32[]{:S(2)}, u32[]{:S(2)}) collective-permute-start(bf16[2,32,2176]{2,1,0:T(8,128)(2,1)S(1)} %pad_maximum_fusion.3), channel_id=1, source_target_pairs={{0,1},{1,0},{2,6},{3,7},{4,5},{5,4},{6,2},{7,3},{8,9},{9,8},{10,14... | collective-permute-start | bytes 835592 | tf_op jit(solution)/shard_map/ppermute | solution.py:630
  162.9 3.3 %finish_ffn.1 = (f32[512,1024]{1,0:T(8,128)}, f32[1024,512]{1,0:T(8,128)}) custom-call(s32[14]{0:T(128)S(1)} %stack.82.at, bf16[2,256,512]{2,1,0:T(8,128)(2,1)S(1)} %pad_maximum_fusion.2.refs_0_, bf16[2,256,512]{2,1,0:T(8,128)(2,1)S(1)} %collective-permute-done.15.refs_1_, bf16[2,256,512]{2,1,0:T(8,128)(2,1)S(1)} %collective-permute-done.17.refs_2_, ...), custom_call_target="tpu_custom_call" | custom-call | bytes 524288 | tf_op jit(solution)/shard_map/finish_ffn/pallas_call | solution.py:467
  166.3 1.2 collective-permute-done.16
  167.5 2.1 %collective-permute-start.19 = (bf16[4,32,2176]{2,1,0:T(8,128)(2,1)S(1)}, bf16[4,32,2176]{2,1,0:T(8,128)(2,1)S(1)}, u32[]{:S(2)}, u32[]{:S(2)}) collective-permute-start(bf16[4,32,2176]{2,1,0:T(8,128)(2,1)S(1)} %pad_maximum_fusion.1.refs_0_), channel_id=1, source_target_pairs={{0,4},{1,5},{2,3},{3,2},{4,0},{5,1},{6,7},{7,6},{8,12},{9,13},{10,... | collective-permute-start | bytes 1671176 | tf_op jit(solution)/shard_map/ppermute | solution.py:630
  169.6 7.5 %collective-permute-done.19.refs_1_ = bf16[4,32,2176]{2,1,0:T(8,128)(2,1)S(1)} collective-permute-done((bf16[4,32,2176]{2,1,0:T(8,128)(2,1)S(1)}, bf16[4,32,2176]{2,1,0:T(8,128)(2,1)S(1)}, u32[]{:S(2)}, u32[]{:S(2)}) %collective-permute-start.19) | collective-permute-done | bytes 557088 | tf_op jit(solution)/shard_map/ppermute | solution.py:630
  177.3 1.8 collective-permute-done.21.refs_3_
  179.1 3.2 %finish_rest.1 = (f32[512,1536]{1,0:T(8,128)}, f32[2,512]{1,0:T(2,128)}, f32[512,512]{1,0:T(8,128)}, f32[1,512]{1,0:T(1,128)}, f32[1,512]{1,0:T(1,128)}, /*index...) custom-call(s32[14]{0:T(128)S(1)} %stack.82.at, ...), custom_call_target="tpu_custom_call" | custom-call | bytes 1048576 | tf_op jit(solution)/shard_map/finish_rest/pallas_call | solution.py:578
  (95 shorter events, 9.6 us)
Async XLA Ops:
  1.5 5.6 %copy-start.16 = (bf16[2,512]{1,0:T(2,128)(2,1)S(1)}, bf16[2,512]{1,0:T(2,128)(2,1)}, u32[]{:S(2)}) copy-start(bf16[2,512]{1,0:T(2,128)(2,1)} %param.20) | copy-start | bytes 6148
  1.5 5.7 %copy-start = (bf16[512,1536]{1,0:T(8,128)(2,1)S(1)}, bf16[512,1536]{1,0:T(8,128)(2,1)}, u32[]{:S(2)}) copy-start(bf16[512,1536]{1,0:T(8,128)(2,1)} %wqkv.5) | copy-start | bytes 4718596
  1.5 5.7 %copy-start.7 = (bf16[512,512]{1,0:T(8,128)(2,1)S(1)}, bf16[512,512]{1,0:T(8,128)(2,1)}, u32[]{:S(2)}) copy-start(bf16[512,512]{1,0:T(8,128)(2,1)} %wo.3) | copy-start | bytes 1572868
  1.5 5.7 %copy-start.12 = (s32[16,128]{1,0:T(8,128)S(1)}, s32[16,128]{1,0:T(8,128)}, u32[]{:S(2)}) copy-start(s32[16,128]{1,0:T(8,128)} %param.16) | copy-start | bytes 24580
  4.0 35.1 %collective-permute-start = (bf16[1040,512]{1,0:T(8,128)(2,1)}, bf16[1040,512]{1,0:T(8,128)(2,1)}, u32[]{:S(2)}, u32[]{:S(2)}) collective-permute-start(bf16[1040,512]{1,0:T(8,128)(2,1)} %pad_maximum_fusion), channel_id=1, source_target_pairs={{0,1},{1,0},{2,3},{3,2},{4,5},{5,4},{6,7},{7,6},{8,9},{9,8},{10,11... | collective-permute-start | bytes 3194888 | tf_op jit(solution)/shard_map/ppermute | solution.py:630
  7.2 14.0 %copy-start.1 = (bf16[1024,512]{1,0:T(8,128)(2,1)S(1)}, bf16[1024,512]{1,0:T(8,128)(2,1)}, u32[]{:S(2)}) copy-start(bf16[1024,512]{1,0:T(8,128)(2,1)} %down.3) | copy-start | bytes 3145732
  7.2 14.0 %copy-start.6 = (bf16[512,1024]{1,0:T(8,128)(2,1)S(1)}, bf16[512,1024]{1,0:T(8,128)(2,1)}, u32[]{:S(2)}) copy-start(bf16[512,1024]{1,0:T(8,128)(2,1)} %up.1) | copy-start | bytes 3145732
  39.1 21.7 %copy-start.8 = (bf16[2,512,512]{2,1,0:T(8,128)(2,1)}, bf16[2,512,512]{2,1,0:T(8,128)(2,1)S(1)}, u32[]{:S(2)}) copy-start(bf16[2,512,512]{2,1,0:T(8,128)(2,1)S(1)} %get-tuple-element.90.own_a) | copy-start | bytes 3145732
  39.1 3.0 %collective-permute-start.1 = (bf16[1040,512]{1,0:T(8,128)(2,1)}, bf16[1040,512]{1,0:T(8,128)(2,1)S(1)}, u32[]{:S(2)}, u32[]{:S(2)}) collective-permute-start(bf16[1040,512]{1,0:T(8,128)(2,1)} %collective-permute-done.w_send), channel_id=1, source_target_pairs={{0,2},{1,3},{2,0},{3,1},{4,6},{5,7},{6,4},{7,5},{8,10},{9,11},{10,... | collective-permute-start | bytes 3194888 | tf_op jit(solution)/shard_map/ppermute | solution.py:630
  42.0 18.7 %copy-start.2 = (bf16[1040,512]{1,0:T(8,128)(2,1)}, bf16[1040,512]{1,0:T(8,128)(2,1)S(1)}, u32[]{:S(2)}) copy-start(bf16[1040,512]{1,0:T(8,128)(2,1)S(1)} %collective-permute-done.1.w_keep) | copy-start | bytes 3194884
  63.8 10.1 %collective-permute-start.3 = (bf16[2,512,512]{2,1,0:T(8,128)(2,1)}, bf16[2,512,512]{2,1,0:T(8,128)(2,1)}, u32[]{:S(2)}, u32[]{:S(2)}) collective-permute-start(bf16[2,512,512]{2,1,0:T(8,128)(2,1)} %get-tuple-element.92), channel_id=1, source_target_pairs={{0,2},{1,3},{2,0},{3,1},{4,6},{5,7},{6,4},{7,5},{8,10},{9,11},{10,... | collective-permute-start | bytes 3145736 | tf_op jit(solution)/shard_map/ppermute | solution.py:630
  63.9 10.0 %collective-permute-start.2 = (bf16[2,512,512]{2,1,0:T(8,128)(2,1)}, bf16[2,512,512]{2,1,0:T(8,128)(2,1)}, u32[]{:S(2)}, u32[]{:S(2)}) collective-permute-start(bf16[2,512,512]{2,1,0:T(8,128)(2,1)} %get-tuple-element.81), channel_id=1, source_target_pairs={{0,2},{1,3},{2,0},{3,1},{4,6},{5,7},{6,4},{7,5},{8,10},{9,11},{10,... | collective-permute-start | bytes 3145736 | tf_op jit(solution)/shard_map/ppermute | solution.py:630
  66.6 7.4 %copy-start.9 = (bf16[2,512,512]{2,1,0:T(8,128)(2,1)S(1)}, bf16[2,512,512]{2,1,0:T(8,128)(2,1)}, u32[]{:S(2)}) copy-start(bf16[2,512,512]{2,1,0:T(8,128)(2,1)} %copy-done.8) | copy-start | bytes 3145732
  66.6 7.4 %copy-start.11 = (bf16[2,512,512]{2,1,0:T(8,128)(2,1)S(1)}, bf16[2,512,512]{2,1,0:T(8,128)(2,1)}, u32[]{:S(2)}) copy-start(bf16[2,512,512]{2,1,0:T(8,128)(2,1)} %copy-done.10) | copy-start | bytes 3145732
  76.0 18.2 %collective-permute-start.5 = (bf16[2,512,512]{2,1,0:T(8,128)(2,1)S(1)}, bf16[2,512,512]{2,1,0:T(8,128)(2,1)S(1)}, u32[]{:S(2)}, u32[]{:S(2)}) collective-permute-start(bf16[2,512,512]{2,1,0:T(8,128)(2,1)S(1)} %get-tuple-element.105), channel_id=1, source_target_pairs={{0,4},{1,5},{2,3},{3,2},{4,0},{5,1},{6,7},{7,6},{8,12},{9,13},{10,... | collective-permute-start | bytes 3145736 | tf_op jit(solution)/shard_map/ppermute | solution.py:630
  94.1 8.8 %collective-permute-start.4 = (bf16[8,32,2176]{2,1,0:T(8,128)(2,1)S(1)}, bf16[8,32,2176]{2,1,0:T(8,128)(2,1)S(1)}, u32[]{:S(2)}, u32[]{:S(2)}) collective-permute-start(bf16[8,32,2176]{2,1,0:T(8,128)(2,1)S(1)} %get-tuple-element.102), channel_id=1, source_target_pairs={{0,2},{1,3},{2,0},{3,1},{4,6},{5,7},{6,4},{7,5},{8,10},{9,11},{10,... | collective-permute-start | bytes 3342344 | tf_op jit(solution)/shard_map/ppermute | solution.py:630
  95.0 19.9 %collective-permute-start.7 = (bf16[2,256,512]{2,1,0:T(8,128)(2,1)S(1)}, bf16[2,256,512]{2,1,0:T(8,128)(2,1)S(1)}, u32[]{:S(2)}, u32[]{:S(2)}) collective-permute-start(bf16[2,256,512]{2,1,0:T(8,128)(2,1)S(1)} %bitcast.23), channel_id=1, source_target_pairs={{0,1},{1,0},{2,10},{3,11},{4,5},{5,4},{6,14},{7,15},{8,9},{9,8},{1... | collective-permute-start | bytes 1572872 | tf_op jit(solution)/shard_map/ppermute | solution.py:630
  103.7 13.4 %collective-permute-start.6 = (bf16[4,32,2176]{2,1,0:T(8,128)(2,1)S(1)}, bf16[4,32,2176]{2,1,0:T(8,128)(2,1)S(1)}, u32[]{:S(2)}, u32[]{:S(2)}) collective-permute-start(bf16[4,32,2176]{2,1,0:T(8,128)(2,1)S(1)} %get-tuple-element.112), channel_id=1, source_target_pairs={{0,4},{1,5},{2,3},{3,2},{4,0},{5,1},{6,7},{7,6},{8,12},{9,13},{10,... | collective-permute-start | bytes 1671176 | tf_op jit(solution)/shard_map/ppermute | solution.py:630
  115.5 8.0 %collective-permute-start.9 = (bf16[1,256,512]{2,1,0:T(8,128)(2,1)S(1)}, bf16[1,256,512]{2,1,0:T(8,128)(2,1)S(1)}, u32[]{:S(2)}, u32[]{:S(2)}) collective-permute-start(bf16[1,256,512]{2,1,0:T(8,128)(2,1)S(1)} %get-tuple-element.119), channel_id=1, source_target_pairs={{0,8},{1,9},{2,18},{3,19},{4,12},{5,13},{6,22},{7,23},{8,0},{9,1},... | collective-permute-start | bytes 786440 | tf_op jit(solution)/shard_map/ppermute | solution.py:630
  117.8 7.8 %collective-permute-start.8 = (bf16[2,32,2176]{2,1,0:T(8,128)(2,1)S(1)}, bf16[2,32,2176]{2,1,0:T(8,128)(2,1)S(1)}, u32[]{:S(2)}, u32[]{:S(2)}) collective-permute-start(bf16[2,32,2176]{2,1,0:T(8,128)(2,1)S(1)} %get-tuple-element.118), channel_id=1, source_target_pairs={{0,1},{1,0},{2,6},{3,7},{4,5},{5,4},{6,2},{7,3},{8,9},{9,8},{10,14... | collective-permute-start | bytes 835592 | tf_op jit(solution)/shard_map/ppermute | solution.py:630
  123.6 16.6 %collective-permute-start.11 = (bf16[1,256,512]{2,1,0:T(8,128)(2,1)S(1)}, bf16[1,256,512]{2,1,0:T(8,128)(2,1)S(1)}, u32[]{:S(2)}, u32[]{:S(2)}) collective-permute-start(bf16[1,256,512]{2,1,0:T(8,128)(2,1)S(1)} %add_convert_fusion.1), channel_id=1, source_target_pairs={{0,16},{1,17},{2,6},{3,7},{4,20},{5,21},{6,2},{7,3},{8,24},{9,25},... | collective-permute-start | bytes 786440 | tf_op jit(solution)/shard_map/ppermute | solution.py:630
  126.2 14.9 %collective-permute-start.10 = (bf16[1,32,2176]{2,1,0:T(8,128)(2,1)S(1)}, bf16[1,32,2176]{2,1,0:T(8,128)(2,1)S(1)}, u32[]{:S(2)}, u32[]{:S(2)}) collective-permute-start(bf16[1,32,2176]{2,1,0:T(8,128)(2,1)S(1)} %get-tuple-element.123), channel_id=1, source_target_pairs={{0,8},{1,9},{2,18},{3,19},{4,12},{5,13},{6,22},{7,23},{8,0},{9,1},... | collective-permute-start | bytes 417800 | tf_op jit(solution)/shard_map/ppermute | solution.py:630
  140.3 11.2 %collective-permute-start.13 = (bf16[1,256,512]{2,1,0:T(8,128)(2,1)S(1)}, bf16[1,256,512]{2,1,0:T(8,128)(2,1)S(1)}, u32[]{:S(2)}, u32[]{:S(2)}) collective-permute-start(bf16[1,256,512]{2,1,0:T(8,128)(2,1)S(1)} %add_convert_fusion), channel_id=1, source_target_pairs={{0,8},{1,9},{2,18},{3,19},{4,12},{5,13},{6,22},{7,23},{8,0},{9,1},... | collective-permute-start | bytes 786440 | tf_op jit(solution)/shard_map/ppermute | solution.py:630
  141.1 10.9 %collective-permute-start.12 = (bf16[1,32,2176]{2,1,0:T(8,128)(2,1)S(1)}, bf16[1,32,2176]{2,1,0:T(8,128)(2,1)S(1)}, u32[]{:S(2)}, u32[]{:S(2)}) collective-permute-start(bf16[1,32,2176]{2,1,0:T(8,128)(2,1)S(1)} %add_convert_fusion.3), channel_id=1, source_target_pairs={{0,16},{1,17},{2,10},{3,11},{4,20},{5,21},{6,14},{7,15},{8,24},{9,... | collective-permute-start | bytes 417800 | tf_op jit(solution)/shard_map/ppermute | solution.py:630
  151.5 9.2 %collective-permute-start.15 = (bf16[2,256,512]{2,1,0:T(8,128)(2,1)S(1)}, bf16[2,256,512]{2,1,0:T(8,128)(2,1)S(1)}, u32[]{:S(2)}, u32[]{:S(2)}) collective-permute-start(bf16[2,256,512]{2,1,0:T(8,128)(2,1)S(1)} %pad_maximum_fusion.2.refs_0_), channel_id=1, source_target_pairs={{0,4},{1,5},{2,10},{3,11},{4,0},{5,1},{6,14},{7,15},{8,12},{9,13},... | collective-permute-start | bytes 1572872 | tf_op jit(solution)/shard_map/ppermute | solution.py:630
  152.1 8.6 %collective-permute-start.14 = (bf16[1,32,2176]{2,1,0:T(8,128)(2,1)S(1)}, bf16[1,32,2176]{2,1,0:T(8,128)(2,1)S(1)}, u32[]{:S(2)}, u32[]{:S(2)}) collective-permute-start(bf16[1,32,2176]{2,1,0:T(8,128)(2,1)S(1)} %add_convert_fusion.2), channel_id=1, source_target_pairs={{0,8},{1,9},{2,18},{3,19},{4,12},{5,13},{6,22},{7,23},{8,0},{9,1},... | collective-permute-start | bytes 417800 | tf_op jit(solution)/shard_map/ppermute | solution.py:630
  154.1 8.8 %collective-permute-start.17 = (bf16[2,256,512]{2,1,0:T(8,128)(2,1)S(1)}, bf16[2,256,512]{2,1,0:T(8,128)(2,1)S(1)}, u32[]{:S(2)}, u32[]{:S(2)}) collective-permute-start(bf16[2,256,512]{2,1,0:T(8,128)(2,1)S(1)} %pad_maximum_fusion.2.refs_0_), channel_id=1, source_target_pairs={{0,2},{1,3},{2,0},{3,1},{4,6},{5,7},{6,4},{7,5},{8,10},{9,11},{10,... | collective-permute-start | bytes 1572872 | tf_op jit(solution)/shard_map/ppermute | solution.py:630
  160.7 2.2 %collective-permute-start.18 = (bf16[2,256,512]{2,1,0:T(8,128)(2,1)S(1)}, bf16[2,256,512]{2,1,0:T(8,128)(2,1)S(1)}, u32[]{:S(2)}, u32[]{:S(2)}) collective-permute-start(bf16[2,256,512]{2,1,0:T(8,128)(2,1)S(1)} %collective-permute-done.15.refs_1_), channel_id=1, source_target_pairs={{0,2},{1,3},{2,0},{3,1},{4,6},{5,7},{6,4},{7,5},{8,10},{9,11},{10,... | collective-permute-start | bytes 1572872 | tf_op jit(solution)/shard_map/ppermute | solution.py:630
  160.8 6.7 %collective-permute-start.16 = (bf16[2,32,2176]{2,1,0:T(8,128)(2,1)S(1)}, bf16[2,32,2176]{2,1,0:T(8,128)(2,1)S(1)}, u32[]{:S(2)}, u32[]{:S(2)}) collective-permute-start(bf16[2,32,2176]{2,1,0:T(8,128)(2,1)S(1)} %pad_maximum_fusion.3), channel_id=1, source_target_pairs={{0,1},{1,0},{2,6},{3,7},{4,5},{5,4},{6,2},{7,3},{8,9},{9,8},{10,14... | collective-permute-start | bytes 835592 | tf_op jit(solution)/shard_map/ppermute | solution.py:630
  167.5 9.6 %collective-permute-start.19 = (bf16[4,32,2176]{2,1,0:T(8,128)(2,1)S(1)}, bf16[4,32,2176]{2,1,0:T(8,128)(2,1)S(1)}, u32[]{:S(2)}, u32[]{:S(2)}) collective-permute-start(bf16[4,32,2176]{2,1,0:T(8,128)(2,1)S(1)} %pad_maximum_fusion.1.refs_0_), channel_id=1, source_target_pairs={{0,4},{1,5},{2,3},{3,2},{4,0},{5,1},{6,7},{7,6},{8,12},{9,13},{10,... | collective-permute-start | bytes 1671176 | tf_op jit(solution)/shard_map/ppermute | solution.py:630
  169.6 7.7 %collective-permute-start.20 = (bf16[4,32,2176]{2,1,0:T(8,128)(2,1)S(1)}, bf16[4,32,2176]{2,1,0:T(8,128)(2,1)S(1)}, u32[]{:S(2)}, u32[]{:S(2)}) collective-permute-start(bf16[4,32,2176]{2,1,0:T(8,128)(2,1)S(1)} %pad_maximum_fusion.1.refs_0_), channel_id=1, source_target_pairs={{0,2},{1,3},{2,0},{3,1},{4,6},{5,7},{6,4},{7,5},{8,10},{9,11},{10,... | collective-permute-start | bytes 1671176 | tf_op jit(solution)/shard_map/ppermute | solution.py:630
  177.1 2.0 %collective-permute-start.21 = (bf16[4,32,2176]{2,1,0:T(8,128)(2,1)S(1)}, bf16[4,32,2176]{2,1,0:T(8,128)(2,1)S(1)}, u32[]{:S(2)}, u32[]{:S(2)}) collective-permute-start(bf16[4,32,2176]{2,1,0:T(8,128)(2,1)S(1)} %collective-permute-done.19.refs_1_), channel_id=1, source_target_pairs={{0,2},{1,3},{2,0},{3,1},{4,6},{5,7},{6,4},{7,5},{8,10},{9,11},{10,... | collective-permute-start | bytes 1671176 | tf_op jit(solution)/shard_map/ppermute | solution.py:630
  (11 other events, 46.6 us)

commit v3 on v2

--- a/solution.py
+++ b/solution.py
@@ -15,7 +15,8 @@
 C1 = C0 * 0.044715
 LIMIT = 20 * 1024 * 1024
 BOTH = ("rows", "mlp")
-SCALE = 8
+OWN_LIMIT = 24 * 1024 * 1024
+OTHER_LIMIT = 32 * 1024 * 1024
 
 
 def mm(a, b, ca=1, cb=0):
@@ -60,6 +61,11 @@
     return pl.BlockSpec(a.shape, lambda i, *_: zeros)
 
 
+def once(a):
+    zeros = (0,) * len(a.shape)
+    return pl.BlockSpec(a.shape, lambda i, *_: zeros, pipeline_mode=pl.Buffered(buffer_count=1))
+
+
 def rows_spec(r, w):
     return pl.BlockSpec((r, w), lambda i, *_: (i, 0))
 
@@ -73,7 +79,7 @@
 
 
 def cost(macs, nbytes=0):
-    return pl.CostEstimate(flops=macs // SCALE, bytes_accessed=nbytes // SCALE, transcendentals=0)
+    return pl.CostEstimate(flops=8 * macs, bytes_accessed=1, transcendentals=0)
 
 
 def slab(ref, r, c):
@@ -92,7 +98,7 @@
     bias = jnp.concatenate([bq, jnp.zeros_like(bq), bv], axis=1)
     joined = (mm(h1, wqkv[...]) + bias).astype(BF)
     joined_o[...] = joined
-    group = 2
+    group = 4
     done = []
     for s0 in range(0, rows // SEQ, group):
         items = [(s, p) for s in range(s0, s0 + group) for p in range(pairs)]
@@ -127,38 +133,94 @@
         attn_fwd_body,
         grid=(t // rows,),
         in_specs=[rows_spec(rows, d), pl.BlockSpec((1, rows // SEQ, SEQ), lambda i: (i, 0, 0))]
-        + [whole(a) for a in (vecs, wqkv, wo)],
+        + [once(a) for a in (vecs, wqkv, wo)],
         out_specs=[rows_spec(rows, w) for w in (3 * d, d, d, d)] + [pl.BlockSpec((d, rows), lambda i: (0, i))],
-        out_shape=[in_hbm((t, 3 * d), BF), in_hbm((t, d), BF), in_hbm((t, d), F32), shape((t, d), BF), in_hbm((d, t), BF)],
+        out_shape=[in_hbm((t, 3 * d), BF), in_hbm((t, d), BF), in_hbm((t, d), F32), in_hbm((t, d), BF), in_hbm((d, t), BF)],
         compiler_params=pltpu.CompilerParams(vmem_limit_bytes=LIMIT),
         cost_estimate=cost(3 * t * d * 4 * d),
         name="attn_fwd",
     )(tok, seg.reshape(t // rows, rows // SEQ, SEQ), vecs, wqkv, wo)
 
 
-def ffn_block(hv, gv, up, ub, down, chunk, gated_o, gup, gdn, gub):
+def fetch_body(first, up, down, bias, out_o):
+    d, half = up.shape
+    out_o[0:d] = up[...]
+    out_o[d : d + half] = down[...]
+    bias = bias[...].astype(F32)
+    bias = jnp.where(first[0] == 0, bias[0:1], bias[1:2])
+    out_o[d + half :] = jnp.broadcast_to(bias, (16, half)).astype(BF)
+
+
+def fetch(first, up, down, bias):
     d, f = up.shape
-    cuts = [slice(c * chunk, (c + 1) * chunk) for c in range(f // chunk)]
-    ahead = [(mm(hv, up[:, s]), mm(gv, down[s, :], 1, 1)) for s in cuts]
-    gates, slopes = [], []
-    for s, (v, dg) in zip(cuts, ahead):
-        v = v + ub[:, s]
-        v2 = v * v
-        a = 0.5 + 0.5 * jnp.tanh(v * (C0 + C1 * v2))
-        act = v * a
-        slope = a + act * (1.0 - a) * (2.0 * C0 + 6.0 * C1 * v2)
-        dh = (dg * slope).astype(BF)
-        gates.append(act.astype(BF))
-        slopes.append(dh)
-        gub[:, s] += fold(dh.astype(F32))
-    gated, dhid = jnp.concatenate(gates, axis=1), jnp.concatenate(slopes, axis=1)
-    gated_o[...] = gated
-    gup[...] += mm(hv.T, dhid)
-    gdn[...] += mm(gv.T, gated)
-    return mm(dhid, up[...], 1, 1)
-
-
-def ffn_own_body(core, h2, g, up, ub, down, gated_o, dh2_o, keep_o, send_o, gub_o, gup, gdn, gub):
+    half = f // 2
+    return pl.pallas_call(
+        fetch_body,
+        grid_spec=pltpu.PrefetchScalarGridSpec(
+            num_scalar_prefetch=1,
+            grid=(1,),
+            in_specs=[
+                pl.BlockSpec((d, half), lambda i, at: (0, at[0])),
+                pl.BlockSpec((half, d), lambda i, at: (at[0], 0)),
+                whole(bias),
+            ],
+            out_specs=pl.BlockSpec((d + half + 16, half), lambda i, at: (0, 0)),
+        ),
+        out_shape=shape((d + half + 16, half), BF),
+        compiler_params=pltpu.CompilerParams(vmem_limit_bytes=LIMIT),
+        cost_estimate=cost(0, 1024 * 1024),
+        name="fetch",
+    )(first, up, down, bias)
+
+
+def gate(v, dg, bias):
+    v = v + bias
+    v2 = v * v
+    a = 0.5 + 0.5 * jnp.tanh(v * (C0 + C1 * v2))
+    act = v * a
+    slope = a + act * (1.0 - a) * (2.0 * C0 + 6.0 * C1 * v2)
+    return act.astype(BF), (dg * slope).astype(BF)
+
+
+def ffn_block(h2, g, up, ub, down, gated_o, dhid, gup, gdn, gub):
+    f = up.shape[1]
+    side, tile = 256, 64
+    units = [(r, c) for r in range(0, h2.shape[0], side) for c in range(0, f, side)]
+
+    def products(r, c):
+        return mm(h2[r : r + side, :], up[:, c : c + side]), mm(g[r : r + side, :], down[c : c + side, :], 1, 1)
+
+    ahead = products(*units[0])
+    for k, (r, c) in enumerate(units):
+        v, dg = ahead
+        if k + 1 < len(units):
+            ahead = products(*units[k + 1])
+        for t in range(0, side, tile):
+            act, dh = gate(v[t : t + tile], dg[t : t + tile], ub[:, c : c + side])
+            gated_o[r + t : r + t + tile, c : c + side] = act
+            dhid[r + t : r + t + tile, c : c + side] = dh
+    dh = dhid[...]
+    gup[...] += mm(h2[...].T, dh)
+    gdn[...] += mm(g[...].T, gated_o[...])
+    gub[...] += fold(dh.astype(F32))
+    return mm(dh, up[...], 1, 1)
+
+
+def put_grads(o, gup, gdn, cols):
+    n = gup.shape[0] // 2
+    for j in range(2):
+        o[j] = gup[j * n : (j + 1) * n, cols].astype(BF)
+        o[2 + j] = gdn[j * n : (j + 1) * n, cols].astype(BF)
+
+
+def put_bias(o, gub):
+    half = o.shape[1]
+    total = jnp.sum(gub[...], axis=0, keepdims=True)
+    for j in range(2):
+        o[j : j + 1] = total[:, j * half : (j + 1) * half]
+
+
+def ffn_own_body(core, h2, g, up, vecs, down, gated_o, dh2_o, keep_o, send_o, gub_o, gup, gdn, gub, dhid):
     i = pl.program_id(0)
     half = up.shape[1] // 2
 
@@ -167,104 +229,61 @@
         for a in (gup, gdn, gub):
             a[...] = jnp.zeros_like(a)
 
-    bias = jnp.concatenate([ub[j : j + 1] for j in range(2)], axis=1).astype(F32)
-    dh2_o[...] = ffn_block(h2[...], g[...], up, bias, down, 256, gated_o, gup, gdn, gub)
+    bias = vecs[...].astype(F32)
+    bias = jnp.concatenate([bias[8:9], bias[9:10]], axis=1)
+    dh2_o[...] = ffn_block(h2, g, up, bias, down, gated_o, dhid, gup, gdn, gub)
 
     @pl.when(i == pl.num_programs(0) - 1)
     def _():
-        mine = pl.ds(pl.multiple_of(core[0] * half, 128), half)
-        theirs = pl.ds(pl.multiple_of((1 - core[0]) * half, 128), half)
-        keep_o[0] = gup[:, mine].astype(BF)
-        keep_o[1] = gdn[:, mine].astype(BF)
-        send_o[0] = gup[:, theirs].astype(BF)
-        send_o[1] = gdn[:, theirs].astype(BF)
-        total = jnp.sum(gub[...], axis=0, keepdims=True)
-        for j in range(2):
-            gub_o[j : j + 1] = total[:, j * half : (j + 1) * half]
-
-
-def ffn_outs(t, d, f):
-    half = f // 2
-    return [in_hbm((t, f), BF), pltpu.VMEM((t, d), F32), shape((2, d, half), BF), shape((2, d, half), BF), shape((2, half), F32)]
-
-
-def ffn_scratch(d, f):
-    return [pltpu.VMEM((d, f), F32), pltpu.VMEM((d, f), F32), pltpu.VMEM((8, f), F32)]
-
-
-def ffn_own(core, h2, g, up, ub, down, rows):
+        put_grads(keep_o, gup, gdn, pl.ds(pl.multiple_of(core[0] * half, 128), half))
+        put_grads(send_o, gup, gdn, pl.ds(pl.multiple_of((1 - core[0]) * half, 128), half))
+        put_bias(gub_o, gub)
+
+
+def ffn_scratch(rows, d, f):
+    return [pltpu.VMEM((d, f), F32), pltpu.VMEM((d, f), F32), pltpu.VMEM((8, f), F32), pltpu.VMEM((rows, f), BF)]
+
+
+def ffn_own(core, h2, g, up, vecs, down, rows):
     t, d = h2.shape
     f = up.shape[1]
-    outs = ffn_outs(t, d, f)
+    half = f // 2
+    outs = [in_hbm((t, f), BF), in_hbm((t, d), F32)] + [shape((4, d // 2, half), BF)] * 2 + [shape((2, half), F32)]
     return pl.pallas_call(
         ffn_own_body,
         grid_spec=pltpu.PrefetchScalarGridSpec(
             num_scalar_prefetch=1,
             grid=(t // rows,),
-            in_specs=[rows_spec(rows, d), rows_spec(rows, d), whole(up), whole(ub), whole(down)],
+            in_specs=[rows_spec(rows, d), rows_spec(rows, d), once(up), whole(vecs), once(down)],
             out_specs=[rows_spec(rows, f), rows_spec(rows, d)] + [whole(o) for o in outs[2:]],
-            scratch_shapes=ffn_scratch(d, f),
+            scratch_shapes=ffn_scratch(rows, d, f),
         ),
         out_shape=outs,
-        compiler_params=pltpu.CompilerParams(vmem_limit_bytes=LIMIT),
+        compiler_params=pltpu.CompilerParams(vmem_limit_bytes=OWN_LIMIT),
         cost_estimate=cost(2 * 5 * t * d * f),
         name="ffn_own",
-    )(core, h2, g, up, ub, down)
-
-
-def ffn_other_body(h2, g, w_send, w_keep, dh2_p, gated_o, dh2_o, keep_o, send_o, gub_o, gup, gdn, gub, up, down, ub):
+    )(core, h2, g, up, vecs, down)
+
+
+def ffn_other_body(
+    h2, g, w_send, w_keep, dh2_p, resid, ctx, wo, vecs,
+    gated_o, dattn_o, dctx_o, keep_o, send_o, gub_o, gout_o, vec_o,
+    gup, gdn, gub, dhid, up, down, ub, gout, vec,
+):
     i = pl.program_id(0)
     d = h2.shape[1]
     half = w_send.shape[1]
 
     @pl.when(i == 0)
     def _():
-        for a in (gup, gdn, gub):
+        for a in (gup, gdn, gub, gout, vec):
             a[...] = jnp.zeros_like(a)
         for c, w in enumerate((w_send, w_keep)):
             up[:, c * half : (c + 1) * half] = w[0:d, :]
             down[c * half : (c + 1) * half, :] = w[d : d + half, :]
             ub[:, c * half : (c + 1) * half] = w[d + half : d + half + 16, :].astype(F32)[0:8]
 
-    dh2_o[...] = dh2_p[...] + ffn_block(h2[...], g[...], up, ub[0:1], down, 256, gated_o, gup, gdn, gub)
-
-    @pl.when(i == pl.num_programs(0) - 1)
-    def _():
-        send_o[0] = gup[:, 0:half].astype(BF)
-        send_o[1] = gdn[:, 0:half].astype(BF)
-        keep_o[0] = gup[:, half:].astype(BF)
-        keep_o[1] = gdn[:, half:].astype(BF)
-        total = jnp.sum(gub[...], axis=0, keepdims=True)
-        for j in range(2):
-            gub_o[j : j + 1] = total[:, j * half : (j + 1) * half]
-
-
-def ffn_other(h2, g, w_send, w_keep, dh2_p, rows):
-    t, d = h2.shape
-    f = 2 * w_send.shape[1]
-    outs = ffn_outs(t, d, f)
-    return pl.pallas_call(
-        ffn_other_body,
-        grid=(t // rows,),
-        in_specs=[rows_spec(rows, d), rows_spec(rows, d), whole(w_send), whole(w_keep), rows_spec(rows, d)],
-        out_specs=[rows_spec(rows, f), rows_spec(rows, d)] + [whole(o) for o in outs[2:]],
-        out_shape=outs,
-        scratch_shapes=ffn_scratch(d, f) + [pltpu.VMEM((d, f), BF), pltpu.VMEM((f, d), BF), pltpu.VMEM((8, f), F32)],
-        compiler_params=pltpu.CompilerParams(vmem_limit_bytes=LIMIT),
-        cost_estimate=cost(2 * 5 * t * d * f),
-        name="ffn_other",
-    )(h2, g, w_send, w_keep, dh2_p)
-
-
-def mid_body(dh2, resid, g, ctx, wo, vecs, dattn_o, dctx_o, gout_o, vec_o, gout, vec):
-    i = pl.program_id(0)
-
-    @pl.when(i == 0)
-    def _():
-        gout[...] = jnp.zeros_like(gout)
-        vec[...] = jnp.zeros_like(vec)
-
-    dh = dh2[...]
+    dh = dh2_p[...] + ffn_block(h2, g, up, ub[0:1], down, gated_o, dhid, gup, gdn, gub)
     n2, inv2 = layer_norm(resid[...])
     gf = g[...].astype(F32)
     dattn = (gf + norm_back(dh, n2, inv2, vecs[...].astype(F32)[3:4])).astype(BF)
@@ -276,25 +295,38 @@
 
     @pl.when(i == pl.num_programs(0) - 1)
     def _():
+        put_grads(send_o, gup, gdn, slice(0, half))
+        put_grads(keep_o, gup, gdn, slice(half, 2 * half))
         gout_o[...] = gout[...].astype(BF)
+        put_bias(gub_o, gub)
         for j in range(4):
             vec_o[j : j + 1] = jnp.sum(vec[j], axis=0, keepdims=True)
 
 
-def mid(dh2, resid, g, ctx, wo, vecs, rows):
-    t, d = dh2.shape
-    outs = [pltpu.VMEM((t, d), BF), pltpu.VMEM((t, d), BF), shape((d, d), BF), shape((4, d), F32)]
+def ffn_other(h2, g, w_send, w_keep, dh2_p, resid, ctx, wo, vecs, rows):
+    t, d = h2.shape
+    half = w_send.shape[1]
+    f = 2 * half
+    outs = [in_hbm((t, f), BF), in_hbm((t, d), BF), in_hbm((t, d), BF)]
+    outs += [shape((4, d // 2, half), BF)] * 2 + [shape((2, half), F32), in_hbm((d, d), BF), shape((4, d), F32)]
     return pl.pallas_call(
-        mid_body,
-        grid=(t // rows,),
-        in_specs=[rows_spec(rows, d)] * 4 + [whole(wo), whole(vecs)],
-        out_specs=[rows_spec(rows, d)] * 2 + [whole(o) for o in outs[2:]],
+        ffn_other_body,
+        grid_spec=pltpu.PrefetchScalarGridSpec(
+            num_scalar_prefetch=0,
+            grid=(t // rows,),
+            in_specs=[rows_spec(rows, d), rows_spec(rows, d), once(w_send), once(w_keep)]
+            + [rows_spec(rows, d)] * 3
+            + [once(wo), whole(vecs)],
+            out_specs=[rows_spec(rows, f), rows_spec(rows, d), rows_spec(rows, d)] + [whole(o) for o in outs[3:]],
+            scratch_shapes=ffn_scratch(rows, d, f)
+            + [pltpu.VMEM((d, f), BF), pltpu.VMEM((f, d), BF), pltpu.VMEM((8, f), F32)]
+            + [pltpu.VMEM((d, d), F32), pltpu.VMEM((4, 8, d), F32)],
+        ),
         out_shape=outs,
-        scratch_shapes=[pltpu.VMEM((d, d), F32), pltpu.VMEM((4, 8, d), F32)],
-        compiler_params=pltpu.CompilerParams(vmem_limit_bytes=LIMIT),
-        cost_estimate=cost(3 * 2 * t * d * d),
-        name="mid",
-    )(dh2, resid, g, ctx, wo, vecs)
+        compiler_params=pltpu.CompilerParams(vmem_limit_bytes=OTHER_LIMIT),
+        cost_estimate=cost(2 * (5 * t * d * f + 2 * t * d * d)),
+        name="ffn_other",
+    )(h2, g, w_send, w_keep, dh2_p, resid, ctx, wo, vecs)
 
 
 def attn_bwd_block(q, k, v, dc, seg, dj_o):
@@ -408,7 +440,7 @@
                 pl.BlockSpec((1, rows // SEQ, SEQ), lambda i, *_: (i, 0, 0)),
                 pl.BlockSpec((d, rows), lambda i, *_: (0, i)),
             ]
-            + [whole(a) for a in rest],
+            + [once(a) for a in rest],
             out_specs=[rows_spec(rows, 3 * d)] + [whole(o) for o in outs[1:]],
             scratch_shapes=[pltpu.VMEM((d, 3 * d), F32), pltpu.VMEM((8, 3 * d), F32), pltpu.VMEM((64, 128), F32)],
         ),
@@ -419,48 +451,38 @@
     )(place, joined, dctx, seg.reshape(t // rows, rows // SEQ, SEQ), n1t, *rest)
 
 
-def in_grad_body(dj, tok, dattn, wqkv, vecs, out_o):
+def in_grad_body(dj, tok, dattn, wqkv, vecs, *refs):
     dh1 = mm(dj[...], wqkv[...], 1, 1)
     n1, inv1 = layer_norm(tok[...].astype(F32))
     gain = vecs[...].astype(F32)[0:1]
-    out_o[...] = (dattn[...].astype(F32) + norm_back(dh1, n1, inv1, gain)).astype(BF)
-
-
-def in_grad_of(dj, tok, dattn, wqkv, vecs, rows):
-    t, d = tok.shape
+    refs[-1][...] = (dattn[...].astype(F32) + norm_back(dh1, n1, inv1, gain)).astype(BF)
+
+
+def in_part(body, rows, first, count, streams, fixed, before, macs, name):
+    t, d = streams[1].shape
+    spec = lambda w: pl.BlockSpec((rows, w), lambda i: (i + first, 0))
+    args = (*streams, *fixed) + (() if before is None else (before,))
     return pl.pallas_call(
-        in_grad_body,
-        grid=(t // rows,),
-        in_specs=[rows_spec(rows, 3 * d), rows_spec(rows, d), rows_spec(rows, d), whole(wqkv), whole(vecs)],
-        out_specs=rows_spec(rows, d),
-        out_shape=shape((t, d), BF),
+        body,
+        grid=(count,),
+        in_specs=[spec(a.shape[1]) for a in streams]
+        + [once(a) for a in fixed]
+        + ([] if before is None else [pl.BlockSpec(memory_space=pl.ANY)]),
+        out_specs=spec(d),
+        out_shape=in_hbm((t, d), BF),
+        input_output_aliases={} if before is None else {len(args) - 1: 0},
         compiler_params=pltpu.CompilerParams(vmem_limit_bytes=LIMIT),
-        cost_estimate=cost(2 * t * d * 3 * d),
-        name="in_grad",
-    )(dj, tok, dattn, wqkv, vecs)
-
-
-def layer_out_body(own, oth, resid, down, w_send, w_keep, vecs, out_o):
+        cost_estimate=cost(2 * rows * count * macs),
+        name=name,
+    )(*args)
+
+
+def layer_out_body(own, resid, oth, down, w_send, w_keep, vecs, *refs):
     d = resid.shape[1]
     half = w_send.shape[1]
     out = mm(own[...], down[...])
     out += mm(oth[:, 0:half], w_send[d : d + half, :]) + mm(oth[:, half:], w_keep[d : d + half, :])
-    out_o[...] = (resid[...] + out + vecs[...].astype(F32)[7:8]).astype(BF)
-
-
-def layer_out_of(own, oth, resid, down, w_send, w_keep, vecs, rows):
-    t, d = resid.shape
-    f = own.shape[1]
-    return pl.pallas_call(
-        layer_out_body,
-        grid=(t // rows,),
-        in_specs=[rows_spec(rows, f)] * 2 + [rows_spec(rows, d)] + [whole(a) for a in (down, w_send, w_keep, vecs)],
-        out_specs=rows_spec(rows, d),
-        out_shape=shape((t, d), BF),
-        compiler_params=pltpu.CompilerParams(vmem_limit_bytes=LIMIT),
-        cost_estimate=cost(2 * t * d * 2 * f),
-        name="layer_out",
-    )(own, oth, resid, down, w_send, w_keep, vecs)
+    refs[-1][...] = (resid[...] + out + vecs[...].astype(F32)[7:8]).astype(BF)
 
 
 def on_chip(body, outs, at, *args, name):
@@ -480,22 +502,23 @@
 
 
 def split_body(at, own_a, own_b, oth_a, oth_b, keep_o, send_o):
-    def total(o, h):
+    def total(o, j):
         a, b = (own_a, own_b) if o == 0 else (oth_a, oth_b)
-        return plus(a[h], b[h])
+        return plus(a[j], b[j])
 
     @pl.when(at[0] == 0)
     def _():
         v = at[1]
         for o in range(2):
-            keep_o[o] = total(o, v)
-            send_o[o] = total(o, 1 - v)
+            for p in range(2):
+                keep_o[2 * o + p] = total(o, 2 * v + p)
+                send_o[2 * o + p] = total(o, 2 * (1 - v) + p)
 
     @pl.when(at[0] == 1)
     def _():
-        for h in range(2):
-            keep_o[h] = total(0, h)
-            send_o[h] = total(1, h)
+        for j in range(4):
+            keep_o[j] = total(0, j)
+            send_o[j] = total(1, j)
 
 
 def halve(at, which, a, b):
@@ -534,7 +557,7 @@
 
 def finish_rest_body(at, columns, *refs):
     qkv_o, qv_o, gout_o, gain1_o, bias1_o, bo_o, gain2_o, bias2_o, gub_o, b2_o, small = refs[4:]
-    d = gout_o.shape[0]
+    d = qkv_o.shape[0]
     step, n = d // 16, d // 128
     pieces = []
     for c in range(2):
@@ -636,106 +659,112 @@
         return lax.optimization_barrier((value, *done))[0]
 
     u0 = [0, "y"] + list(range(1, up_dims))
-    u1 = ["y"] + list(range(1, up_dims)) + [0]
+    u1 = ["y", 1, 0] + list(range(2, up_dims))
     q0 = [0, "y", 1, 2] + list(range(3, up_dims))
     q1 = ["y", 0, 2, 1] + list(range(3, up_dims))
-    big, small = (by_core(bit(u0[0]), bit(u1[1])), by_core(bit(u1[1]), bit(u0[0]))), (
-        by_core(bit(u0[2]), bit(u1[2])), by_core(bit(u1[2]), bit(u0[2])),
-    )
     at = jnp.stack(
-        [core, bit(0), by_core(0, bit(u1[1])), big[0], small[0], big[1], small[1]]
+        [core, bit(0), by_core(0, bit(u1[1]))]
+        + [by_core(bit(u0[0]), bit(u1[1])), by_core(bit(u0[2]), bit(u1[2]))]
+        + [by_core(bit(u1[1]), bit(u0[0])), by_core(bit(u1[2]), bit(u0[2]))]
         + [by_core(bit(a), bit(b)) for a, b in zip(q0[:3], q1[:3])]
         + [y]
         + [by_core(bit(b), bit(a)) for a, b in zip(q0[:3], q1[:3])]
     ).astype(jnp.int32)
     place = jnp.stack([y, core]).astype(jnp.int32)
     core_s = core.reshape(1).astype(jnp.int32)
-    vmem = lambda v: pltpu.with_memory_space_constraint(v, pltpu.VMEM)
     hbm = lambda v: pltpu.with_memory_space_constraint(v, pltpu.HBM)
-    tokens, out_grad = hbm(tokens), hbm(out_grad)
-
-    first = 1 - core
-    bias_rows = jnp.broadcast_to(lax.dynamic_slice(up_bias, (first * half,), (half,))[None], (16, half))
-    w_mine = jnp.concatenate(
-        [
-            lax.dynamic_slice(up_weight, (0, first * half), (d, half)),
-            lax.dynamic_slice(down_weight, (first * half, 0), (half, d)),
-            bias_rows,
-        ],
-        axis=0,
-    )
-    w_send = swap(w_mine, "y")
+    qkv_free, down_free = qkv_weight, down_weight
+    tokens, out_grad, qkv_weight, out_weight, up_weight, down_weight = map(
+        hbm, (tokens, out_grad, qkv_weight, out_weight, up_weight, down_weight)
+    )
+
+    bias = up_bias.reshape(2, half)
     vecs = jnp.concatenate(
         [
             jnp.stack([ln1_gain, ln1_bias, out_bias, ln2_gain, ln2_bias, qv_bias[0], qv_bias[1], down_bias]),
-            up_bias.reshape(2, half),
+            bias,
             jnp.zeros((6, d), BF),
         ]
     )
     columns = jnp.stack([ln1_gain, ln1_bias], axis=1).astype(F32)
+
+    w_send = swap(fetch(1 - core_s, up_weight, down_weight, bias), "y")
     joined, ctx, resid, h2, n1t = attn_fwd(tokens, segment_ids, vecs, qkv_weight, out_weight, rows=512)
     gated_own, dh2_own, own_keep, own_send, gub_own = ffn_own(
-        core_s, h2, out_grad, up_weight, vecs[8:10], down_weight, rows=512
-    )
-    w_send = after(w_send, own_send)
+        core_s, hbm(h2), out_grad, up_weight, vecs, down_weight, rows=512
+    )
+    w_send = hbm(after(w_send, own_send))
     w_keep = swap(w_send, "core")
     own_recv = swap(own_send, "core")
-    gated_oth, dh2, oth_keep, oth_send, gub_oth = ffn_other(h2, out_grad, w_send, w_keep, vmem(dh2_own), rows=512)
+    gated_oth, dattn, dctx, oth_keep, oth_send, gub_oth, gout, vec = ffn_other(
+        hbm(h2), out_grad, w_send, w_keep, hbm(dh2_own), hbm(resid), hbm(ctx), out_weight, vecs, rows=512
+    )
     oth_recv = swap(oth_send, "core")
-    dattn, dctx, gout, vec = mid(vmem(dh2), hbm(resid), out_grad, hbm(ctx), out_weight, vecs, rows=512)
-
-    block = shape((2, d, half), BF)
-    oth_recv = after(oth_recv, vec)
+    blocks = t // 512
+
+    def layer_out_part(first, count, before, *ready):
+        return in_part(
+            layer_out_body, 512, first, count, (hbm(gated_own), hbm(after(resid, *ready)), hbm(gated_oth)),
+            (down_weight, w_send, hbm(w_keep), vecs), before, 4 * half * d, "layer_out",
+        )
+
+    def in_grad_part(first, count, before, *ready):
+        return in_part(
+            in_grad_body, 512, first, count, (dj, tokens, hbm(after(dattn, *ready))), (qkv_free, vecs), before,
+            3 * d * d, "in_grad",
+        )
+
+    block = shape((4, d // 2, half), BF)
     u_keep, u_send = on_chip(split_body, [block] * 2, at, own_keep, own_recv, oth_keep, oth_recv, name="split")
     u_recv = swap(u_send, u0[0], u1[0])
     dj, q_keep, q_send = attn_bwd(
-        place, hbm(joined), after(dctx, u_keep), segment_ids, hbm(n1t), qkv_weight, gout, gub_own, gub_oth, vec, rows=512
+        place, hbm(joined), hbm(after(dctx, u_keep)), segment_ids, hbm(n1t), qkv_weight, hbm(gout), gub_own, gub_oth, vec,
+        rows=512,
     )
     q_recv = swap(q_send, "core")
-    cut = lambda v: v.reshape(2, d // 2, half)
     u_keep, u_send = halve(at, 2, u_keep, after(u_recv, q_send))
-    u_recv = swap(cut(u_send), u0[1], u1[1])
-    in_grad = in_grad_of(dj, tokens, after(dattn, u_keep), qkv_weight, vecs, rows=512)
+    u_recv = swap(u_send, u0[1], u1[1])
+    in_grad = in_grad_part(0, blocks // 2, None, u_keep)
     q_keep, q_send = halve(at, 7, q_keep, after(q_recv, in_grad))
     q_recv = swap(q_send, q0[0], q1[0])
-    layer_out = layer_out_of(
-        hbm(gated_own), hbm(gated_oth), hbm(after(resid, q_keep)), down_weight, w_send, w_keep, vecs, rows=512
-    )
-    u_keep, u_send = halve(at, 4, cut(u_keep), after(u_recv, layer_out))
+    in_grad = in_grad_part(blocks // 2, blocks // 2, in_grad, q_keep)
+    u_keep, u_send = halve(at, 4, u_keep, after(u_recv, in_grad))
     u_recv = swap(u_send, u0[2], u1[2])
     q_keep, q_send = halve(at, 8, q_keep, after(q_recv, u_keep))
     q_recv = swap(q_send, q0[1], q1[1])
     u_one = plus(u_keep, after(u_recv, q_keep))
+    u_recv = swap(u_one, u0[3], u1[3])
+    q_keep, q_send = halve(at, 9, q_keep, after(q_recv, u_one))
+    q_recv = swap(q_send, q0[2], q1[2])
+    layer_out = layer_out_part(0, blocks // 2, None, q_keep)
+    q_one = plus(q_keep, after(q_recv, layer_out))
     for k in range(3, len(u0)):
-        u_recv = swap(u_one, u0[k], u1[k])
-        if k == 3:
-            q_keep, q_send = halve(at, 9, q_keep, after(q_recv, u_one))
-            q_recv = swap(q_send, q0[2], q1[2])
-            u_recv = after(u_recv, q_keep)
-        u_one = plus(u_one, u_recv)
+        q_recv = swap(q_one, q0[k], q1[k])
+        u_one = plus(u_one, after(u_recv, q_one))
+        if k + 1 < len(u0):
+            u_recv = swap(u_one, u0[k + 1], u1[k + 1])
+            q_one = plus(q_one, after(q_recv, u_one))
     u_ag = swap(u_one, u0[2], u1[2])
-    q_one = plus(q_keep, after(q_recv, u_one))
-    for k in range(3, len(q0)):
-        q_recv = swap(q_one, q0[k], q1[k])
-        if k == 3:
-            u_pair = jnp.concatenate([u_one, after(u_ag, q_one)], axis=0)
-            u_far = swap(u_pair, u0[0], u1[1])
-            u_pair_c = swap(u_pair, "core")
-            q_recv = after(q_recv, u_pair)
-        q_one = plus(q_one, q_recv)
+    q_one = plus(q_one, after(q_recv, u_one))
     q_ag = swap(q_one, q0[2], q1[2])
-    u_far = after(u_far, q_one)
+    u_pair = jnp.concatenate([u_one, after(u_ag, q_one)], axis=0)
+    u_far = swap(u_pair, u0[0], u1[1])
+    u_pair_c = swap(u_pair, "core")
+    q_pair = jnp.concatenate([q_one, after(q_ag, u_pair)], axis=0)
+    q_ag = swap(q_pair, q0[1], q1[1])
+    q_four = jnp.concatenate([q_pair, after(q_ag, u_pair)], axis=0)
+    q_far = swap(q_four, q0[0], q1[0])
+    q_four_c = swap(q_four, "core")
+    layer_out = layer_out_part(blocks // 2, blocks // 2, layer_out, q_four)
+    u_far = after(u_far, layer_out)
     u_far_c = swap(u_far, "core")
-    q_pair = jnp.concatenate([q_one, after(q_ag, u_far)], axis=0)
-    q_ag = swap(q_pair, q0[1], q1[1])
     grad_up, grad_down = on_chip(
         finish_ffn_body, [shape((d, 2 * half), F32), shape((2 * half, d), F32)], at,
-        u_pair, u_far, u_pair_c, after(u_far_c, q_pair), name="finish_ffn",
-    )
-    q_four = jnp.concatenate([q_pair, after(q_ag, grad_up)], axis=0)
-    q_far = swap(q_four, q0[0], q1[0])
+        u_pair, u_far, u_pair_c, u_far_c, name="finish_ffn",
+    )
+    q_far = after(q_far, grad_up)
     grad_qkv, grad_qv, grad_wo, g1, c1, bo, g2, c2, gub, b2 = finish_rest(
-        at, columns, q_four, q_far, swap(q_four, "core"), swap(q_far, "core")
+        at, columns, q_four, q_far, q_four_c, swap(q_far, "core")
     )
     flat = lambda v: v.reshape(-1)
     return (

time: 183 us -> 164 us (0.90)
  waiting for transfers between devices: 43.2 us -> 20.7 us
  starting transfers between devices: 25.3 us -> 31.4 us
  local copies, waits for them, and re-layouts: 7.81 us -> 2.16 us
  Pallas kernels: 103 us -> 108 us
    ppermute x22, waiting for transfers between devices: 43.2 us -> 20.7 us  [swap(): return lax.ppermute(value, BOTH, pairs)]
    ppermute x22, starting transfers between devices: 25.3 us -> 31.4 us  [swap(): return lax.ppermute(value, BOTH, pairs)]
    unnamed x42 -> x26, local copies, waits for them, and re-layouts: 5.28 us -> 1.1 us
    pallas_call x4 -> x6, Pallas kernels: 43.1 us -> 47 us  [the longest x1 23.4 us: ffn_other(): pl.pallas_call(ffn_other_body, grid_spec=pltpu.PrefetchScalarGridSpec(num...]
    dynamic_slice x2 -> x0, local copies, waits for them, and re-layouts: 2.19 us -> none  [the longest x1 1.43 us: local(): lax.dynamic_slice(down_weight, (first * half, 0), (half, d))]
  transfers between devices with their start and end apart: 22 -> 22, of which waited for: 8 -> 11; matrix products, arithmetic and copies ran while one was open for 0% -> 0% of each run, Pallas kernels for 44% -> 62%
where the time goes in v3:
time: 164 us
  Pallas kernels  108 us (66%)
  starting transfers between devices  31.4 us (19%)
  waiting for transfers between devices  20.7 us (13%)
  local copies, waits for them, and re-layouts  2.16 us (1%)
    ppermute x22, starting transfers between devices, swap(): return lax.ppermute(value, BOTH, pairs)  31.4 us
    pallas_call x1, Pallas kernels, ffn_other(): pl.pallas_call(ffn_other_body, grid_spec=pltpu.PrefetchScalarGridSpec(num...  23.4 us
    pallas_call x4, Pallas kernels, in_part(): pl.pallas_call(body, grid=(count,), in_specs=[spec(a.shape[1]) for a in s...  22.3 us
    ppermute x22, waiting for transfers between devices, swap(): return lax.ppermute(value, BOTH, pairs)  20.7 us
    pallas_call x1, Pallas kernels, attn_bwd(): pl.pallas_call(attn_bwd_body, grid_spec=pltpu.PrefetchScalarGridSpec(num_...  17.5 us
    pallas_call x1, Pallas kernels, ffn_own(): pl.pallas_call(ffn_own_body, grid_spec=pltpu.PrefetchScalarGridSpec(num_s...  17.4 us
    pallas_call x1, Pallas kernels, attn_fwd(): pl.pallas_call(attn_fwd_body, grid=(t // rows,), in_specs=[rows_spec(rows...  14.5 us
    pallas_call x7, Pallas kernels, on_chip(): pl.pallas_call(body, in_specs=[pl.BlockSpec(memory_space=pltpu.SMEM)] + [...  8.83 us
  transfers between devices with their start and end apart: 22, of which 11 were waited for; matrix products, arithmetic and copies ran while one was open for 0% of the time, Pallas kernels for 62%

profile of v3, /device:TPU:0, one launch (start us, length us, event | category | flops | bytes accessed | tf_op | source)
XLA Modules:
  0.0 164.1 jit_solution(4100636903915998409)
XLA Ops:
  1.5 1.3 fetch.1
  2.7 3.0 %collective-permute-start = (bf16[1040,512]{1,0:T(8,128)(2,1)S(1)}, bf16[1040,512]{1,0:T(8,128)(2,1)}, u32[]{:S(2)}, u32[]{:S(2)}) collective-permute-start(bf16[1040,512]{1,0:T(8,128)(2,1)S(1)} %fetch.1), channel_id=1, source_target_pairs={{0,1},{1,0},{2,3},{3,2},{4,5},{5,4},{6,7},{7,6},{8,9},{9,8},{10,11... | collective-permute-start | bytes 3194888 | tf_op jit(solution)/shard_map/ppermute | solution.py:653
  6.0 14.5 %attn_fwd.1 = (bf16[2048,1536]{1,0:T(8,128)(2,1)}, bf16[2048,512]{1,0:T(8,128)(2,1)}, f32[2048,512]{1,0:T(8,128)}, bf16[2048,512]{1,0:T(8,128)(2,1)}, bf16[512,2048]{1,0:T(8,128)(2,1)}) custom-call(bf16[2048,512]{1,0:T(8,128)(2,1)} %tok.5, s32[4,4,128]{2,1,0:T(4,128)S(1)} %bitcast.18, bf16[16,512]{1,0:T(8,128)(2,1)S(1)} %concatenate.13.vecs, ...), custom_call_target="tpu_custom_call" | custom-call | flops 51539607552 | bytes 1 | tf_op jit(solution)/shard_map/attn_fwd/pallas_call | solution.py:132
  20.5 17.4 %ffn_own.1 = (bf16[2048,1024]{1,0:T(8,128)(2,1)}, f32[2048,512]{1,0:T(8,128)}, bf16[4,256,512]{2,1,0:T(8,128)(2,1)S(1)}, bf16[4,256,512]{2,1,0:T(8,128)(2,1)}, f32[2,512]{1,0:T(2,128)S(1)}) custom-call(s32[1]{0:T(128)} %bitcast.core, bf16[2048,512]{1,0:T(8,128)(2,1)} %get-tuple-element.79.h2, bf16[2048,512]{1,0:T(8,128)(2,1)} %g.3, bf16[512,1024]{1,0:T(8,128)(2,1)} %up.3, ...), custom_call_target="tpu_custom_call" | custom-call | flops 85899345920 | bytes 1 | tf_op jit(solution)/shard_map/ffn_own/pallas_call | solution.py:252
  38.4 2.4 %collective-permute-done.1.w_keep = bf16[1040,512]{1,0:T(8,128)(2,1)S(1)} collective-permute-done((bf16[1040,512]{1,0:T(8,128)(2,1)}, bf16[1040,512]{1,0:T(8,128)(2,1)S(1)}, u32[]{:S(2)}, u32[]{:S(2)}) %collective-permute-start.1) | collective-permute-done | bytes 1064992 | tf_op jit(solution)/shard_map/ppermute | solution.py:653
  41.9 23.4 %ffn_other.1 = (bf16[2048,1024]{1,0:T(8,128)(2,1)}, bf16[2048,512]{1,0:T(8,128)(2,1)}, bf16[2048,512]{1,0:T(8,128)(2,1)}, bf16[4,256,512]{2,1,0:T(8,128)(2,1)S(1...) custom-call(bf16[2048,512]{1,0:T(8,128)(2,1)} %get-tuple-element.79.h2, ...), custom_call_target="tpu_custom_call" | custom-call | flops 103079215104 | bytes 1 | tf_op jit(solution)/shard_map/ffn_other/pallas_call | solution.py:312
  65.7 2.7 %collective-permute-done.3.oth_b = bf16[4,256,512]{2,1,0:T(8,128)(2,1)} collective-permute-done((bf16[4,256,512]{2,1,0:T(8,128)(2,1)}, bf16[4,256,512]{2,1,0:T(8,128)(2,1)}, u32[]{:S(2)}, u32[]{:S(2)}) %collective-permute-start.3) | collective-permute-done | bytes 1048608 | tf_op jit(solution)/shard_map/ppermute | solution.py:653
  68.4 1.9 %split.1 = (bf16[4,256,512]{2,1,0:T(8,128)(2,1)S(1)}, bf16[4,256,512]{2,1,0:T(8,128)(2,1)S(1)}) custom-call(s32[14]{0:T(128)S(1)} %stack.82.at, bf16[4,256,512]{2,1,0:T(8,128)(2,1)S(1)} %get-tuple-element.88.own_a, bf16[4,256,512]{2,1,0:T(8,128)(2,1)S(1)} %collective-permute-done.2.own_b, bf16[4,256,512]{2,1,0:T(8,128)(2,1)S(1)} %get-tuple-element.89.oth_a, ...), custom_call_target="tpu_custom_call" | custom-call | bytes 1 | tf_op jit(solution)/shard_map/split/pallas_call | solution.py:489
  70.3 1.6 collective-permute-start.5
  71.8 17.5 %attn_bwd.1 = (bf16[2048,1536]{1,0:T(8,128)(2,1)S(1)}, bf16[8,32,2176]{2,1,0:T(8,128)(2,1)S(1)}, bf16[8,32,2176]{2,1,0:T(8,128)(2,1)S(1)}) custom-call(s32[2]{0:T(128)S(1)} %pad_add_fusion.place, bf16[2048,1536]{1,0:T(8,128)(2,1)} %get-tuple-element.82.joined, bf16[2048,512]{1,0:T(8,128)(2,1)} %get-tuple-element.92.dc, s32[4,4,128]{2,1,0:T(4,128)S(1)} %bitcast.19, ...), custom_call_target="tpu_custom_call" | custom-call | flops 103079215104 | bytes 1 | tf_op jit(solution)/shard_map/attn_bwd/pallas_call | solution.py:432
  90.8 4.7 %in_grad.2.refs_0_ = bf16[2048,512]{1,0:T(8,128)(2,1)} custom-call(bf16[2048,1536]{1,0:T(8,128)(2,1)S(1)} %get-tuple-element.100.dj, bf16[2048,512]{1,0:T(8,128)(2,1)} %tok.5, bf16[2048,512]{1,0:T(8,128)(2,1)} %get-tuple-element.110.dattn, bf16[512,1536]{1,0:T(8,128)(2,1)S(1)} %copy-done, bf16[16,512]{1,0:T(8,128)(2,1)S(1)} %concatenate.13.vecs), custom_call_target="tpu_custom_call" | custom-call | flops 12884901888 | bytes 1 | tf_op jit(solution)/shard_map/in_grad/pallas_call | solution.py:465
  96.3 1.5 collective-permute-start.6
  97.8 4.7 %in_grad.3 = bf16[2048,512]{1,0:T(8,128)(2,1)} custom-call(bf16[2048,1536]{1,0:T(8,128)(2,1)S(1)} %get-tuple-element.100.dj, bf16[2048,512]{1,0:T(8,128)(2,1)} %tok.5, bf16[2048,512]{1,0:T(8,128)(2,1)} %get-tuple-element.110.dattn, bf16[512,1536]{1,0:T(8,128)(2,1)S(1)} %copy-done, ...), custom_call_target="tpu_custom_call", output_to_operand_aliasing={{}: (5, {})} | custom-call | flops 12884901888 | bytes 1 | tf_op jit(solution)/shard_map/in_grad/pallas_call | solution.py:465
  103.2 1.6 %collective-permute-start.9 = (bf16[1,256,512]{2,1,0:T(8,128)(2,1)S(1)}, bf16[1,256,512]{2,1,0:T(8,128)(2,1)S(1)}, u32[]{:S(2)}, u32[]{:S(2)}) collective-permute-start(bf16[1,256,512]{2,1,0:T(8,128)(2,1)S(1)} %get-tuple-element.116), channel_id=1, source_target_pairs={{0,8},{1,9},{2,6},{3,7},{4,12},{5,13},{6,2},{7,3},{8,0},{9,1},{10,... | collective-permute-start | bytes 786440 | tf_op jit(solution)/shard_map/ppermute | solution.py:653
  106.6 1.6 collective-permute-start.8
  108.2 1.4 collective-permute-done.9
  109.7 2.7 %collective-permute-start.12 = (bf16[1,256,512]{2,1,0:T(8,128)(2,1)S(1)}, bf16[1,256,512]{2,1,0:T(8,128)(2,1)S(1)}, u32[]{:S(2)}, u32[]{:S(2)}) collective-permute-start(bf16[1,256,512]{2,1,0:T(8,128)(2,1)S(1)} %add_convert_fusion.1), channel_id=1, source_target_pairs={{0,16},{1,17},{2,18},{3,19},{4,20},{5,21},{6,22},{7,23},{8,24},{9,... | collective-permute-start | bytes 786440 | tf_op jit(solution)/shard_map/ppermute | solution.py:653
  113.8 2.7 %collective-permute-start.10 = (bf16[1,32,2176]{2,1,0:T(8,128)(2,1)S(1)}, bf16[1,32,2176]{2,1,0:T(8,128)(2,1)S(1)}, u32[]{:S(2)}, u32[]{:S(2)}) collective-permute-start(bf16[1,32,2176]{2,1,0:T(8,128)(2,1)S(1)} %get-tuple-element.120), channel_id=1, source_target_pairs={{0,8},{1,9},{2,18},{3,19},{4,12},{5,13},{6,22},{7,23},{8,0},{9,1},... | collective-permute-start | bytes 417800 | tf_op jit(solution)/shard_map/ppermute | solution.py:653
  116.5 6.4 %layer_out.2.refs_0_ = bf16[2048,512]{1,0:T(8,128)(2,1)} custom-call(bf16[2048,1024]{1,0:T(8,128)(2,1)} %get-tuple-element.80.own, f32[2048,512]{1,0:T(8,128)} %get-tuple-element.129.resid, bf16[2048,1024]{1,0:T(8,128)(2,1)} %get-tuple-element.122.oth, bf16[1024,512]{1,0:T(8,128)(2,1)} %down.7, bf16[1040,512]{1,0:T(8,128)(2,1)} %collective-permute-done.w_send, ...), custom_call_target="tpu_custom_call" | custom-call | flops 17179869184 | bytes 1 | tf_op jit(solution)/shard_map/layer_out/pallas_call | solution.py:465
  123.0 5.8 %collective-permute-start.11 = (bf16[1,32,2176]{2,1,0:T(8,128)(2,1)S(1)}, bf16[1,32,2176]{2,1,0:T(8,128)(2,1)S(1)}, u32[]{:S(2)}, u32[]{:S(2)}) collective-permute-start(bf16[1,32,2176]{2,1,0:T(8,128)(2,1)S(1)} %add_convert_fusion.3), channel_id=1, source_target_pairs={{0,16},{1,17},{2,10},{3,11},{4,20},{5,21},{6,14},{7,15},{8,24},{9,... | collective-permute-start | bytes 417800 | tf_op jit(solution)/shard_map/ppermute | solution.py:653
  128.9 2.5 %collective-permute-start.14 = (bf16[1,256,512]{2,1,0:T(8,128)(2,1)S(1)}, bf16[1,256,512]{2,1,0:T(8,128)(2,1)S(1)}, u32[]{:S(2)}, u32[]{:S(2)}) collective-permute-start(bf16[1,256,512]{2,1,0:T(8,128)(2,1)S(1)} %add_convert_fusion), channel_id=1, source_target_pairs={{0,8},{1,9},{2,6},{3,7},{4,12},{5,13},{6,2},{7,3},{8,0},{9,1},{10,... | collective-permute-start | bytes 786440 | tf_op jit(solution)/shard_map/ppermute | solution.py:653
  132.0 2.7 %collective-permute-start.13 = (bf16[1,32,2176]{2,1,0:T(8,128)(2,1)S(1)}, bf16[1,32,2176]{2,1,0:T(8,128)(2,1)S(1)}, u32[]{:S(2)}, u32[]{:S(2)}) collective-permute-start(bf16[1,32,2176]{2,1,0:T(8,128)(2,1)S(1)} %add_convert_fusion.2), channel_id=1, source_target_pairs={{0,8},{1,9},{2,18},{3,19},{4,12},{5,13},{6,22},{7,23},{8,0},{9,1},... | collective-permute-start | bytes 417800 | tf_op jit(solution)/shard_map/ppermute | solution.py:653
  134.7 2.1 %collective-permute-done.14 = bf16[1,256,512]{2,1,0:T(8,128)(2,1)S(1)} collective-permute-done((bf16[1,256,512]{2,1,0:T(8,128)(2,1)S(1)}, bf16[1,256,512]{2,1,0:T(8,128)(2,1)S(1)}, u32[]{:S(2)}, u32[]{:S(2)}) %collective-permute-start.14) | collective-permute-done | bytes 262176 | tf_op jit(solution)/shard_map/ppermute | solution.py:653
  136.9 2.0 %collective-permute-done.13 = bf16[1,32,2176]{2,1,0:T(8,128)(2,1)S(1)} collective-permute-done((bf16[1,32,2176]{2,1,0:T(8,128)(2,1)S(1)}, bf16[1,32,2176]{2,1,0:T(8,128)(2,1)S(1)}, u32[]{:S(2)}, u32[]{:S(2)}) %collective-permute-start.13) | collective-permute-done | bytes 139296 | tf_op jit(solution)/shard_map/ppermute | solution.py:653
  139.0 1.6 collective-permute-start.15
  141.1 4.5 %collective-permute-done.15 = bf16[2,32,2176]{2,1,0:T(8,128)(2,1)S(1)} collective-permute-done((bf16[2,32,2176]{2,1,0:T(8,128)(2,1)S(1)}, bf16[2,32,2176]{2,1,0:T(8,128)(2,1)S(1)}, u32[]{:S(2)}, u32[]{:S(2)}) %collective-permute-start.15) | collective-permute-done | bytes 278560 | tf_op jit(solution)/shard_map/ppermute | solution.py:653
  145.6 1.5 collective-permute-start.16
  147.2 6.5 %layer_out.3 = bf16[2048,512]{1,0:T(8,128)(2,1)} custom-call(bf16[2048,1024]{1,0:T(8,128)(2,1)} %get-tuple-element.80.own, f32[2048,512]{1,0:T(8,128)} %get-tuple-element.129.resid, bf16[2048,1024]{1,0:T(8,128)(2,1)} %get-tuple-element.122.oth, bf16[1024,512]{1,0:T(8,128)(2,1)} %down.7, ...), custom_call_target="tpu_custom_call", output_to_operand_aliasing={{}: (7, {})} | custom-call | flops 17179869184 | bytes 1 | tf_op jit(solution)/shard_map/layer_out/pallas_call | solution.py:465
  154.2 1.4 collective-permute-done.19.refs_3_
  155.6 3.3 %finish_ffn.1 = (f32[512,1024]{1,0:T(8,128)}, f32[1024,512]{1,0:T(8,128)}) custom-call(s32[14]{0:T(128)S(1)} %stack.82.at, bf16[2,256,512]{2,1,0:T(8,128)(2,1)S(1)} %pad_maximum_fusion.1.refs_0_, bf16[2,256,512]{2,1,0:T(8,128)(2,1)S(1)} %collective-permute-done.17.refs_1_, bf16[2,256,512]{2,1,0:T(8,128)(2,1)S(1)} %collective-permute-done.18.refs_2_, ...), custom_call_target="tpu_custom_call" | custom-call | bytes 1 | tf_op jit(solution)/shard_map/finish_ffn/pallas_call | solution.py:489
  159.3 1.6 collective-permute-done.21.refs_3_
  160.9 3.2 %finish_rest.1 = (f32[512,1536]{1,0:T(8,128)}, f32[2,512]{1,0:T(2,128)}, f32[512,512]{1,0:T(8,128)}, f32[1,512]{1,0:T(1,128)}, f32[1,512]{1,0:T(1,128)}, /*index...) custom-call(s32[14]{0:T(128)S(1)} %stack.82.at, ...), custom_call_target="tpu_custom_call" | custom-call | bytes 1 | tf_op jit(solution)/shard_map/finish_rest/pallas_call | solution.py:601
  (77 shorter events, 11.4 us)
Async XLA Ops:
  0.6 5.1 %copy-start.5 = (bf16[512]{0:T(512)(128)(2,1)S(1)}, bf16[512]{0:T(512)(128)(2,1)}, u32[]{:S(2)}) copy-start(bf16[512]{0:T(512)(128)(2,1)} %param.17) | copy-start | bytes 3076
  0.7 5.1 %copy-start.3 = (bf16[512]{0:T(512)(128)(2,1)S(1)}, bf16[512]{0:T(512)(128)(2,1)}, u32[]{:S(2)}) copy-start(bf16[512]{0:T(512)(128)(2,1)} %param.18) | copy-start | bytes 3076
  0.7 5.1 %copy-start.8 = (bf16[512]{0:T(512)(128)(2,1)S(1)}, bf16[512]{0:T(512)(128)(2,1)}, u32[]{:S(2)}) copy-start(bf16[512]{0:T(512)(128)(2,1)} %param.22) | copy-start | bytes 3076
  0.7 5.1 %copy-start.9 = (bf16[512]{0:T(512)(128)(2,1)S(1)}, bf16[512]{0:T(512)(128)(2,1)}, u32[]{:S(2)}) copy-start(bf16[512]{0:T(512)(128)(2,1)} %param.23) | copy-start | bytes 3076
  0.7 5.2 %copy-start.10 = (bf16[512]{0:T(512)(128)(2,1)S(1)}, bf16[512]{0:T(512)(128)(2,1)}, u32[]{:S(2)}) copy-start(bf16[512]{0:T(512)(128)(2,1)} %param.24) | copy-start | bytes 3076
  0.7 5.2 %copy-start.11 = (bf16[512]{0:T(512)(128)(2,1)S(1)}, bf16[512]{0:T(512)(128)(2,1)}, u32[]{:S(2)}) copy-start(bf16[512]{0:T(512)(128)(2,1)} %param.28) | copy-start | bytes 3076
  0.7 5.2 %copy-start.7 = (bf16[2,512]{1,0:T(2,128)(2,1)S(1)}, bf16[2,512]{1,0:T(2,128)(2,1)}, u32[]{:S(2)}) copy-start(bf16[2,512]{1,0:T(2,128)(2,1)} %param.20) | copy-start | bytes 6148
  0.7 5.2 %copy-start.1 = (s32[16,128]{1,0:T(8,128)S(1)}, s32[16,128]{1,0:T(8,128)}, u32[]{:S(2)}) copy-start(s32[16,128]{1,0:T(8,128)} %param.16) | copy-start | bytes 24580
  2.7 35.1 %collective-permute-start = (bf16[1040,512]{1,0:T(8,128)(2,1)S(1)}, bf16[1040,512]{1,0:T(8,128)(2,1)}, u32[]{:S(2)}, u32[]{:S(2)}) collective-permute-start(bf16[1040,512]{1,0:T(8,128)(2,1)S(1)} %fetch.1), channel_id=1, source_target_pairs={{0,1},{1,0},{2,3},{3,2},{4,5},{5,4},{6,7},{7,6},{8,9},{9,8},{10,11... | collective-permute-start | bytes 3194888 | tf_op jit(solution)/shard_map/ppermute | solution.py:653
  37.9 3.0 %collective-permute-start.1 = (bf16[1040,512]{1,0:T(8,128)(2,1)}, bf16[1040,512]{1,0:T(8,128)(2,1)S(1)}, u32[]{:S(2)}, u32[]{:S(2)}) collective-permute-start(bf16[1040,512]{1,0:T(8,128)(2,1)} %collective-permute-done.w_send), channel_id=1, source_target_pairs={{0,2},{1,3},{2,0},{3,1},{4,6},{5,7},{6,4},{7,5},{8,10},{9,11},{10,... | collective-permute-start | bytes 3194888 | tf_op jit(solution)/shard_map/ppermute | solution.py:653
  37.9 27.7 %collective-permute-start.2 = (bf16[4,256,512]{2,1,0:T(8,128)(2,1)}, bf16[4,256,512]{2,1,0:T(8,128)(2,1)S(1)}, u32[]{:S(2)}, u32[]{:S(2)}) collective-permute-start(bf16[4,256,512]{2,1,0:T(8,128)(2,1)} %get-tuple-element.83), channel_id=1, source_target_pairs={{0,2},{1,3},{2,0},{3,1},{4,6},{5,7},{6,4},{7,5},{8,10},{9,11},{10,... | collective-permute-start | bytes 3145736 | tf_op jit(solution)/shard_map/ppermute | solution.py:653
  65.3 3.1 %collective-permute-start.3 = (bf16[4,256,512]{2,1,0:T(8,128)(2,1)}, bf16[4,256,512]{2,1,0:T(8,128)(2,1)}, u32[]{:S(2)}, u32[]{:S(2)}) collective-permute-start(bf16[4,256,512]{2,1,0:T(8,128)(2,1)} %get-tuple-element.90), channel_id=1, source_target_pairs={{0,2},{1,3},{2,0},{3,1},{4,6},{5,7},{6,4},{7,5},{8,10},{9,11},{10,... | collective-permute-start | bytes 3145736 | tf_op jit(solution)/shard_map/ppermute | solution.py:653
  70.3 19.1 %collective-permute-start.5 = (bf16[4,256,512]{2,1,0:T(8,128)(2,1)S(1)}, bf16[4,256,512]{2,1,0:T(8,128)(2,1)S(1)}, u32[]{:S(2)}, u32[]{:S(2)}) collective-permute-start(bf16[4,256,512]{2,1,0:T(8,128)(2,1)S(1)} %get-tuple-element.102), channel_id=1, source_target_pairs={{0,4},{1,5},{2,3},{3,2},{4,0},{5,1},{6,7},{7,6},{8,12},{9,13},{10,... | collective-permute-start | bytes 3145736 | tf_op jit(solution)/shard_map/ppermute | solution.py:653
  89.3 6.2 %collective-permute-start.4 = (bf16[8,32,2176]{2,1,0:T(8,128)(2,1)S(1)}, bf16[8,32,2176]{2,1,0:T(8,128)(2,1)S(1)}, u32[]{:S(2)}, u32[]{:S(2)}) collective-permute-start(bf16[8,32,2176]{2,1,0:T(8,128)(2,1)S(1)} %get-tuple-element.99), channel_id=1, source_target_pairs={{0,2},{1,3},{2,0},{3,1},{4,6},{5,7},{6,4},{7,5},{8,10},{9,11},{10,... | collective-permute-start | bytes 3342344 | tf_op jit(solution)/shard_map/ppermute | solution.py:653
  90.2 12.3 %collective-permute-start.7 = (bf16[2,256,512]{2,1,0:T(8,128)(2,1)S(1)}, bf16[2,256,512]{2,1,0:T(8,128)(2,1)S(1)}, u32[]{:S(2)}, u32[]{:S(2)}) collective-permute-start(bf16[2,256,512]{2,1,0:T(8,128)(2,1)S(1)} %get-tuple-element.109), channel_id=1, source_target_pairs={{0,1},{1,0},{2,10},{3,11},{4,5},{5,4},{6,14},{7,15},{8,9},{9,8},{1... | collective-permute-start | bytes 1572872 | tf_op jit(solution)/shard_map/ppermute | solution.py:653
  96.3 9.6 %collective-permute-start.6 = (bf16[4,32,2176]{2,1,0:T(8,128)(2,1)S(1)}, bf16[4,32,2176]{2,1,0:T(8,128)(2,1)S(1)}, u32[]{:S(2)}, u32[]{:S(2)}) collective-permute-start(bf16[4,32,2176]{2,1,0:T(8,128)(2,1)S(1)} %get-tuple-element.108), channel_id=1, source_target_pairs={{0,4},{1,5},{2,3},{3,2},{4,0},{5,1},{6,7},{7,6},{8,12},{9,13},{10,... | collective-permute-start | bytes 1671176 | tf_op jit(solution)/shard_map/ppermute | solution.py:653
  103.2 6.4 %collective-permute-start.9 = (bf16[1,256,512]{2,1,0:T(8,128)(2,1)S(1)}, bf16[1,256,512]{2,1,0:T(8,128)(2,1)S(1)}, u32[]{:S(2)}, u32[]{:S(2)}) collective-permute-start(bf16[1,256,512]{2,1,0:T(8,128)(2,1)S(1)} %get-tuple-element.116), channel_id=1, source_target_pairs={{0,8},{1,9},{2,6},{3,7},{4,12},{5,13},{6,2},{7,3},{8,0},{9,1},{10,... | collective-permute-start | bytes 786440 | tf_op jit(solution)/shard_map/ppermute | solution.py:653
  106.6 6.6 %collective-permute-start.8 = (bf16[2,32,2176]{2,1,0:T(8,128)(2,1)S(1)}, bf16[2,32,2176]{2,1,0:T(8,128)(2,1)S(1)}, u32[]{:S(2)}, u32[]{:S(2)}) collective-permute-start(bf16[2,32,2176]{2,1,0:T(8,128)(2,1)S(1)} %get-tuple-element.115), channel_id=1, source_target_pairs={{0,1},{1,0},{2,6},{3,7},{4,5},{5,4},{6,2},{7,3},{8,9},{9,8},{10,14... | collective-permute-start | bytes 835592 | tf_op jit(solution)/shard_map/ppermute | solution.py:653
  109.7 19.2 %collective-permute-start.12 = (bf16[1,256,512]{2,1,0:T(8,128)(2,1)S(1)}, bf16[1,256,512]{2,1,0:T(8,128)(2,1)S(1)}, u32[]{:S(2)}, u32[]{:S(2)}) collective-permute-start(bf16[1,256,512]{2,1,0:T(8,128)(2,1)S(1)} %add_convert_fusion.1), channel_id=1, source_target_pairs={{0,16},{1,17},{2,18},{3,19},{4,20},{5,21},{6,22},{7,23},{8,24},{9,... | collective-permute-start | bytes 786440 | tf_op jit(solution)/shard_map/ppermute | solution.py:653
  113.8 9.2 %collective-permute-start.10 = (bf16[1,32,2176]{2,1,0:T(8,128)(2,1)S(1)}, bf16[1,32,2176]{2,1,0:T(8,128)(2,1)S(1)}, u32[]{:S(2)}, u32[]{:S(2)}) collective-permute-start(bf16[1,32,2176]{2,1,0:T(8,128)(2,1)S(1)} %get-tuple-element.120), channel_id=1, source_target_pairs={{0,8},{1,9},{2,18},{3,19},{4,12},{5,13},{6,22},{7,23},{8,0},{9,1},... | collective-permute-start | bytes 417800 | tf_op jit(solution)/shard_map/ppermute | solution.py:653
  123.0 8.9 %collective-permute-start.11 = (bf16[1,32,2176]{2,1,0:T(8,128)(2,1)S(1)}, bf16[1,32,2176]{2,1,0:T(8,128)(2,1)S(1)}, u32[]{:S(2)}, u32[]{:S(2)}) collective-permute-start(bf16[1,32,2176]{2,1,0:T(8,128)(2,1)S(1)} %add_convert_fusion.3), channel_id=1, source_target_pairs={{0,16},{1,17},{2,10},{3,11},{4,20},{5,21},{6,14},{7,15},{8,24},{9,... | collective-permute-start | bytes 417800 | tf_op jit(solution)/shard_map/ppermute | solution.py:653
  128.9 7.9 %collective-permute-start.14 = (bf16[1,256,512]{2,1,0:T(8,128)(2,1)S(1)}, bf16[1,256,512]{2,1,0:T(8,128)(2,1)S(1)}, u32[]{:S(2)}, u32[]{:S(2)}) collective-permute-start(bf16[1,256,512]{2,1,0:T(8,128)(2,1)S(1)} %add_convert_fusion), channel_id=1, source_target_pairs={{0,8},{1,9},{2,6},{3,7},{4,12},{5,13},{6,2},{7,3},{8,0},{9,1},{10,... | collective-permute-start | bytes 786440 | tf_op jit(solution)/shard_map/ppermute | solution.py:653
  132.0 6.9 %collective-permute-start.13 = (bf16[1,32,2176]{2,1,0:T(8,128)(2,1)S(1)}, bf16[1,32,2176]{2,1,0:T(8,128)(2,1)S(1)}, u32[]{:S(2)}, u32[]{:S(2)}) collective-permute-start(bf16[1,32,2176]{2,1,0:T(8,128)(2,1)S(1)} %add_convert_fusion.2), channel_id=1, source_target_pairs={{0,8},{1,9},{2,18},{3,19},{4,12},{5,13},{6,22},{7,23},{8,0},{9,1},... | collective-permute-start | bytes 417800 | tf_op jit(solution)/shard_map/ppermute | solution.py:653
  139.0 6.6 %collective-permute-start.15 = (bf16[2,32,2176]{2,1,0:T(8,128)(2,1)S(1)}, bf16[2,32,2176]{2,1,0:T(8,128)(2,1)S(1)}, u32[]{:S(2)}, u32[]{:S(2)}) collective-permute-start(bf16[2,32,2176]{2,1,0:T(8,128)(2,1)S(1)} %pad_maximum_fusion.2), channel_id=1, source_target_pairs={{0,1},{1,0},{2,6},{3,7},{4,5},{5,4},{6,2},{7,3},{8,9},{9,8},{10,14... | collective-permute-start | bytes 835592 | tf_op jit(solution)/shard_map/ppermute | solution.py:653
  140.5 13.1 %collective-permute-start.17 = (bf16[2,256,512]{2,1,0:T(8,128)(2,1)S(1)}, bf16[2,256,512]{2,1,0:T(8,128)(2,1)S(1)}, u32[]{:S(2)}, u32[]{:S(2)}) collective-permute-start(bf16[2,256,512]{2,1,0:T(8,128)(2,1)S(1)} %pad_maximum_fusion.1.refs_0_), channel_id=1, source_target_pairs={{0,4},{1,5},{2,10},{3,11},{4,0},{5,1},{6,14},{7,15},{8,12},{9,13},... | collective-permute-start | bytes 1572872 | tf_op jit(solution)/shard_map/ppermute | solution.py:653
  141.1 13.1 %collective-permute-start.18 = (bf16[2,256,512]{2,1,0:T(8,128)(2,1)S(1)}, bf16[2,256,512]{2,1,0:T(8,128)(2,1)S(1)}, u32[]{:S(2)}, u32[]{:S(2)}) collective-permute-start(bf16[2,256,512]{2,1,0:T(8,128)(2,1)S(1)} %pad_maximum_fusion.1.refs_0_), channel_id=1, source_target_pairs={{0,2},{1,3},{2,0},{3,1},{4,6},{5,7},{6,4},{7,5},{8,10},{9,11},{10,... | collective-permute-start | bytes 1572872 | tf_op jit(solution)/shard_map/ppermute | solution.py:653
  145.6 13.3 %collective-permute-start.16 = (bf16[4,32,2176]{2,1,0:T(8,128)(2,1)S(1)}, bf16[4,32,2176]{2,1,0:T(8,128)(2,1)S(1)}, u32[]{:S(2)}, u32[]{:S(2)}) collective-permute-start(bf16[4,32,2176]{2,1,0:T(8,128)(2,1)S(1)} %pad_maximum_fusion.refs_0_), channel_id=1, source_target_pairs={{0,4},{1,5},{2,3},{3,2},{4,0},{5,1},{6,7},{7,6},{8,12},{9,13},{10,... | collective-permute-start | bytes 1671176 | tf_op jit(solution)/shard_map/ppermute | solution.py:653
  153.6 5.5 %copy-start.4 = (bf16[512]{0:T(512)(128)(2,1)S(1)}, bf16[512]{0:T(512)(128)(2,1)}, u32[]{:S(2)}) copy-start(bf16[512]{0:T(512)(128)(2,1)} %param.18) | copy-start | bytes 3076
  153.6 5.5 %copy-start.6 = (bf16[512]{0:T(512)(128)(2,1)S(1)}, bf16[512]{0:T(512)(128)(2,1)}, u32[]{:S(2)}) copy-start(bf16[512]{0:T(512)(128)(2,1)} %param.17) | copy-start | bytes 3076
  153.6 2.0 %collective-permute-start.19 = (bf16[2,256,512]{2,1,0:T(8,128)(2,1)S(1)}, bf16[2,256,512]{2,1,0:T(8,128)(2,1)S(1)}, u32[]{:S(2)}, u32[]{:S(2)}) collective-permute-start(bf16[2,256,512]{2,1,0:T(8,128)(2,1)S(1)} %collective-permute-done.17.refs_1_), channel_id=1, source_target_pairs={{0,2},{1,3},{2,0},{3,1},{4,6},{5,7},{6,4},{7,5},{8,10},{9,11},{10,... | collective-permute-start | bytes 1572872 | tf_op jit(solution)/shard_map/ppermute | solution.py:653
  153.7 5.6 %collective-permute-start.20 = (bf16[4,32,2176]{2,1,0:T(8,128)(2,1)S(1)}, bf16[4,32,2176]{2,1,0:T(8,128)(2,1)S(1)}, u32[]{:S(2)}, u32[]{:S(2)}) collective-permute-start(bf16[4,32,2176]{2,1,0:T(8,128)(2,1)S(1)} %pad_maximum_fusion.refs_0_), channel_id=1, source_target_pairs={{0,2},{1,3},{2,0},{3,1},{4,6},{5,7},{6,4},{7,5},{8,10},{9,11},{10,... | collective-permute-start | bytes 1671176 | tf_op jit(solution)/shard_map/ppermute | solution.py:653
  159.0 2.0 %collective-permute-start.21 = (bf16[4,32,2176]{2,1,0:T(8,128)(2,1)S(1)}, bf16[4,32,2176]{2,1,0:T(8,128)(2,1)S(1)}, u32[]{:S(2)}, u32[]{:S(2)}) collective-permute-start(bf16[4,32,2176]{2,1,0:T(8,128)(2,1)S(1)} %collective-permute-done.16.refs_1_), channel_id=1, source_target_pairs={{0,2},{1,3},{2,0},{3,1},{4,6},{5,7},{6,4},{7,5},{8,10},{9,11},{10,... | collective-permute-start | bytes 1671176 | tf_op jit(solution)/shard_map/ppermute | solution.py:653
  (3 other events, 6.0 us)

commit v4 on v3

--- a/solution.py
+++ b/solution.py
@@ -86,7 +86,7 @@
     return ref[r, c * 128 : (c + 1) * 128]
 
 
-def attn_fwd_body(tok, seg, vecs, wqkv, wo, joined_o, ctx_o, resid_o, h2_o, n1t_o):
+def attn_fwd_body(tok, seg, vecs, wqkv, wo, joined_o, ctx_o, resid_o, h2_o, n1t_o, probs_o):
     rows, width = tok.shape
     pairs = width // 128
     vec = vecs[...].astype(F32)
@@ -116,6 +116,9 @@
                 e = jnp.exp(v - jnp.max(v, axis=0, keepdims=True))
                 two.append((e * (1.0 / jnp.sum(e, axis=0, keepdims=True))).astype(BF))
             probs.append(jnp.concatenate(two, axis=0))
+            for h in range(2):
+                at = (2 * p + h) * SEQ
+                probs_o[s * SEQ : (s + 1) * SEQ, at : at + SEQ] = two[h]
         outs = [mm(pr, stack_heads(part(s, 2, p)), 0, 0).astype(BF) for (s, p), pr in zip(items, probs)]
         for j in range(group):
             done.append(jnp.concatenate(outs[j * pairs : (j + 1) * pairs], axis=1))
@@ -134,8 +137,8 @@
         grid=(t // rows,),
         in_specs=[rows_spec(rows, d), pl.BlockSpec((1, rows // SEQ, SEQ), lambda i: (i, 0, 0))]
         + [once(a) for a in (vecs, wqkv, wo)],
-        out_specs=[rows_spec(rows, w) for w in (3 * d, d, d, d)] + [pl.BlockSpec((d, rows), lambda i: (0, i))],
-        out_shape=[in_hbm((t, 3 * d), BF), in_hbm((t, d), BF), in_hbm((t, d), F32), in_hbm((t, d), BF), in_hbm((d, t), BF)],
+        out_specs=[rows_spec(rows, w) for w in (3 * d, d, d, d)] + [pl.BlockSpec((d, rows), lambda i: (0, i)), rows_spec(rows, 2 * d)],
+        out_shape=[in_hbm((t, 3 * d), BF), in_hbm((t, d), BF), in_hbm((t, d), F32), in_hbm((t, d), BF), in_hbm((d, t), BF), in_hbm((t, 2 * d), BF)],
         compiler_params=pltpu.CompilerParams(vmem_limit_bytes=LIMIT),
         cost_estimate=cost(3 * t * d * 4 * d),
         name="attn_fwd",
@@ -329,35 +332,27 @@
     )(h2, g, w_send, w_keep, dh2_p, resid, ctx, wo, vecs)
 
 
-def attn_bwd_block(q, k, v, dc, seg, dj_o):
+def attn_bwd_block(q, k, v, dc, probs, dj_o):
     rows, width = q.shape
     pairs = width // 128
     group = 2
     for s0 in range(0, rows // SEQ, group):
         items = [(slice(s * SEQ, (s + 1) * SEQ), p) for s in range(s0, s0 + group) for p in range(pairs)]
-        allow = [allowed_of(seg[0, s : s + 1, :], True) for s in range(s0, s0 + group) for p in range(pairs)]
+        both = lambda r, p: probs[r, 2 * p * SEQ : 2 * (p + 1) * SEQ]
         qs = [stack_heads(slab(q, r, p) * BF(0.125)) for r, p in items]
         dcs = [stack_heads(slab(dc, r, p)) for r, p in items]
-        scores = [mm(slab(k, r, p), a, 1, 1) for (r, p), a in zip(items, qs)]
         dprobs = [mm(slab(v, r, p), a, 1, 1) for (r, p), a in zip(items, dcs)]
-        probs, dscores = [], []
-        for ok, sc, dp in zip(allow, scores, dprobs):
-            pb, ds = [], []
-            for h in range(2):
-                cols = slice(h * SEQ, (h + 1) * SEQ)
-                w = jnp.where(ok, sc[:, cols], -1e9)
-                e = jnp.exp(w - jnp.max(w, axis=0, keepdims=True))
-                pr = e * (1.0 / jnp.sum(e, axis=0, keepdims=True))
-                ds.append((pr * (dp[:, cols] - jnp.sum(pr * dp[:, cols], axis=0, keepdims=True))).astype(BF))
-                pb.append(pr.astype(BF))
-            probs.append(pb)
-            dscores.append(ds)
-        for (r, p), pb, a in zip(items, probs, dcs):
-            dj_o[r, 2 * width + p * 128 : 2 * width + (p + 1) * 128] = mm(jnp.concatenate(pb, axis=1), a).astype(BF)
+        dscores = []
+        for (r, p), dp in zip(items, dprobs):
+            pr = both(r, p).astype(F32)
+            dscores.append((pr * (dp - jnp.sum(pr * dp, axis=0, keepdims=True))).astype(BF))
+        for (r, p), a in zip(items, dcs):
+            dj_o[r, 2 * width + p * 128 : 2 * width + (p + 1) * 128] = mm(both(r, p), a).astype(BF)
         for (r, p), ds, a in zip(items, dscores, qs):
-            dj_o[r, width + p * 128 : width + (p + 1) * 128] = mm(jnp.concatenate(ds, axis=1), a).astype(BF)
+            dj_o[r, width + p * 128 : width + (p + 1) * 128] = mm(ds, a).astype(BF)
         for (r, p), ds in zip(items, dscores):
-            dq = mm(jnp.concatenate(ds, axis=0), stack_heads(slab(k, r, p)), 0, 0) * 0.125
+            tall = jnp.concatenate([ds[:, 0:SEQ], ds[:, SEQ:]], axis=0)
+            dq = mm(tall, stack_heads(slab(k, r, p)), 0, 0) * 0.125
             dj_o[r, p * 128 : (p + 1) * 128] = dq.astype(BF)
 
 
@@ -369,7 +364,7 @@
     return gain, jnp.sum(mm(hi, w, 1, 1) + mm(lo, w, 1, 1), axis=0, keepdims=True)
 
 
-def attn_bwd_body(place, joined, dc, seg, n1t, wqkv, gout, gub_own, gub_oth, vec, dj_o, keep_o, send_o, acc, cs, small):
+def attn_bwd_body(place, joined, dc, probs, n1t, wqkv, gout, gub_own, gub_oth, vec, dj_o, keep_o, send_o, acc, cs, small):
     i = pl.program_id(0)
     d = n1t.shape[0]
     step = d // 16
@@ -380,7 +375,7 @@
         cs[...] = jnp.zeros_like(cs)
 
     q, k, v = (joined.at[:, j * d : (j + 1) * d] for j in range(3))
-    attn_bwd_block(q, k, v, dc, seg, dj_o)
+    attn_bwd_block(q, k, v, dc, probs, dj_o)
     dj = dj_o[...]
     acc[...] += mm(n1t[...], dj)
     cs[...] += fold(dj.astype(F32))
@@ -425,7 +420,7 @@
                 send_o[b, :, 4 * d :] = small[b * step : (b + 1) * step].astype(BF)
 
 
-def attn_bwd(place, joined, dctx, seg, n1t, wqkv, gout, gub_own, gub_oth, vec, rows):
+def attn_bwd(place, joined, dctx, probs, n1t, wqkv, gout, gub_own, gub_oth, vec, rows):
     d, t = n1t.shape
     outs = [pltpu.VMEM((t, 3 * d), BF)] + [shape((8, d // 16, 4 * d + 128), BF)] * 2
     rest = (wqkv, gout, gub_own, gub_oth, vec)
@@ -437,7 +432,7 @@
             in_specs=[
                 rows_spec(rows, 3 * d),
                 rows_spec(rows, d),
-                pl.BlockSpec((1, rows // SEQ, SEQ), lambda i, *_: (i, 0, 0)),
+                rows_spec(rows, 2 * d),
                 pl.BlockSpec((d, rows), lambda i, *_: (0, i)),
             ]
             + [once(a) for a in rest],
@@ -448,7 +443,7 @@
         compiler_params=pltpu.CompilerParams(vmem_limit_bytes=LIMIT + 8 * 1024 * 1024),
         cost_estimate=cost(8 * t * d * 3 * d),
         name="attn_bwd",
-    )(place, joined, dctx, seg.reshape(t // rows, rows // SEQ, SEQ), n1t, *rest)
+    )(place, joined, dctx, probs, n1t, *rest)
 
 
 def in_grad_body(dj, tok, dattn, wqkv, vecs, *refs):
@@ -535,29 +530,52 @@
 
 def finish_ffn_body(at, *refs):
     up_o, down_o = refs[4:]
+    quarter = refs[0].shape[1]
     for c in range(2):
-        chunk = at[0] if c == 0 else 1 - at[0]
-        quarter, half = refs[0].shape[1:]
-        units = pl.ds(pl.multiple_of(chunk * half, 128), half)
-        for j in range(2):
-            pair = refs[2 * c + j]
-            which = at[3 + 2 * c] if j == 0 else 1 - at[3 + 2 * c]
-            for i in range(2):
-                part = at[4 + 2 * c] if i == 0 else 1 - at[4 + 2 * c]
-                cols = pl.ds(pl.multiple_of(part * quarter, 128), quarter)
-
-                @pl.when(which == 0)
-                def _(pair=pair, i=i, cols=cols, units=units):
-                    up_o[cols, units] = pair[i].astype(F32)
-
-                @pl.when(which == 1)
-                def _(pair=pair, i=i, cols=cols, units=units):
-                    down_o[units, cols] = pair[i].astype(F32).T
+
+        @pl.when(pl.program_id(0) == c)
+        def _(c=c):
+            for j in range(2):
+                pair = refs[2 * c + j]
+                which = at[3 + 2 * c] if j == 0 else 1 - at[3 + 2 * c]
+                for i in range(2):
+                    part = at[4 + 2 * c] if i == 0 else 1 - at[4 + 2 * c]
+                    cols = pl.ds(pl.multiple_of(part * quarter, 128), quarter)
+
+                    @pl.when(which == 0)
+                    def _(pair=pair, i=i, cols=cols):
+                        up_o[cols, :] = pair[i].astype(F32)
+
+                    @pl.when(which == 1)
+                    def _(pair=pair, i=i, cols=cols):
+                        down_o[:, cols] = pair[i].astype(F32).T
+
+
+def finish_ffn(at, *pairs):
+    half = pairs[0].shape[2]
+    d = 2 * pairs[0].shape[1]
+    unit = lambda i, at: jnp.where(i == 0, at[0], 1 - at[0])
+    return pl.pallas_call(
+        finish_ffn_body,
+        grid_spec=pltpu.PrefetchScalarGridSpec(
+            num_scalar_prefetch=1,
+            grid=(2,),
+            in_specs=[whole(a) for a in pairs],
+            out_specs=[
+                pl.BlockSpec((d, half), lambda i, at: (0, unit(i, at))),
+                pl.BlockSpec((half, d), lambda i, at: (unit(i, at), 0)),
+            ],
+        ),
+        out_shape=[shape((d, 2 * half), F32), shape((2 * half, d), F32)],
+        compiler_params=pltpu.CompilerParams(vmem_limit_bytes=24 * 1024 * 1024),
+        cost_estimate=cost(0, 4 * 1024 * 1024),
+        name="finish_ffn",
+    )(at, *pairs)
 
 
 def finish_rest_body(at, columns, *refs):
     qkv_o, qv_o, gout_o, gain1_o, bias1_o, bo_o, gain2_o, bias2_o, gub_o, b2_o, small = refs[4:]
-    d = qkv_o.shape[0]
+    d = gout_o.shape[1]
     step, n = d // 16, d // 128
     pieces = []
     for c in range(2):
@@ -567,30 +585,40 @@
             for i in range(4):
                 bits = (a0 if j == 0 else 1 - a0, b0 if i < 2 else 1 - b0, c0 if i % 2 == 0 else 1 - c0)
                 pieces.append((refs[2 * c + j], i, 8 * core + 4 * bits[0] + 2 * bits[1] + bits[2]))
-    for ref, i, at_ in pieces:
-
-        @pl.when(at_ < 2)
-        def _(ref=ref, i=i, at_=at_):
-            small[pl.ds(pl.multiple_of(at_ * step, step), step)] = ref[i, :, 4 * d :].astype(F32)
+    @pl.when(pl.program_id(0) == 0)
+    def _():
+        for ref, i, at_ in pieces:
+
+            @pl.when(at_ < 2)
+            def _(ref=ref, i=i, at_=at_):
+                small[pl.ds(pl.multiple_of(at_ * step, step), step)] = ref[i, :, 4 * d :].astype(F32)
 
     def row(first, count):
         return jnp.concatenate([small[first + j : first + j + 1] for j in range(count)], axis=1)
 
     csum = row(8 * n, 3 * n)
-    for ref, i, at_ in pieces:
-        rows = pl.ds(pl.multiple_of(at_ * step, step), step)
-        gain, bias = columns[rows, 0:1], columns[rows, 1:2]
-        qkv_o[rows, :] = ref[i, :, 0 : 3 * d].astype(F32) * gain + bias * csum
-        gout_o[rows, :] = ref[i, :, 3 * d : 4 * d].astype(F32)
-    qv_o[0:1] = csum[:, 0:d]
-    qv_o[1:2] = csum[:, 2 * d :]
-    for o, j in ((bo_o, 0), (gain2_o, 1), (bias2_o, 2), (b2_o, 3)):
-        o[...] = row(j * n, n)
-    gain1_o[...] = row(11 * n, n)
-    bias1_o[...] = row(12 * n, n)
-    first = 4 * n + 2 * n * at[10]
-    for j in range(2 * n):
-        gub_o[:, j * 128 : (j + 1) * 128] = small[pl.ds(first + j, 1)]
+    for c in range(2):
+
+        @pl.when(pl.program_id(0) == c)
+        def _(c=c):
+            for ref, i, at_ in pieces[8 * c : 8 * c + 8]:
+                rows = pl.ds(pl.multiple_of(at_ * step, step), step)
+                here = pl.ds(pl.multiple_of((at_ % 8) * step, step), step)
+                gain, bias = columns[rows, 0:1], columns[rows, 1:2]
+                qkv_o[here, :] = ref[i, :, 0 : 3 * d].astype(F32) * gain + bias * csum
+                gout_o[here, :] = ref[i, :, 3 * d : 4 * d].astype(F32)
+
+    @pl.when(pl.program_id(0) == 0)
+    def _():
+        qv_o[0:1] = csum[:, 0:d]
+        qv_o[1:2] = csum[:, 2 * d :]
+        for o, j in ((bo_o, 0), (gain2_o, 1), (bias2_o, 2), (b2_o, 3)):
+            o[...] = row(j * n, n)
+        gain1_o[...] = row(11 * n, n)
+        bias1_o[...] = row(12 * n, n)
+        first = 4 * n + 2 * n * at[10]
+        for j in range(2 * n):
+            gub_o[:, j * 128 : (j + 1) * 128] = small[pl.ds(first + j, 1)]
 
 
 def finish_rest(at, columns, *pieces):
@@ -598,12 +626,18 @@
     one = shape((1, d), F32)
     outs = [shape((d, 3 * d), F32), shape((2, d), F32), shape((d, d), F32)] + [one] * 5 + [shape((1, 2 * d), F32), one]
     args = (columns, *pieces)
+    half = lambda i, at: (jnp.where(i == 0, at[0], 1 - at[0]), 0)
     return pl.pallas_call(
         finish_rest_body,
-        in_specs=[pl.BlockSpec(memory_space=pltpu.SMEM)] + [pl.BlockSpec(memory_space=pltpu.VMEM)] * len(args),
-        out_specs=[pl.BlockSpec(memory_space=pltpu.VMEM)] * len(outs),
+        grid_spec=pltpu.PrefetchScalarGridSpec(
+            num_scalar_prefetch=1,
+            grid=(2,),
+            in_specs=[whole(a) for a in args],
+            out_specs=[pl.BlockSpec((d // 2, 3 * d), half), whole(outs[1]), pl.BlockSpec((d // 2, d), half)]
+            + [whole(o) for o in outs[3:]],
+            scratch_shapes=[pltpu.VMEM((64, 128), F32)],
+        ),
         out_shape=outs,
-        scratch_shapes=[pltpu.VMEM((64, 128), F32)],
         compiler_params=pltpu.CompilerParams(vmem_limit_bytes=24 * 1024 * 1024),
         cost_estimate=cost(0, 8 * 1024 * 1024),
         name="finish_rest",
@@ -660,8 +694,8 @@
 
     u0 = [0, "y"] + list(range(1, up_dims))
     u1 = ["y", 1, 0] + list(range(2, up_dims))
-    q0 = [0, "y", 1, 2] + list(range(3, up_dims))
-    q1 = ["y", 0, 2, 1] + list(range(3, up_dims))
+    q0 = ["y", 1, 0, 2] + list(range(3, up_dims))
+    q1 = [0, "y", 1, 2] + list(range(3, up_dims))
     at = jnp.stack(
         [core, bit(0), by_core(0, bit(u1[1]))]
         + [by_core(bit(u0[0]), bit(u1[1])), by_core(bit(u0[2]), bit(u1[2]))]
@@ -689,7 +723,7 @@
     columns = jnp.stack([ln1_gain, ln1_bias], axis=1).astype(F32)
 
     w_send = swap(fetch(1 - core_s, up_weight, down_weight, bias), "y")
-    joined, ctx, resid, h2, n1t = attn_fwd(tokens, segment_ids, vecs, qkv_weight, out_weight, rows=512)
+    joined, ctx, resid, h2, n1t, probs = attn_fwd(tokens, segment_ids, vecs, qkv_weight, out_weight, rows=512)
     gated_own, dh2_own, own_keep, own_send, gub_own = ffn_own(
         core_s, hbm(h2), out_grad, up_weight, vecs, down_weight, rows=512
     )
@@ -718,7 +752,7 @@
     u_keep, u_send = on_chip(split_body, [block] * 2, at, own_keep, own_recv, oth_keep, oth_recv, name="split")
     u_recv = swap(u_send, u0[0], u1[0])
     dj, q_keep, q_send = attn_bwd(
-        place, hbm(joined), hbm(after(dctx, u_keep)), segment_ids, hbm(n1t), qkv_weight, hbm(gout), gub_own, gub_oth, vec,
+        place, hbm(joined), hbm(after(dctx, u_keep)), hbm(probs), hbm(n1t), qkv_weight, hbm(gout), gub_own, gub_oth, vec,
         rows=512,
     )
     q_recv = swap(q_send, "core")
@@ -758,10 +792,7 @@
     layer_out = layer_out_part(blocks // 2, blocks // 2, layer_out, q_four)
     u_far = after(u_far, layer_out)
     u_far_c = swap(u_far, "core")
-    grad_up, grad_down = on_chip(
-        finish_ffn_body, [shape((d, 2 * half), F32), shape((2 * half, d), F32)], at,
-        u_pair, u_far, u_pair_c, u_far_c, name="finish_ffn",
-    )
+    grad_up, grad_down = finish_ffn(at, u_pair, u_far, u_pair_c, u_far_c)
     q_far = after(q_far, grad_up)
     grad_qkv, grad_qv, grad_wo, g1, c1, bo, g2, c2, gub, b2 = finish_rest(
         at, columns, q_four, q_far, q_four_c, swap(q_far, "core")

time: 164 us -> 161 us (0.982)
  starting transfers between devices: 31.4 us -> 23.7 us
  waiting for transfers between devices: 20.7 us -> 26.9 us
  Pallas kernels: 108 us -> 106 us
    ppermute x22, starting transfers between devices: 31.4 us -> 23.7 us  [swap(): return lax.ppermute(value, BOTH, pairs)]
    ppermute x22, waiting for transfers between devices: 20.7 us -> 26.9 us  [swap(): return lax.ppermute(value, BOTH, pairs)]
    pallas_call x7 -> x6, Pallas kernels: 8.83 us -> 5.44 us  [on_chip(): pl.pallas_call(body, in_specs=[pl.BlockSpec(memory_space=pltpu.SMEM)] + [...]
    pallas_call x1 -> x2, Pallas kernels: 3.23 us -> 6.05 us  [the longest x1 3.06 us: finish_rest(): pl.pallas_call(finish_rest_body, grid_spec=pltpu.PrefetchScalarGridSpec(n...]
    pallas_call x1, Pallas kernels: 17.5 us -> 15 us  [attn_bwd(): pl.pallas_call(attn_bwd_body, grid_spec=pltpu.PrefetchScalarGridSpec(num_...]
  transfers between devices with their start and end apart: 22 -> 22, of which waited for: 11 -> 12; matrix products, arithmetic and copies ran while one was open for 0% -> 0% of each run, Pallas kernels for 62% -> 62%
where the time goes in v4:
time: 161 us; the launch traced here: 160 us
  Pallas kernels  106 us (66%)
  waiting for transfers between devices  26.9 us (17%)
  starting transfers between devices  23.7 us (15%)
  local copies, waits for them, and re-layouts  2.14 us (1%)
    ppermute x22, waiting for transfers between devices, swap(): return lax.ppermute(value, BOTH, pairs)  26.9 us
    ppermute x22, starting transfers between devices, swap(): return lax.ppermute(value, BOTH, pairs)  23.7 us
    pallas_call x1, Pallas kernels, ffn_other(): pl.pallas_call(ffn_other_body, grid_spec=pltpu.PrefetchScalarGridSpec(num...  23.4 us
    pallas_call x4, Pallas kernels, in_part(): pl.pallas_call(body, grid=(count,), in_specs=[spec(a.shape[1]) for a in s...  22.3 us
    pallas_call x1, Pallas kernels, ffn_own(): pl.pallas_call(ffn_own_body, grid_spec=pltpu.PrefetchScalarGridSpec(num_s...  17.4 us
    pallas_call x1, Pallas kernels, attn_fwd(): pl.pallas_call(attn_fwd_body, grid=(t // rows,), in_specs=[rows_spec(rows...  15.2 us
    pallas_call x1, Pallas kernels, attn_bwd(): pl.pallas_call(attn_bwd_body, grid_spec=pltpu.PrefetchScalarGridSpec(num_...  15 us
    pallas_call x6, Pallas kernels, on_chip(): pl.pallas_call(body, in_specs=[pl.BlockSpec(memory_space=pltpu.SMEM)] + [...  5.44 us
  transfers between devices with their start and end apart: 22, of which 12 were waited for; matrix products, arithmetic and copies ran while one was open for 0% of the time, Pallas kernels for 62%

profile of v4, /device:TPU:0, one launch (start us, length us, event | category | flops | bytes accessed | tf_op | source)
XLA Modules:
  0.0 160.5 jit_solution(8454763349071289698)
XLA Ops:
  1.5 1.3 fetch.1
  2.7 3.0 %collective-permute-start = (bf16[1040,512]{1,0:T(8,128)(2,1)S(1)}, bf16[1040,512]{1,0:T(8,128)(2,1)}, u32[]{:S(2)}, u32[]{:S(2)}) collective-permute-start(bf16[1040,512]{1,0:T(8,128)(2,1)S(1)} %fetch.1), channel_id=1, source_target_pairs={{0,1},{1,0},{2,3},{3,2},{4,5},{5,4},{6,7},{7,6},{8,9},{9,8},{10,11... | collective-permute-start | bytes 3194888 | tf_op jit(solution)/shard_map/ppermute | solution.py:687
  6.0 15.2 %attn_fwd.1 = (bf16[2048,1536]{1,0:T(8,128)(2,1)}, bf16[2048,512]{1,0:T(8,128)(2,1)}, f32[2048,512]{1,0:T(8,128)}, bf16[2048,512]{1,0:T(8,128)(2,1)}, bf16[512,2...) custom-call(bf16[2048,512]{1,0:T(8,128)(2,1)} %tok.5, s32[4,4,128]{2,1,0:T(4,128)S(1)} %bitcast.18, ...), custom_call_target="tpu_custom_call" | custom-call | flops 51539607552 | bytes 1 | tf_op jit(solution)/shard_map/attn_fwd/pallas_call | solution.py:135
  21.2 17.4 %ffn_own.1 = (bf16[2048,1024]{1,0:T(8,128)(2,1)}, f32[2048,512]{1,0:T(8,128)}, bf16[4,256,512]{2,1,0:T(8,128)(2,1)S(1)}, bf16[4,256,512]{2,1,0:T(8,128)(2,1)}, f32[2,512]{1,0:T(2,128)S(1)}) custom-call(s32[1]{0:T(128)} %bitcast.core, bf16[2048,512]{1,0:T(8,128)(2,1)} %get-tuple-element.80.h2, bf16[2048,512]{1,0:T(8,128)(2,1)} %g.3, bf16[512,1024]{1,0:T(8,128)(2,1)} %up.3, ...), custom_call_target="tpu_custom_call" | custom-call | flops 85899345920 | bytes 1 | tf_op jit(solution)/shard_map/ffn_own/pallas_call | solution.py:255
  39.2 2.4 %collective-permute-done.1.w_keep = bf16[1040,512]{1,0:T(8,128)(2,1)S(1)} collective-permute-done((bf16[1040,512]{1,0:T(8,128)(2,1)}, bf16[1040,512]{1,0:T(8,128)(2,1)S(1)}, u32[]{:S(2)}, u32[]{:S(2)}) %collective-permute-start.1) | collective-permute-done | bytes 1064992 | tf_op jit(solution)/shard_map/ppermute | solution.py:687
  42.6 23.4 %ffn_other.1 = (bf16[2048,1024]{1,0:T(8,128)(2,1)}, bf16[2048,512]{1,0:T(8,128)(2,1)}, bf16[2048,512]{1,0:T(8,128)(2,1)}, bf16[4,256,512]{2,1,0:T(8,128)(2,1)S(1...) custom-call(bf16[2048,512]{1,0:T(8,128)(2,1)} %get-tuple-element.80.h2, ...), custom_call_target="tpu_custom_call" | custom-call | flops 103079215104 | bytes 1 | tf_op jit(solution)/shard_map/ffn_other/pallas_call | solution.py:315
  66.3 2.7 %collective-permute-done.3.oth_b = bf16[4,256,512]{2,1,0:T(8,128)(2,1)} collective-permute-done((bf16[4,256,512]{2,1,0:T(8,128)(2,1)}, bf16[4,256,512]{2,1,0:T(8,128)(2,1)}, u32[]{:S(2)}, u32[]{:S(2)}) %collective-permute-start.3) | collective-permute-done | bytes 1048608 | tf_op jit(solution)/shard_map/ppermute | solution.py:687
  69.0 1.9 %split.1 = (bf16[4,256,512]{2,1,0:T(8,128)(2,1)S(1)}, bf16[4,256,512]{2,1,0:T(8,128)(2,1)S(1)}) custom-call(s32[14]{0:T(128)S(1)} %stack.82.at, bf16[4,256,512]{2,1,0:T(8,128)(2,1)S(1)} %get-tuple-element.89.own_a, bf16[4,256,512]{2,1,0:T(8,128)(2,1)S(1)} %collective-permute-done.2.own_b, bf16[4,256,512]{2,1,0:T(8,128)(2,1)S(1)} %get-tuple-element.90.oth_a, ...), custom_call_target="tpu_custom_call" | custom-call | bytes 1 | tf_op jit(solution)/shard_map/split/pallas_call | solution.py:484
  70.9 1.6 collective-permute-start.5
  72.5 15.0 %attn_bwd.1 = (bf16[2048,1536]{1,0:T(8,128)(2,1)S(1)}, bf16[8,32,2176]{2,1,0:T(8,128)(2,1)S(1)}, bf16[8,32,2176]{2,1,0:T(8,128)(2,1)S(1)}) custom-call(s32[2]{0:T(128)S(1)} %pad_add_fusion.place, bf16[2048,1536]{1,0:T(8,128)(2,1)} %get-tuple-element.83.joined, bf16[2048,512]{1,0:T(8,128)(2,1)} %get-tuple-element.93.dc, ...), custom_call_target="tpu_custom_call" | custom-call | flops 103079215104 | bytes 1 | tf_op jit(solution)/shard_map/attn_bwd/pallas_call | solution.py:427
  89.0 4.7 %in_grad.2.refs_0_ = bf16[2048,512]{1,0:T(8,128)(2,1)} custom-call(bf16[2048,1536]{1,0:T(8,128)(2,1)S(1)} %get-tuple-element.102.dj, bf16[2048,512]{1,0:T(8,128)(2,1)} %tok.5, bf16[2048,512]{1,0:T(8,128)(2,1)} %get-tuple-element.112.dattn, bf16[512,1536]{1,0:T(8,128)(2,1)S(1)} %copy-done, bf16[16,512]{1,0:T(8,128)(2,1)S(1)} %concatenate.13.vecs), custom_call_target="tpu_custom_call" | custom-call | flops 12884901888 | bytes 1 | tf_op jit(solution)/shard_map/in_grad/pallas_call | solution.py:460
  94.5 1.6 collective-permute-start.6
  96.1 4.7 %in_grad.3 = bf16[2048,512]{1,0:T(8,128)(2,1)} custom-call(bf16[2048,1536]{1,0:T(8,128)(2,1)S(1)} %get-tuple-element.102.dj, bf16[2048,512]{1,0:T(8,128)(2,1)} %tok.5, bf16[2048,512]{1,0:T(8,128)(2,1)} %get-tuple-element.112.dattn, bf16[512,1536]{1,0:T(8,128)(2,1)S(1)} %copy-done, ...), custom_call_target="tpu_custom_call", output_to_operand_aliasing={{}: (5, {})} | custom-call | flops 12884901888 | bytes 1 | tf_op jit(solution)/shard_map/in_grad/pallas_call | solution.py:460
  101.5 1.6 %collective-permute-start.9 = (bf16[1,256,512]{2,1,0:T(8,128)(2,1)S(1)}, bf16[1,256,512]{2,1,0:T(8,128)(2,1)S(1)}, u32[]{:S(2)}, u32[]{:S(2)}) collective-permute-start(bf16[1,256,512]{2,1,0:T(8,128)(2,1)S(1)} %get-tuple-element.118), channel_id=1, source_target_pairs={{0,8},{1,9},{2,6},{3,7},{4,12},{5,13},{6,2},{7,3},{8,0},{9,1},{10,... | collective-permute-start | bytes 786440 | tf_op jit(solution)/shard_map/ppermute | solution.py:687
  104.8 1.6 %collective-permute-start.8 = (bf16[2,32,2176]{2,1,0:T(8,128)(2,1)S(1)}, bf16[2,32,2176]{2,1,0:T(8,128)(2,1)S(1)}, u32[]{:S(2)}, u32[]{:S(2)}) collective-permute-start(bf16[2,32,2176]{2,1,0:T(8,128)(2,1)S(1)} %get-tuple-element.117), channel_id=1, source_target_pairs={{0,8},{1,9},{2,3},{3,2},{4,12},{5,13},{6,7},{7,6},{8,0},{9,1},{10,... | collective-permute-start | bytes 835592 | tf_op jit(solution)/shard_map/ppermute | solution.py:687
  106.4 1.5 collective-permute-done.9
  108.0 2.7 %collective-permute-start.12 = (bf16[1,256,512]{2,1,0:T(8,128)(2,1)S(1)}, bf16[1,256,512]{2,1,0:T(8,128)(2,1)S(1)}, u32[]{:S(2)}, u32[]{:S(2)}) collective-permute-start(bf16[1,256,512]{2,1,0:T(8,128)(2,1)S(1)} %add_convert_fusion.1), channel_id=1, source_target_pairs={{0,16},{1,17},{2,18},{3,19},{4,20},{5,21},{6,22},{7,23},{8,24},{9,... | collective-permute-start | bytes 786440 | tf_op jit(solution)/shard_map/ppermute | solution.py:687
  110.6 1.2 collective-permute-done.8.b
  112.5 1.7 %collective-permute-start.10 = (bf16[1,32,2176]{2,1,0:T(8,128)(2,1)S(1)}, bf16[1,32,2176]{2,1,0:T(8,128)(2,1)S(1)}, u32[]{:S(2)}, u32[]{:S(2)}) collective-permute-start(bf16[1,32,2176]{2,1,0:T(8,128)(2,1)S(1)} %get-tuple-element.122), channel_id=1, source_target_pairs={{0,4},{1,5},{2,10},{3,11},{4,0},{5,1},{6,14},{7,15},{8,12},{9,13},... | collective-permute-start | bytes 417800 | tf_op jit(solution)/shard_map/ppermute | solution.py:687
  114.1 6.4 %layer_out.2.refs_0_ = bf16[2048,512]{1,0:T(8,128)(2,1)} custom-call(bf16[2048,1024]{1,0:T(8,128)(2,1)} %get-tuple-element.81.own, f32[2048,512]{1,0:T(8,128)} %get-tuple-element.131.resid, bf16[2048,1024]{1,0:T(8,128)(2,1)} %get-tuple-element.124.oth, bf16[1024,512]{1,0:T(8,128)(2,1)} %down.7, bf16[1040,512]{1,0:T(8,128)(2,1)} %collective-permute-done.w_send, ...), custom_call_target="tpu_custom_call" | custom-call | flops 17179869184 | bytes 1 | tf_op jit(solution)/shard_map/layer_out/pallas_call | solution.py:460
  120.6 4.8 %collective-permute-start.11 = (bf16[1,32,2176]{2,1,0:T(8,128)(2,1)S(1)}, bf16[1,32,2176]{2,1,0:T(8,128)(2,1)S(1)}, u32[]{:S(2)}, u32[]{:S(2)}) collective-permute-start(bf16[1,32,2176]{2,1,0:T(8,128)(2,1)S(1)} %add_convert_fusion.3), channel_id=1, source_target_pairs={{0,16},{1,17},{2,18},{3,19},{4,20},{5,21},{6,22},{7,23},{8,24},{9,... | collective-permute-start | bytes 417800 | tf_op jit(solution)/shard_map/ppermute | solution.py:687
  125.5 1.1 collective-permute-start.14
  126.6 3.5 %collective-permute-done.11 = bf16[1,32,2176]{2,1,0:T(8,128)(2,1)S(1)} collective-permute-done((bf16[1,32,2176]{2,1,0:T(8,128)(2,1)S(1)}, bf16[1,32,2176]{2,1,0:T(8,128)(2,1)S(1)}, u32[]{:S(2)}, u32[]{:S(2)}) %collective-permute-start.11) | collective-permute-done | bytes 139296 | tf_op jit(solution)/shard_map/ppermute | solution.py:687
  130.6 2.2 %collective-permute-done.14 = bf16[1,256,512]{2,1,0:T(8,128)(2,1)S(1)} collective-permute-done((bf16[1,256,512]{2,1,0:T(8,128)(2,1)S(1)}, bf16[1,256,512]{2,1,0:T(8,128)(2,1)S(1)}, u32[]{:S(2)}, u32[]{:S(2)}) %collective-permute-start.14) | collective-permute-done | bytes 262176 | tf_op jit(solution)/shard_map/ppermute | solution.py:687
  132.9 2.3 %collective-permute-done.13 = bf16[1,32,2176]{2,1,0:T(8,128)(2,1)S(1)} collective-permute-done((bf16[1,32,2176]{2,1,0:T(8,128)(2,1)S(1)}, bf16[1,32,2176]{2,1,0:T(8,128)(2,1)S(1)}, u32[]{:S(2)}, u32[]{:S(2)}) %collective-permute-start.13) | collective-permute-done | bytes 139296 | tf_op jit(solution)/shard_map/ppermute | solution.py:687
  135.9 6.0 %collective-permute-done.15 = bf16[2,32,2176]{2,1,0:T(8,128)(2,1)S(1)} collective-permute-done((bf16[2,32,2176]{2,1,0:T(8,128)(2,1)S(1)}, bf16[2,32,2176]{2,1,0:T(8,128)(2,1)S(1)}, u32[]{:S(2)}, u32[]{:S(2)}) %collective-permute-start.15) | collective-permute-done | bytes 278560 | tf_op jit(solution)/shard_map/ppermute | solution.py:687
  142.7 6.5 %layer_out.3 = bf16[2048,512]{1,0:T(8,128)(2,1)} custom-call(bf16[2048,1024]{1,0:T(8,128)(2,1)} %get-tuple-element.81.own, f32[2048,512]{1,0:T(8,128)} %get-tuple-element.131.resid, bf16[2048,1024]{1,0:T(8,128)(2,1)} %get-tuple-element.124.oth, bf16[1024,512]{1,0:T(8,128)(2,1)} %down.7, ...), custom_call_target="tpu_custom_call", output_to_operand_aliasing={{}: (7, {})} | custom-call | flops 17179869184 | bytes 1 | tf_op jit(solution)/shard_map/layer_out/pallas_call | solution.py:460
  149.2 1.2 collective-permute-done.17.refs_1_
  150.9 1.4 collective-permute-done.19.refs_3_
  152.3 3.0 %finish_ffn.1 = (f32[512,1024]{1,0:T(8,128)}, f32[1024,512]{1,0:T(8,128)}) custom-call(s32[14]{0:T(128)S(1)} %stack.82.at, bf16[2,256,512]{2,1,0:T(8,128)(2,1)S(1)} %pad_maximum_fusion.1.refs_0_, bf16[2,256,512]{2,1,0:T(8,128)(2,1)S(1)} %collective-permute-done.17.refs_1_, bf16[2,256,512]{2,1,0:T(8,128)(2,1)S(1)} %collective-permute-done.18.refs_2_, ...), custom_call_target="tpu_custom_call" | custom-call | bytes 1 | tf_op jit(solution)/shard_map/finish_ffn/pallas_call | solution.py:558
  155.6 1.6 %collective-permute-done.21.refs_3_ = bf16[4,32,2176]{2,1,0:T(8,128)(2,1)S(1)} collective-permute-done((bf16[4,32,2176]{2,1,0:T(8,128)(2,1)S(1)}, bf16[4,32,2176]{2,1,0:T(8,128)(2,1)S(1)}, u32[]{:S(2)}, u32[]{:S(2)}) %collective-permute-start.21) | collective-permute-done | bytes 557088 | tf_op jit(solution)/shard_map/ppermute | solution.py:687
  157.3 3.1 %finish_rest.1 = (f32[512,1536]{1,0:T(8,128)}, f32[2,512]{1,0:T(2,128)}, f32[512,512]{1,0:T(8,128)}, f32[1,512]{1,0:T(1,128)}, f32[1,512]{1,0:T(1,128)}, /*index...) custom-call(s32[14]{0:T(128)S(1)} %stack.82.at, ...), custom_call_target="tpu_custom_call" | custom-call | bytes 1 | tf_op jit(solution)/shard_map/finish_rest/pallas_call | solution.py:630
  (75 shorter events, 11.2 us)
Async XLA Ops:
  0.6 5.1 %copy-start.4 = (bf16[512]{0:T(512)(128)(2,1)S(1)}, bf16[512]{0:T(512)(128)(2,1)}, u32[]{:S(2)}) copy-start(bf16[512]{0:T(512)(128)(2,1)} %param.17) | copy-start | bytes 3076
  0.7 5.1 %copy-start.2 = (bf16[512]{0:T(512)(128)(2,1)S(1)}, bf16[512]{0:T(512)(128)(2,1)}, u32[]{:S(2)}) copy-start(bf16[512]{0:T(512)(128)(2,1)} %param.18) | copy-start | bytes 3076
  0.7 5.1 %copy-start.7 = (bf16[512]{0:T(512)(128)(2,1)S(1)}, bf16[512]{0:T(512)(128)(2,1)}, u32[]{:S(2)}) copy-start(bf16[512]{0:T(512)(128)(2,1)} %param.22) | copy-start | bytes 3076
  0.7 5.1 %copy-start.8 = (bf16[512]{0:T(512)(128)(2,1)S(1)}, bf16[512]{0:T(512)(128)(2,1)}, u32[]{:S(2)}) copy-start(bf16[512]{0:T(512)(128)(2,1)} %param.23) | copy-start | bytes 3076
  0.7 5.2 %copy-start.9 = (bf16[512]{0:T(512)(128)(2,1)S(1)}, bf16[512]{0:T(512)(128)(2,1)}, u32[]{:S(2)}) copy-start(bf16[512]{0:T(512)(128)(2,1)} %param.24) | copy-start | bytes 3076
  0.7 5.2 %copy-start.10 = (bf16[512]{0:T(512)(128)(2,1)S(1)}, bf16[512]{0:T(512)(128)(2,1)}, u32[]{:S(2)}) copy-start(bf16[512]{0:T(512)(128)(2,1)} %param.28) | copy-start | bytes 3076
  0.7 5.2 %copy-start.6 = (bf16[2,512]{1,0:T(2,128)(2,1)S(1)}, bf16[2,512]{1,0:T(2,128)(2,1)}, u32[]{:S(2)}) copy-start(bf16[2,512]{1,0:T(2,128)(2,1)} %param.20) | copy-start | bytes 6148
  0.7 5.2 %copy-start.1 = (s32[16,128]{1,0:T(8,128)S(1)}, s32[16,128]{1,0:T(8,128)}, u32[]{:S(2)}) copy-start(s32[16,128]{1,0:T(8,128)} %param.16) | copy-start | bytes 24580
  2.7 35.8 %collective-permute-start = (bf16[1040,512]{1,0:T(8,128)(2,1)S(1)}, bf16[1040,512]{1,0:T(8,128)(2,1)}, u32[]{:S(2)}, u32[]{:S(2)}) collective-permute-start(bf16[1040,512]{1,0:T(8,128)(2,1)S(1)} %fetch.1), channel_id=1, source_target_pairs={{0,1},{1,0},{2,3},{3,2},{4,5},{5,4},{6,7},{7,6},{8,9},{9,8},{10,11... | collective-permute-start | bytes 3194888 | tf_op jit(solution)/shard_map/ppermute | solution.py:687
  38.6 3.0 %collective-permute-start.1 = (bf16[1040,512]{1,0:T(8,128)(2,1)}, bf16[1040,512]{1,0:T(8,128)(2,1)S(1)}, u32[]{:S(2)}, u32[]{:S(2)}) collective-permute-start(bf16[1040,512]{1,0:T(8,128)(2,1)} %collective-permute-done.w_send), channel_id=1, source_target_pairs={{0,2},{1,3},{2,0},{3,1},{4,6},{5,7},{6,4},{7,5},{8,10},{9,11},{10,... | collective-permute-start | bytes 3194888 | tf_op jit(solution)/shard_map/ppermute | solution.py:687
  38.7 27.6 %collective-permute-start.2 = (bf16[4,256,512]{2,1,0:T(8,128)(2,1)}, bf16[4,256,512]{2,1,0:T(8,128)(2,1)S(1)}, u32[]{:S(2)}, u32[]{:S(2)}) collective-permute-start(bf16[4,256,512]{2,1,0:T(8,128)(2,1)} %get-tuple-element.84), channel_id=1, source_target_pairs={{0,2},{1,3},{2,0},{3,1},{4,6},{5,7},{6,4},{7,5},{8,10},{9,11},{10,... | collective-permute-start | bytes 3145736 | tf_op jit(solution)/shard_map/ppermute | solution.py:687
  65.9 3.1 %collective-permute-start.3 = (bf16[4,256,512]{2,1,0:T(8,128)(2,1)}, bf16[4,256,512]{2,1,0:T(8,128)(2,1)}, u32[]{:S(2)}, u32[]{:S(2)}) collective-permute-start(bf16[4,256,512]{2,1,0:T(8,128)(2,1)} %get-tuple-element.91), channel_id=1, source_target_pairs={{0,2},{1,3},{2,0},{3,1},{4,6},{5,7},{6,4},{7,5},{8,10},{9,11},{10,... | collective-permute-start | bytes 3145736 | tf_op jit(solution)/shard_map/ppermute | solution.py:687
  70.9 16.7 %collective-permute-start.5 = (bf16[4,256,512]{2,1,0:T(8,128)(2,1)S(1)}, bf16[4,256,512]{2,1,0:T(8,128)(2,1)S(1)}, u32[]{:S(2)}, u32[]{:S(2)}) collective-permute-start(bf16[4,256,512]{2,1,0:T(8,128)(2,1)S(1)} %get-tuple-element.104), channel_id=1, source_target_pairs={{0,4},{1,5},{2,3},{3,2},{4,0},{5,1},{6,7},{7,6},{8,12},{9,13},{10,... | collective-permute-start | bytes 3145736 | tf_op jit(solution)/shard_map/ppermute | solution.py:687
  87.5 6.2 %collective-permute-start.4 = (bf16[8,32,2176]{2,1,0:T(8,128)(2,1)S(1)}, bf16[8,32,2176]{2,1,0:T(8,128)(2,1)S(1)}, u32[]{:S(2)}, u32[]{:S(2)}) collective-permute-start(bf16[8,32,2176]{2,1,0:T(8,128)(2,1)S(1)} %get-tuple-element.101), channel_id=1, source_target_pairs={{0,2},{1,3},{2,0},{3,1},{4,6},{5,7},{6,4},{7,5},{8,10},{9,11},{10,... | collective-permute-start | bytes 3342344 | tf_op jit(solution)/shard_map/ppermute | solution.py:687
  88.4 12.4 %collective-permute-start.7 = (bf16[2,256,512]{2,1,0:T(8,128)(2,1)S(1)}, bf16[2,256,512]{2,1,0:T(8,128)(2,1)S(1)}, u32[]{:S(2)}, u32[]{:S(2)}) collective-permute-start(bf16[2,256,512]{2,1,0:T(8,128)(2,1)S(1)} %get-tuple-element.111), channel_id=1, source_target_pairs={{0,1},{1,0},{2,10},{3,11},{4,5},{5,4},{6,14},{7,15},{8,9},{9,8},{1... | collective-permute-start | bytes 1572872 | tf_op jit(solution)/shard_map/ppermute | solution.py:687
  94.5 9.6 %collective-permute-start.6 = (bf16[4,32,2176]{2,1,0:T(8,128)(2,1)S(1)}, bf16[4,32,2176]{2,1,0:T(8,128)(2,1)S(1)}, u32[]{:S(2)}, u32[]{:S(2)}) collective-permute-start(bf16[4,32,2176]{2,1,0:T(8,128)(2,1)S(1)} %get-tuple-element.110), channel_id=1, source_target_pairs={{0,1},{1,0},{2,6},{3,7},{4,5},{5,4},{6,2},{7,3},{8,9},{9,8},{10,14... | collective-permute-start | bytes 1671176 | tf_op jit(solution)/shard_map/ppermute | solution.py:687
  101.5 6.4 %collective-permute-start.9 = (bf16[1,256,512]{2,1,0:T(8,128)(2,1)S(1)}, bf16[1,256,512]{2,1,0:T(8,128)(2,1)S(1)}, u32[]{:S(2)}, u32[]{:S(2)}) collective-permute-start(bf16[1,256,512]{2,1,0:T(8,128)(2,1)S(1)} %get-tuple-element.118), channel_id=1, source_target_pairs={{0,8},{1,9},{2,6},{3,7},{4,12},{5,13},{6,2},{7,3},{8,0},{9,1},{10,... | collective-permute-start | bytes 786440 | tf_op jit(solution)/shard_map/ppermute | solution.py:687
  104.8 7.1 %collective-permute-start.8 = (bf16[2,32,2176]{2,1,0:T(8,128)(2,1)S(1)}, bf16[2,32,2176]{2,1,0:T(8,128)(2,1)S(1)}, u32[]{:S(2)}, u32[]{:S(2)}) collective-permute-start(bf16[2,32,2176]{2,1,0:T(8,128)(2,1)S(1)} %get-tuple-element.117), channel_id=1, source_target_pairs={{0,8},{1,9},{2,3},{3,2},{4,12},{5,13},{6,7},{7,6},{8,0},{9,1},{10,... | collective-permute-start | bytes 835592 | tf_op jit(solution)/shard_map/ppermute | solution.py:687
  108.0 17.4 %collective-permute-start.12 = (bf16[1,256,512]{2,1,0:T(8,128)(2,1)S(1)}, bf16[1,256,512]{2,1,0:T(8,128)(2,1)S(1)}, u32[]{:S(2)}, u32[]{:S(2)}) collective-permute-start(bf16[1,256,512]{2,1,0:T(8,128)(2,1)S(1)} %add_convert_fusion.1), channel_id=1, source_target_pairs={{0,16},{1,17},{2,18},{3,19},{4,20},{5,21},{6,22},{7,23},{8,24},{9,... | collective-permute-start | bytes 786440 | tf_op jit(solution)/shard_map/ppermute | solution.py:687
  112.5 8.1 %collective-permute-start.10 = (bf16[1,32,2176]{2,1,0:T(8,128)(2,1)S(1)}, bf16[1,32,2176]{2,1,0:T(8,128)(2,1)S(1)}, u32[]{:S(2)}, u32[]{:S(2)}) collective-permute-start(bf16[1,32,2176]{2,1,0:T(8,128)(2,1)S(1)} %get-tuple-element.122), channel_id=1, source_target_pairs={{0,4},{1,5},{2,10},{3,11},{4,0},{5,1},{6,14},{7,15},{8,12},{9,13},... | collective-permute-start | bytes 417800 | tf_op jit(solution)/shard_map/ppermute | solution.py:687
  120.6 9.4 %collective-permute-start.11 = (bf16[1,32,2176]{2,1,0:T(8,128)(2,1)S(1)}, bf16[1,32,2176]{2,1,0:T(8,128)(2,1)S(1)}, u32[]{:S(2)}, u32[]{:S(2)}) collective-permute-start(bf16[1,32,2176]{2,1,0:T(8,128)(2,1)S(1)} %add_convert_fusion.3), channel_id=1, source_target_pairs={{0,16},{1,17},{2,18},{3,19},{4,20},{5,21},{6,22},{7,23},{8,24},{9,... | collective-permute-start | bytes 417800 | tf_op jit(solution)/shard_map/ppermute | solution.py:687
  125.5 7.3 %collective-permute-start.14 = (bf16[1,256,512]{2,1,0:T(8,128)(2,1)S(1)}, bf16[1,256,512]{2,1,0:T(8,128)(2,1)S(1)}, u32[]{:S(2)}, u32[]{:S(2)}) collective-permute-start(bf16[1,256,512]{2,1,0:T(8,128)(2,1)S(1)} %add_convert_fusion), channel_id=1, source_target_pairs={{0,8},{1,9},{2,6},{3,7},{4,12},{5,13},{6,2},{7,3},{8,0},{9,1},{10,... | collective-permute-start | bytes 786440 | tf_op jit(solution)/shard_map/ppermute | solution.py:687
  130.1 5.1 %collective-permute-start.13 = (bf16[1,32,2176]{2,1,0:T(8,128)(2,1)S(1)}, bf16[1,32,2176]{2,1,0:T(8,128)(2,1)S(1)}, u32[]{:S(2)}, u32[]{:S(2)}) collective-permute-start(bf16[1,32,2176]{2,1,0:T(8,128)(2,1)S(1)} %add_convert_fusion.2), channel_id=1, source_target_pairs={{0,4},{1,5},{2,10},{3,11},{4,0},{5,1},{6,14},{7,15},{8,12},{9,13},... | collective-permute-start | bytes 417800 | tf_op jit(solution)/shard_map/ppermute | solution.py:687
  135.2 6.6 %collective-permute-start.15 = (bf16[2,32,2176]{2,1,0:T(8,128)(2,1)S(1)}, bf16[2,32,2176]{2,1,0:T(8,128)(2,1)S(1)}, u32[]{:S(2)}, u32[]{:S(2)}) collective-permute-start(bf16[2,32,2176]{2,1,0:T(8,128)(2,1)S(1)} %pad_maximum_fusion.2), channel_id=1, source_target_pairs={{0,8},{1,9},{2,3},{3,2},{4,12},{5,13},{6,7},{7,6},{8,0},{9,1},{10,... | collective-permute-start | bytes 835592 | tf_op jit(solution)/shard_map/ppermute | solution.py:687
  135.8 14.6 %collective-permute-start.17 = (bf16[2,256,512]{2,1,0:T(8,128)(2,1)S(1)}, bf16[2,256,512]{2,1,0:T(8,128)(2,1)S(1)}, u32[]{:S(2)}, u32[]{:S(2)}) collective-permute-start(bf16[2,256,512]{2,1,0:T(8,128)(2,1)S(1)} %pad_maximum_fusion.1.refs_0_), channel_id=1, source_target_pairs={{0,4},{1,5},{2,10},{3,11},{4,0},{5,1},{6,14},{7,15},{8,12},{9,13},... | collective-permute-start | bytes 1572872 | tf_op jit(solution)/shard_map/ppermute | solution.py:687
  135.9 15.0 %collective-permute-start.18 = (bf16[2,256,512]{2,1,0:T(8,128)(2,1)S(1)}, bf16[2,256,512]{2,1,0:T(8,128)(2,1)S(1)}, u32[]{:S(2)}, u32[]{:S(2)}) collective-permute-start(bf16[2,256,512]{2,1,0:T(8,128)(2,1)S(1)} %pad_maximum_fusion.1.refs_0_), channel_id=1, source_target_pairs={{0,2},{1,3},{2,0},{3,1},{4,6},{5,7},{6,4},{7,5},{8,10},{9,11},{10,... | collective-permute-start | bytes 1572872 | tf_op jit(solution)/shard_map/ppermute | solution.py:687
  141.9 13.4 %collective-permute-start.16 = (bf16[4,32,2176]{2,1,0:T(8,128)(2,1)S(1)}, bf16[4,32,2176]{2,1,0:T(8,128)(2,1)S(1)}, u32[]{:S(2)}, u32[]{:S(2)}) collective-permute-start(bf16[4,32,2176]{2,1,0:T(8,128)(2,1)S(1)} %pad_maximum_fusion.refs_0_), channel_id=1, source_target_pairs={{0,1},{1,0},{2,6},{3,7},{4,5},{5,4},{6,2},{7,3},{8,9},{9,8},{10,14... | collective-permute-start | bytes 1671176 | tf_op jit(solution)/shard_map/ppermute | solution.py:687
  149.2 6.2 %copy-start.3 = (bf16[512]{0:T(512)(128)(2,1)S(1)}, bf16[512]{0:T(512)(128)(2,1)}, u32[]{:S(2)}) copy-start(bf16[512]{0:T(512)(128)(2,1)} %param.18) | copy-start | bytes 3076
  149.2 6.2 %copy-start.5 = (bf16[512]{0:T(512)(128)(2,1)S(1)}, bf16[512]{0:T(512)(128)(2,1)}, u32[]{:S(2)}) copy-start(bf16[512]{0:T(512)(128)(2,1)} %param.17) | copy-start | bytes 3076
  150.4 1.9 %collective-permute-start.19 = (bf16[2,256,512]{2,1,0:T(8,128)(2,1)S(1)}, bf16[2,256,512]{2,1,0:T(8,128)(2,1)S(1)}, u32[]{:S(2)}, u32[]{:S(2)}) collective-permute-start(bf16[2,256,512]{2,1,0:T(8,128)(2,1)S(1)} %collective-permute-done.17.refs_1_), channel_id=1, source_target_pairs={{0,2},{1,3},{2,0},{3,1},{4,6},{5,7},{6,4},{7,5},{8,10},{9,11},{10,... | collective-permute-start | bytes 1572872 | tf_op jit(solution)/shard_map/ppermute | solution.py:687
  150.4 5.2 %collective-permute-start.20 = (bf16[4,32,2176]{2,1,0:T(8,128)(2,1)S(1)}, bf16[4,32,2176]{2,1,0:T(8,128)(2,1)S(1)}, u32[]{:S(2)}, u32[]{:S(2)}) collective-permute-start(bf16[4,32,2176]{2,1,0:T(8,128)(2,1)S(1)} %pad_maximum_fusion.refs_0_), channel_id=1, source_target_pairs={{0,2},{1,3},{2,0},{3,1},{4,6},{5,7},{6,4},{7,5},{8,10},{9,11},{10,... | collective-permute-start | bytes 1671176 | tf_op jit(solution)/shard_map/ppermute | solution.py:687
  155.3 2.0 %collective-permute-start.21 = (bf16[4,32,2176]{2,1,0:T(8,128)(2,1)S(1)}, bf16[4,32,2176]{2,1,0:T(8,128)(2,1)S(1)}, u32[]{:S(2)}, u32[]{:S(2)}) collective-permute-start(bf16[4,32,2176]{2,1,0:T(8,128)(2,1)S(1)} %collective-permute-done.16.refs_1_), channel_id=1, source_target_pairs={{0,2},{1,3},{2,0},{3,1},{4,6},{5,7},{6,4},{7,5},{8,10},{9,11},{10,... | collective-permute-start | bytes 1671176 | tf_op jit(solution)/shard_map/ppermute | solution.py:687
  (2 other events, 2.5 us)

commit v5 on v4

--- a/solution.py
+++ b/solution.py
@@ -138,7 +138,7 @@
         in_specs=[rows_spec(rows, d), pl.BlockSpec((1, rows // SEQ, SEQ), lambda i: (i, 0, 0))]
         + [once(a) for a in (vecs, wqkv, wo)],
         out_specs=[rows_spec(rows, w) for w in (3 * d, d, d, d)] + [pl.BlockSpec((d, rows), lambda i: (0, i)), rows_spec(rows, 2 * d)],
-        out_shape=[in_hbm((t, 3 * d), BF), in_hbm((t, d), BF), in_hbm((t, d), F32), in_hbm((t, d), BF), in_hbm((d, t), BF), in_hbm((t, 2 * d), BF)],
+        out_shape=[in_hbm((t, 3 * d), BF), in_hbm((t, d), BF), in_hbm((t, d), F32), pltpu.VMEM((t, d), BF), in_hbm((d, t), BF), in_hbm((t, 2 * d), BF)],
         compiler_params=pltpu.CompilerParams(vmem_limit_bytes=LIMIT),
         cost_estimate=cost(3 * t * d * 4 * d),
         name="attn_fwd",
@@ -251,7 +251,7 @@
     t, d = h2.shape
     f = up.shape[1]
     half = f // 2
-    outs = [in_hbm((t, f), BF), in_hbm((t, d), F32)] + [shape((4, d // 2, half), BF)] * 2 + [shape((2, half), F32)]
+    outs = [in_hbm((t, f), BF), pltpu.VMEM((t, d), F32)] + [shape((4, d // 2, half), BF)] * 2 + [shape((2, half), F32)]
     return pl.pallas_call(
         ffn_own_body,
         grid_spec=pltpu.PrefetchScalarGridSpec(
@@ -357,11 +357,15 @@
 
 
 def ln1_parts(acc, cs, w):
-    ones = jnp.ones((8, w.shape[1]), BF)
-    gain = mm(ones, (acc * w.astype(F32)).astype(BF), 1, 1)[0:1]
-    hi = cs.astype(BF)
-    lo = (cs - hi.astype(F32)).astype(BF)
-    return gain, jnp.sum(mm(hi, w, 1, 1) + mm(lo, w, 1, 1), axis=0, keepdims=True)
+    def parts(v):
+        hi = v.astype(BF)
+        return hi, (v - hi.astype(F32)).astype(BF)
+
+    narrow = sum(acc[:, j : j + 128] * w[:, j : j + 128].astype(F32) for j in range(0, w.shape[1], 128))
+    ones = jnp.ones((16, 128), BF)
+    gain = sum(mm(ones, v, 1, 1) for v in parts(narrow))[0:1]
+    bias = mm(jnp.concatenate(parts(cs), axis=0), w, 1, 1)
+    return gain, jnp.sum(bias, axis=0, keepdims=True)
 
 
 def attn_bwd_body(place, joined, dc, probs, n1t, wqkv, gout, gub_own, gub_oth, vec, dj_o, keep_o, send_o, acc, cs, small):
@@ -707,6 +711,7 @@
     place = jnp.stack([y, core]).astype(jnp.int32)
     core_s = core.reshape(1).astype(jnp.int32)
     hbm = lambda v: pltpu.with_memory_space_constraint(v, pltpu.HBM)
+    vmem = lambda v: pltpu.with_memory_space_constraint(v, pltpu.VMEM)
     qkv_free, down_free = qkv_weight, down_weight
     tokens, out_grad, qkv_weight, out_weight, up_weight, down_weight = map(
         hbm, (tokens, out_grad, qkv_weight, out_weight, up_weight, down_weight)
@@ -725,13 +730,13 @@
     w_send = swap(fetch(1 - core_s, up_weight, down_weight, bias), "y")
     joined, ctx, resid, h2, n1t, probs = attn_fwd(tokens, segment_ids, vecs, qkv_weight, out_weight, rows=512)
     gated_own, dh2_own, own_keep, own_send, gub_own = ffn_own(
-        core_s, hbm(h2), out_grad, up_weight, vecs, down_weight, rows=512
+        core_s, vmem(h2), out_grad, up_weight, vecs, down_weight, rows=512
     )
     w_send = hbm(after(w_send, own_send))
     w_keep = swap(w_send, "core")
     own_recv = swap(own_send, "core")
     gated_oth, dattn, dctx, oth_keep, oth_send, gub_oth, gout, vec = ffn_other(
-        hbm(h2), out_grad, w_send, w_keep, hbm(dh2_own), hbm(resid), hbm(ctx), out_weight, vecs, rows=512
+        vmem(h2), out_grad, w_send, w_keep, vmem(dh2_own), hbm(resid), hbm(ctx), out_weight, vecs, rows=512
     )
     oth_recv = swap(oth_send, "core")
     blocks = t // 512

time: 161 us -> 160 us (level)
  transfers between devices with their start and end apart: 22 -> 22, of which waited for: 12 -> 11; matrix products, arithmetic and copies ran while one was open for 0% -> 0% of each run, Pallas kernels for 62% -> 62%
where the time goes in v5:
time: 160 us; the launch traced here: 159 us
  Pallas kernels  105 us (66%)
  waiting for transfers between devices  26 us (16%)
  starting transfers between devices  24.3 us (15%)
  local copies, waits for them, and re-layouts  2.09 us (1%)
    ppermute x22, waiting for transfers between devices, swap(): return lax.ppermute(value, BOTH, pairs)  26 us
    ppermute x22, starting transfers between devices, swap(): return lax.ppermute(value, BOTH, pairs)  24.3 us
    pallas_call x1, Pallas kernels, ffn_other(): pl.pallas_call(ffn_other_body, grid_spec=pltpu.PrefetchScalarGridSpec(num...  23.2 us
    pallas_call x4, Pallas kernels, in_part(): pl.pallas_call(body, grid=(count,), in_specs=[spec(a.shape[1]) for a in s...  22.3 us
    pallas_call x1, Pallas kernels, ffn_own(): pl.pallas_call(ffn_own_body, grid_spec=pltpu.PrefetchScalarGridSpec(num_s...  17.2 us
    pallas_call x1, Pallas kernels, attn_fwd(): pl.pallas_call(attn_fwd_body, grid=(t // rows,), in_specs=[rows_spec(rows...  15.1 us
    pallas_call x1, Pallas kernels, attn_bwd(): pl.pallas_call(attn_bwd_body, grid_spec=pltpu.PrefetchScalarGridSpec(num_...  14.6 us
    pallas_call x6, Pallas kernels, on_chip(): pl.pallas_call(body, in_specs=[pl.BlockSpec(memory_space=pltpu.SMEM)] + [...  5.44 us
  transfers between devices with their start and end apart: 22, of which 11 were waited for; matrix products, arithmetic and copies ran while one was open for 0% of the time, Pallas kernels for 62%

profile of v5, /device:TPU:0, one launch (start us, length us, event | category | flops | bytes accessed | tf_op | source)
XLA Modules:
  0.0 159.2 jit_solution(13516655243750223001)
XLA Ops:
  1.5 1.3 fetch.1
  2.7 3.0 %collective-permute-start = (bf16[1040,512]{1,0:T(8,128)(2,1)S(1)}, bf16[1040,512]{1,0:T(8,128)(2,1)}, u32[]{:S(2)}, u32[]{:S(2)}) collective-permute-start(bf16[1040,512]{1,0:T(8,128)(2,1)S(1)} %fetch.1), channel_id=1, source_target_pairs={{0,1},{1,0},{2,3},{3,2},{4,5},{5,4},{6,7},{7,6},{8,9},{9,8},{10,11... | collective-permute-start | bytes 3194888 | tf_op jit(solution)/shard_map/ppermute | solution.py:691
  6.0 15.1 %attn_fwd.1 = (bf16[2048,1536]{1,0:T(8,128)(2,1)}, bf16[2048,512]{1,0:T(8,128)(2,1)}, f32[2048,512]{1,0:T(8,128)}, bf16[2048,512]{1,0:T(8,128)(2,1)S(1)}, bf16[5...) custom-call(bf16[2048,512]{1,0:T(8,128)(2,1)} %tok.5, s32[4,4,128]{2,1,0:T(4,128)S(1)} %bitcast.18, ...), custom_call_target="tpu_custom_call" | custom-call | flops 51539607552 | bytes 1 | tf_op jit(solution)/shard_map/attn_fwd/pallas_call | solution.py:135
  21.0 17.2 %ffn_own.1 = (bf16[2048,1024]{1,0:T(8,128)(2,1)}, f32[2048,512]{1,0:T(8,128)S(1)}, bf16[4,256,512]{2,1,0:T(8,128)(2,1)S(1)}, bf16[4,256,512]{2,1,0:T(8,128)(2,1)}, f32[2,512]{1,0:T(2,128)S(1)}) custom-call(s32[1]{0:T(128)} %bitcast.core, bf16[2048,512]{1,0:T(8,128)(2,1)S(1)} %get-tuple-element.80.h2, bf16[2048,512]{1,0:T(8,128)(2,1)} %g.3, ...), custom_call_target="tpu_custom_call" | custom-call | flops 85899345920 | bytes 1 | tf_op jit(solution)/shard_map/ffn_own/pallas_call | solution.py:255
  38.8 2.4 %collective-permute-done.1.w_keep = bf16[1040,512]{1,0:T(8,128)(2,1)S(1)} collective-permute-done((bf16[1040,512]{1,0:T(8,128)(2,1)}, bf16[1040,512]{1,0:T(8,128)(2,1)S(1)}, u32[]{:S(2)}, u32[]{:S(2)}) %collective-permute-start.1) | collective-permute-done | bytes 1064992 | tf_op jit(solution)/shard_map/ppermute | solution.py:691
  42.1 23.2 %ffn_other.1 = (bf16[2048,1024]{1,0:T(8,128)(2,1)}, bf16[2048,512]{1,0:T(8,128)(2,1)}, bf16[2048,512]{1,0:T(8,128)(2,1)}, bf16[4,256,512]{2,1,0:T(8,128)(2,1)S(1...) custom-call(bf16[2048,512]{1,0:T(8,128)(2,1)S(1)} %get-tuple-element.8, ...), custom_call_target="tpu_custom_call" | custom-call | flops 103079215104 | bytes 1 | tf_op jit(solution)/shard_map/ffn_other/pallas_call | solution.py:315
  65.8 2.7 %collective-permute-done.3.oth_b = bf16[4,256,512]{2,1,0:T(8,128)(2,1)} collective-permute-done((bf16[4,256,512]{2,1,0:T(8,128)(2,1)}, bf16[4,256,512]{2,1,0:T(8,128)(2,1)}, u32[]{:S(2)}, u32[]{:S(2)}) %collective-permute-start.3) | collective-permute-done | bytes 1048608 | tf_op jit(solution)/shard_map/ppermute | solution.py:691
  68.5 1.9 %split.1 = (bf16[4,256,512]{2,1,0:T(8,128)(2,1)S(1)}, bf16[4,256,512]{2,1,0:T(8,128)(2,1)S(1)}) custom-call(s32[14]{0:T(128)S(1)} %stack.82.at, bf16[4,256,512]{2,1,0:T(8,128)(2,1)S(1)} %get-tuple-element.89.own_a, bf16[4,256,512]{2,1,0:T(8,128)(2,1)S(1)} %collective-permute-done.2.own_b, bf16[4,256,512]{2,1,0:T(8,128)(2,1)S(1)} %get-tuple-element.90.oth_a, ...), custom_call_target="tpu_custom_call" | custom-call | bytes 1 | tf_op jit(solution)/shard_map/split/pallas_call | solution.py:488
  70.4 1.6 collective-permute-start.5
  71.9 14.6 %attn_bwd.1 = (bf16[2048,1536]{1,0:T(8,128)(2,1)S(1)}, bf16[8,32,2176]{2,1,0:T(8,128)(2,1)S(1)}, bf16[8,32,2176]{2,1,0:T(8,128)(2,1)S(1)}) custom-call(s32[2]{0:T(128)S(1)} %pad_add_fusion.place, bf16[2048,1536]{1,0:T(8,128)(2,1)} %get-tuple-element.83.joined, bf16[2048,512]{1,0:T(8,128)(2,1)} %get-tuple-element.93.dc, ...), custom_call_target="tpu_custom_call" | custom-call | flops 103079215104 | bytes 1 | tf_op jit(solution)/shard_map/attn_bwd/pallas_call | solution.py:431
  88.0 4.7 %in_grad.2.refs_0_ = bf16[2048,512]{1,0:T(8,128)(2,1)} custom-call(bf16[2048,1536]{1,0:T(8,128)(2,1)S(1)} %get-tuple-element.102.dj, bf16[2048,512]{1,0:T(8,128)(2,1)} %tok.5, bf16[2048,512]{1,0:T(8,128)(2,1)} %get-tuple-element.112.dattn, bf16[512,1536]{1,0:T(8,128)(2,1)S(1)} %copy-done, bf16[16,512]{1,0:T(8,128)(2,1)S(1)} %concatenate.13.vecs), custom_call_target="tpu_custom_call" | custom-call | flops 12884901888 | bytes 1 | tf_op jit(solution)/shard_map/in_grad/pallas_call | solution.py:464
  93.5 1.6 collective-permute-start.6
  95.1 4.7 %in_grad.3 = bf16[2048,512]{1,0:T(8,128)(2,1)} custom-call(bf16[2048,1536]{1,0:T(8,128)(2,1)S(1)} %get-tuple-element.102.dj, bf16[2048,512]{1,0:T(8,128)(2,1)} %tok.5, bf16[2048,512]{1,0:T(8,128)(2,1)} %get-tuple-element.112.dattn, bf16[512,1536]{1,0:T(8,128)(2,1)S(1)} %copy-done, ...), custom_call_target="tpu_custom_call", output_to_operand_aliasing={{}: (5, {})} | custom-call | flops 12884901888 | bytes 1 | tf_op jit(solution)/shard_map/in_grad/pallas_call | solution.py:464
  100.5 1.6 %collective-permute-start.9 = (bf16[1,256,512]{2,1,0:T(8,128)(2,1)S(1)}, bf16[1,256,512]{2,1,0:T(8,128)(2,1)S(1)}, u32[]{:S(2)}, u32[]{:S(2)}) collective-permute-start(bf16[1,256,512]{2,1,0:T(8,128)(2,1)S(1)} %get-tuple-element.118), channel_id=1, source_target_pairs={{0,8},{1,9},{2,6},{3,7},{4,12},{5,13},{6,2},{7,3},{8,0},{9,1},{10,... | collective-permute-start | bytes 786440 | tf_op jit(solution)/shard_map/ppermute | solution.py:691
  103.8 1.6 %collective-permute-start.8 = (bf16[2,32,2176]{2,1,0:T(8,128)(2,1)S(1)}, bf16[2,32,2176]{2,1,0:T(8,128)(2,1)S(1)}, u32[]{:S(2)}, u32[]{:S(2)}) collective-permute-start(bf16[2,32,2176]{2,1,0:T(8,128)(2,1)S(1)} %get-tuple-element.117), channel_id=1, source_target_pairs={{0,8},{1,9},{2,3},{3,2},{4,12},{5,13},{6,7},{7,6},{8,0},{9,1},{10,... | collective-permute-start | bytes 835592 | tf_op jit(solution)/shard_map/ppermute | solution.py:691
  105.5 1.5 collective-permute-done.9
  107.0 2.7 %collective-permute-start.12 = (bf16[1,256,512]{2,1,0:T(8,128)(2,1)S(1)}, bf16[1,256,512]{2,1,0:T(8,128)(2,1)S(1)}, u32[]{:S(2)}, u32[]{:S(2)}) collective-permute-start(bf16[1,256,512]{2,1,0:T(8,128)(2,1)S(1)} %add_convert_fusion.1), channel_id=1, source_target_pairs={{0,16},{1,17},{2,18},{3,19},{4,20},{5,21},{6,22},{7,23},{8,24},{9,... | collective-permute-start | bytes 786440 | tf_op jit(solution)/shard_map/ppermute | solution.py:691
  109.7 1.2 collective-permute-done.8.b
  111.5 1.5 collective-permute-start.10
  113.0 6.4 %layer_out.2.refs_0_ = bf16[2048,512]{1,0:T(8,128)(2,1)} custom-call(bf16[2048,1024]{1,0:T(8,128)(2,1)} %get-tuple-element.81.own, f32[2048,512]{1,0:T(8,128)} %get-tuple-element.131.resid, bf16[2048,1024]{1,0:T(8,128)(2,1)} %get-tuple-element.124.oth, bf16[1024,512]{1,0:T(8,128)(2,1)} %down.7, bf16[1040,512]{1,0:T(8,128)(2,1)} %collective-permute-done.w_send, ...), custom_call_target="tpu_custom_call" | custom-call | flops 17179869184 | bytes 1 | tf_op jit(solution)/shard_map/layer_out/pallas_call | solution.py:464
  119.5 4.8 %collective-permute-start.11 = (bf16[1,32,2176]{2,1,0:T(8,128)(2,1)S(1)}, bf16[1,32,2176]{2,1,0:T(8,128)(2,1)S(1)}, u32[]{:S(2)}, u32[]{:S(2)}) collective-permute-start(bf16[1,32,2176]{2,1,0:T(8,128)(2,1)S(1)} %add_convert_fusion.3), channel_id=1, source_target_pairs={{0,16},{1,17},{2,18},{3,19},{4,20},{5,21},{6,22},{7,23},{8,24},{9,... | collective-permute-start | bytes 417800 | tf_op jit(solution)/shard_map/ppermute | solution.py:691
  124.4 1.0 collective-permute-start.14
  125.4 3.6 %collective-permute-done.11 = bf16[1,32,2176]{2,1,0:T(8,128)(2,1)S(1)} collective-permute-done((bf16[1,32,2176]{2,1,0:T(8,128)(2,1)S(1)}, bf16[1,32,2176]{2,1,0:T(8,128)(2,1)S(1)}, u32[]{:S(2)}, u32[]{:S(2)}) %collective-permute-start.11) | collective-permute-done | bytes 139296 | tf_op jit(solution)/shard_map/ppermute | solution.py:691
  129.5 2.5 %collective-permute-done.14 = bf16[1,256,512]{2,1,0:T(8,128)(2,1)S(1)} collective-permute-done((bf16[1,256,512]{2,1,0:T(8,128)(2,1)S(1)}, bf16[1,256,512]{2,1,0:T(8,128)(2,1)S(1)}, u32[]{:S(2)}, u32[]{:S(2)}) %collective-permute-start.14) | collective-permute-done | bytes 262176 | tf_op jit(solution)/shard_map/ppermute | solution.py:691
  132.0 2.1 %collective-permute-done.13 = bf16[1,32,2176]{2,1,0:T(8,128)(2,1)S(1)} collective-permute-done((bf16[1,32,2176]{2,1,0:T(8,128)(2,1)S(1)}, bf16[1,32,2176]{2,1,0:T(8,128)(2,1)S(1)}, u32[]{:S(2)}, u32[]{:S(2)}) %collective-permute-start.13) | collective-permute-done | bytes 139296 | tf_op jit(solution)/shard_map/ppermute | solution.py:691
  134.7 6.1 %collective-permute-done.15 = bf16[2,32,2176]{2,1,0:T(8,128)(2,1)S(1)} collective-permute-done((bf16[2,32,2176]{2,1,0:T(8,128)(2,1)S(1)}, bf16[2,32,2176]{2,1,0:T(8,128)(2,1)S(1)}, u32[]{:S(2)}, u32[]{:S(2)}) %collective-permute-start.15) | collective-permute-done | bytes 278560 | tf_op jit(solution)/shard_map/ppermute | solution.py:691
  140.9 1.7 %collective-permute-start.16 = (bf16[4,32,2176]{2,1,0:T(8,128)(2,1)S(1)}, bf16[4,32,2176]{2,1,0:T(8,128)(2,1)S(1)}, u32[]{:S(2)}, u32[]{:S(2)}) collective-permute-start(bf16[4,32,2176]{2,1,0:T(8,128)(2,1)S(1)} %pad_maximum_fusion.refs_0_), channel_id=1, source_target_pairs={{0,1},{1,0},{2,6},{3,7},{4,5},{5,4},{6,2},{7,3},{8,9},{9,8},{10,14... | collective-permute-start | bytes 1671176 | tf_op jit(solution)/shard_map/ppermute | solution.py:691
  142.6 6.4 %layer_out.3 = bf16[2048,512]{1,0:T(8,128)(2,1)} custom-call(bf16[2048,1024]{1,0:T(8,128)(2,1)} %get-tuple-element.81.own, f32[2048,512]{1,0:T(8,128)} %get-tuple-element.131.resid, bf16[2048,1024]{1,0:T(8,128)(2,1)} %get-tuple-element.124.oth, bf16[1024,512]{1,0:T(8,128)(2,1)} %down.7, ...), custom_call_target="tpu_custom_call", output_to_operand_aliasing={{}: (7, {})} | custom-call | flops 17179869184 | bytes 1 | tf_op jit(solution)/shard_map/layer_out/pallas_call | solution.py:464
  149.6 1.4 collective-permute-done.19.refs_3_
  151.0 3.0 %finish_ffn.1 = (f32[512,1024]{1,0:T(8,128)}, f32[1024,512]{1,0:T(8,128)}) custom-call(s32[14]{0:T(128)S(1)} %stack.82.at, bf16[2,256,512]{2,1,0:T(8,128)(2,1)S(1)} %pad_maximum_fusion.1.refs_0_, bf16[2,256,512]{2,1,0:T(8,128)(2,1)S(1)} %collective-permute-done.17.refs_1_, bf16[2,256,512]{2,1,0:T(8,128)(2,1)S(1)} %collective-permute-done.18.refs_2_, ...), custom_call_target="tpu_custom_call" | custom-call | bytes 1 | tf_op jit(solution)/shard_map/finish_ffn/pallas_call | solution.py:562
  154.3 1.6 %collective-permute-done.21.refs_3_ = bf16[4,32,2176]{2,1,0:T(8,128)(2,1)S(1)} collective-permute-done((bf16[4,32,2176]{2,1,0:T(8,128)(2,1)S(1)}, bf16[4,32,2176]{2,1,0:T(8,128)(2,1)S(1)}, u32[]{:S(2)}, u32[]{:S(2)}) %collective-permute-start.21) | collective-permute-done | bytes 557088 | tf_op jit(solution)/shard_map/ppermute | solution.py:691
  155.9 3.1 %finish_rest.1 = (f32[512,1536]{1,0:T(8,128)}, f32[2,512]{1,0:T(2,128)}, f32[512,512]{1,0:T(8,128)}, f32[1,512]{1,0:T(1,128)}, f32[1,512]{1,0:T(1,128)}, /*index...) custom-call(s32[14]{0:T(128)S(1)} %stack.82.at, ...), custom_call_target="tpu_custom_call" | custom-call | bytes 1 | tf_op jit(solution)/shard_map/finish_rest/pallas_call | solution.py:634
  (75 shorter events, 10.3 us)
Async XLA Ops:
  0.6 5.1 %copy-start.4 = (bf16[512]{0:T(512)(128)(2,1)S(1)}, bf16[512]{0:T(512)(128)(2,1)}, u32[]{:S(2)}) copy-start(bf16[512]{0:T(512)(128)(2,1)} %param.17) | copy-start | bytes 3076
  0.7 5.1 %copy-start.2 = (bf16[512]{0:T(512)(128)(2,1)S(1)}, bf16[512]{0:T(512)(128)(2,1)}, u32[]{:S(2)}) copy-start(bf16[512]{0:T(512)(128)(2,1)} %param.18) | copy-start | bytes 3076
  0.7 5.1 %copy-start.7 = (bf16[512]{0:T(512)(128)(2,1)S(1)}, bf16[512]{0:T(512)(128)(2,1)}, u32[]{:S(2)}) copy-start(bf16[512]{0:T(512)(128)(2,1)} %param.22) | copy-start | bytes 3076
  0.7 5.1 %copy-start.8 = (bf16[512]{0:T(512)(128)(2,1)S(1)}, bf16[512]{0:T(512)(128)(2,1)}, u32[]{:S(2)}) copy-start(bf16[512]{0:T(512)(128)(2,1)} %param.23) | copy-start | bytes 3076
  0.7 5.2 %copy-start.9 = (bf16[512]{0:T(512)(128)(2,1)S(1)}, bf16[512]{0:T(512)(128)(2,1)}, u32[]{:S(2)}) copy-start(bf16[512]{0:T(512)(128)(2,1)} %param.24) | copy-start | bytes 3076
  0.7 5.2 %copy-start.10 = (bf16[512]{0:T(512)(128)(2,1)S(1)}, bf16[512]{0:T(512)(128)(2,1)}, u32[]{:S(2)}) copy-start(bf16[512]{0:T(512)(128)(2,1)} %param.28) | copy-start | bytes 3076
  0.7 5.2 %copy-start.6 = (bf16[2,512]{1,0:T(2,128)(2,1)S(1)}, bf16[2,512]{1,0:T(2,128)(2,1)}, u32[]{:S(2)}) copy-start(bf16[2,512]{1,0:T(2,128)(2,1)} %param.20) | copy-start | bytes 6148
  0.7 5.2 %copy-start.1 = (s32[16,128]{1,0:T(8,128)S(1)}, s32[16,128]{1,0:T(8,128)}, u32[]{:S(2)}) copy-start(s32[16,128]{1,0:T(8,128)} %param.16) | copy-start | bytes 24580
  2.7 35.5 %collective-permute-start = (bf16[1040,512]{1,0:T(8,128)(2,1)S(1)}, bf16[1040,512]{1,0:T(8,128)(2,1)}, u32[]{:S(2)}, u32[]{:S(2)}) collective-permute-start(bf16[1040,512]{1,0:T(8,128)(2,1)S(1)} %fetch.1), channel_id=1, source_target_pairs={{0,1},{1,0},{2,3},{3,2},{4,5},{5,4},{6,7},{7,6},{8,9},{9,8},{10,11... | collective-permute-start | bytes 3194888 | tf_op jit(solution)/shard_map/ppermute | solution.py:691
  38.2 3.0 %collective-permute-start.1 = (bf16[1040,512]{1,0:T(8,128)(2,1)}, bf16[1040,512]{1,0:T(8,128)(2,1)S(1)}, u32[]{:S(2)}, u32[]{:S(2)}) collective-permute-start(bf16[1040,512]{1,0:T(8,128)(2,1)} %collective-permute-done.w_send), channel_id=1, source_target_pairs={{0,2},{1,3},{2,0},{3,1},{4,6},{5,7},{6,4},{7,5},{8,10},{9,11},{10,... | collective-permute-start | bytes 3194888 | tf_op jit(solution)/shard_map/ppermute | solution.py:691
  38.3 27.5 %collective-permute-start.2 = (bf16[4,256,512]{2,1,0:T(8,128)(2,1)}, bf16[4,256,512]{2,1,0:T(8,128)(2,1)S(1)}, u32[]{:S(2)}, u32[]{:S(2)}) collective-permute-start(bf16[4,256,512]{2,1,0:T(8,128)(2,1)} %get-tuple-element.84), channel_id=1, source_target_pairs={{0,2},{1,3},{2,0},{3,1},{4,6},{5,7},{6,4},{7,5},{8,10},{9,11},{10,... | collective-permute-start | bytes 3145736 | tf_op jit(solution)/shard_map/ppermute | solution.py:691
  65.4 3.1 %collective-permute-start.3 = (bf16[4,256,512]{2,1,0:T(8,128)(2,1)}, bf16[4,256,512]{2,1,0:T(8,128)(2,1)}, u32[]{:S(2)}, u32[]{:S(2)}) collective-permute-start(bf16[4,256,512]{2,1,0:T(8,128)(2,1)} %get-tuple-element.91), channel_id=1, source_target_pairs={{0,2},{1,3},{2,0},{3,1},{4,6},{5,7},{6,4},{7,5},{8,10},{9,11},{10,... | collective-permute-start | bytes 3145736 | tf_op jit(solution)/shard_map/ppermute | solution.py:691
  70.4 16.3 %collective-permute-start.5 = (bf16[4,256,512]{2,1,0:T(8,128)(2,1)S(1)}, bf16[4,256,512]{2,1,0:T(8,128)(2,1)S(1)}, u32[]{:S(2)}, u32[]{:S(2)}) collective-permute-start(bf16[4,256,512]{2,1,0:T(8,128)(2,1)S(1)} %get-tuple-element.104), channel_id=1, source_target_pairs={{0,4},{1,5},{2,3},{3,2},{4,0},{5,1},{6,7},{7,6},{8,12},{9,13},{10,... | collective-permute-start | bytes 3145736 | tf_op jit(solution)/shard_map/ppermute | solution.py:691
  86.6 6.2 %collective-permute-start.4 = (bf16[8,32,2176]{2,1,0:T(8,128)(2,1)S(1)}, bf16[8,32,2176]{2,1,0:T(8,128)(2,1)S(1)}, u32[]{:S(2)}, u32[]{:S(2)}) collective-permute-start(bf16[8,32,2176]{2,1,0:T(8,128)(2,1)S(1)} %get-tuple-element.101), channel_id=1, source_target_pairs={{0,2},{1,3},{2,0},{3,1},{4,6},{5,7},{6,4},{7,5},{8,10},{9,11},{10,... | collective-permute-start | bytes 3342344 | tf_op jit(solution)/shard_map/ppermute | solution.py:691
  87.5 12.4 %collective-permute-start.7 = (bf16[2,256,512]{2,1,0:T(8,128)(2,1)S(1)}, bf16[2,256,512]{2,1,0:T(8,128)(2,1)S(1)}, u32[]{:S(2)}, u32[]{:S(2)}) collective-permute-start(bf16[2,256,512]{2,1,0:T(8,128)(2,1)S(1)} %get-tuple-element.111), channel_id=1, source_target_pairs={{0,1},{1,0},{2,10},{3,11},{4,5},{5,4},{6,14},{7,15},{8,9},{9,8},{1... | collective-permute-start | bytes 1572872 | tf_op jit(solution)/shard_map/ppermute | solution.py:691
  93.5 9.6 %collective-permute-start.6 = (bf16[4,32,2176]{2,1,0:T(8,128)(2,1)S(1)}, bf16[4,32,2176]{2,1,0:T(8,128)(2,1)S(1)}, u32[]{:S(2)}, u32[]{:S(2)}) collective-permute-start(bf16[4,32,2176]{2,1,0:T(8,128)(2,1)S(1)} %get-tuple-element.110), channel_id=1, source_target_pairs={{0,1},{1,0},{2,6},{3,7},{4,5},{5,4},{6,2},{7,3},{8,9},{9,8},{10,14... | collective-permute-start | bytes 1671176 | tf_op jit(solution)/shard_map/ppermute | solution.py:691
  100.5 6.4 %collective-permute-start.9 = (bf16[1,256,512]{2,1,0:T(8,128)(2,1)S(1)}, bf16[1,256,512]{2,1,0:T(8,128)(2,1)S(1)}, u32[]{:S(2)}, u32[]{:S(2)}) collective-permute-start(bf16[1,256,512]{2,1,0:T(8,128)(2,1)S(1)} %get-tuple-element.118), channel_id=1, source_target_pairs={{0,8},{1,9},{2,6},{3,7},{4,12},{5,13},{6,2},{7,3},{8,0},{9,1},{10,... | collective-permute-start | bytes 786440 | tf_op jit(solution)/shard_map/ppermute | solution.py:691
  103.8 7.1 %collective-permute-start.8 = (bf16[2,32,2176]{2,1,0:T(8,128)(2,1)S(1)}, bf16[2,32,2176]{2,1,0:T(8,128)(2,1)S(1)}, u32[]{:S(2)}, u32[]{:S(2)}) collective-permute-start(bf16[2,32,2176]{2,1,0:T(8,128)(2,1)S(1)} %get-tuple-element.117), channel_id=1, source_target_pairs={{0,8},{1,9},{2,3},{3,2},{4,12},{5,13},{6,7},{7,6},{8,0},{9,1},{10,... | collective-permute-start | bytes 835592 | tf_op jit(solution)/shard_map/ppermute | solution.py:691
  107.0 17.3 %collective-permute-start.12 = (bf16[1,256,512]{2,1,0:T(8,128)(2,1)S(1)}, bf16[1,256,512]{2,1,0:T(8,128)(2,1)S(1)}, u32[]{:S(2)}, u32[]{:S(2)}) collective-permute-start(bf16[1,256,512]{2,1,0:T(8,128)(2,1)S(1)} %add_convert_fusion.1), channel_id=1, source_target_pairs={{0,16},{1,17},{2,18},{3,19},{4,20},{5,21},{6,22},{7,23},{8,24},{9,... | collective-permute-start | bytes 786440 | tf_op jit(solution)/shard_map/ppermute | solution.py:691
  111.5 8.0 %collective-permute-start.10 = (bf16[1,32,2176]{2,1,0:T(8,128)(2,1)S(1)}, bf16[1,32,2176]{2,1,0:T(8,128)(2,1)S(1)}, u32[]{:S(2)}, u32[]{:S(2)}) collective-permute-start(bf16[1,32,2176]{2,1,0:T(8,128)(2,1)S(1)} %get-tuple-element.122), channel_id=1, source_target_pairs={{0,4},{1,5},{2,10},{3,11},{4,0},{5,1},{6,14},{7,15},{8,12},{9,13},... | collective-permute-start | bytes 417800 | tf_op jit(solution)/shard_map/ppermute | solution.py:691
  119.5 9.5 %collective-permute-start.11 = (bf16[1,32,2176]{2,1,0:T(8,128)(2,1)S(1)}, bf16[1,32,2176]{2,1,0:T(8,128)(2,1)S(1)}, u32[]{:S(2)}, u32[]{:S(2)}) collective-permute-start(bf16[1,32,2176]{2,1,0:T(8,128)(2,1)S(1)} %add_convert_fusion.3), channel_id=1, source_target_pairs={{0,16},{1,17},{2,18},{3,19},{4,20},{5,21},{6,22},{7,23},{8,24},{9,... | collective-permute-start | bytes 417800 | tf_op jit(solution)/shard_map/ppermute | solution.py:691
  124.4 7.5 %collective-permute-start.14 = (bf16[1,256,512]{2,1,0:T(8,128)(2,1)S(1)}, bf16[1,256,512]{2,1,0:T(8,128)(2,1)S(1)}, u32[]{:S(2)}, u32[]{:S(2)}) collective-permute-start(bf16[1,256,512]{2,1,0:T(8,128)(2,1)S(1)} %add_convert_fusion), channel_id=1, source_target_pairs={{0,8},{1,9},{2,6},{3,7},{4,12},{5,13},{6,2},{7,3},{8,0},{9,1},{10,... | collective-permute-start | bytes 786440 | tf_op jit(solution)/shard_map/ppermute | solution.py:691
  129.0 5.1 %collective-permute-start.13 = (bf16[1,32,2176]{2,1,0:T(8,128)(2,1)S(1)}, bf16[1,32,2176]{2,1,0:T(8,128)(2,1)S(1)}, u32[]{:S(2)}, u32[]{:S(2)}) collective-permute-start(bf16[1,32,2176]{2,1,0:T(8,128)(2,1)S(1)} %add_convert_fusion.2), channel_id=1, source_target_pairs={{0,4},{1,5},{2,10},{3,11},{4,0},{5,1},{6,14},{7,15},{8,12},{9,13},... | collective-permute-start | bytes 417800 | tf_op jit(solution)/shard_map/ppermute | solution.py:691
  134.2 6.6 %collective-permute-start.15 = (bf16[2,32,2176]{2,1,0:T(8,128)(2,1)S(1)}, bf16[2,32,2176]{2,1,0:T(8,128)(2,1)S(1)}, u32[]{:S(2)}, u32[]{:S(2)}) collective-permute-start(bf16[2,32,2176]{2,1,0:T(8,128)(2,1)S(1)} %pad_maximum_fusion.2), channel_id=1, source_target_pairs={{0,8},{1,9},{2,3},{3,2},{4,12},{5,13},{6,7},{7,6},{8,0},{9,1},{10,... | collective-permute-start | bytes 835592 | tf_op jit(solution)/shard_map/ppermute | solution.py:691
  134.6 14.4 %collective-permute-start.17 = (bf16[2,256,512]{2,1,0:T(8,128)(2,1)S(1)}, bf16[2,256,512]{2,1,0:T(8,128)(2,1)S(1)}, u32[]{:S(2)}, u32[]{:S(2)}) collective-permute-start(bf16[2,256,512]{2,1,0:T(8,128)(2,1)S(1)} %pad_maximum_fusion.1.refs_0_), channel_id=1, source_target_pairs={{0,4},{1,5},{2,10},{3,11},{4,0},{5,1},{6,14},{7,15},{8,12},{9,13},... | collective-permute-start | bytes 1572872 | tf_op jit(solution)/shard_map/ppermute | solution.py:691
  134.7 14.9 %collective-permute-start.18 = (bf16[2,256,512]{2,1,0:T(8,128)(2,1)S(1)}, bf16[2,256,512]{2,1,0:T(8,128)(2,1)S(1)}, u32[]{:S(2)}, u32[]{:S(2)}) collective-permute-start(bf16[2,256,512]{2,1,0:T(8,128)(2,1)S(1)} %pad_maximum_fusion.1.refs_0_), channel_id=1, source_target_pairs={{0,2},{1,3},{2,0},{3,1},{4,6},{5,7},{6,4},{7,5},{8,10},{9,11},{10,... | collective-permute-start | bytes 1572872 | tf_op jit(solution)/shard_map/ppermute | solution.py:691
  140.9 13.1 %collective-permute-start.16 = (bf16[4,32,2176]{2,1,0:T(8,128)(2,1)S(1)}, bf16[4,32,2176]{2,1,0:T(8,128)(2,1)S(1)}, u32[]{:S(2)}, u32[]{:S(2)}) collective-permute-start(bf16[4,32,2176]{2,1,0:T(8,128)(2,1)S(1)} %pad_maximum_fusion.refs_0_), channel_id=1, source_target_pairs={{0,1},{1,0},{2,6},{3,7},{4,5},{5,4},{6,2},{7,3},{8,9},{9,8},{10,14... | collective-permute-start | bytes 1671176 | tf_op jit(solution)/shard_map/ppermute | solution.py:691
  149.0 5.1 %copy-start.3 = (bf16[512]{0:T(512)(128)(2,1)S(1)}, bf16[512]{0:T(512)(128)(2,1)}, u32[]{:S(2)}) copy-start(bf16[512]{0:T(512)(128)(2,1)} %param.18) | copy-start | bytes 3076
  149.0 5.1 %copy-start.5 = (bf16[512]{0:T(512)(128)(2,1)S(1)}, bf16[512]{0:T(512)(128)(2,1)}, u32[]{:S(2)}) copy-start(bf16[512]{0:T(512)(128)(2,1)} %param.17) | copy-start | bytes 3076
  149.0 2.0 %collective-permute-start.19 = (bf16[2,256,512]{2,1,0:T(8,128)(2,1)S(1)}, bf16[2,256,512]{2,1,0:T(8,128)(2,1)S(1)}, u32[]{:S(2)}, u32[]{:S(2)}) collective-permute-start(bf16[2,256,512]{2,1,0:T(8,128)(2,1)S(1)} %collective-permute-done.17.refs_1_), channel_id=1, source_target_pairs={{0,2},{1,3},{2,0},{3,1},{4,6},{5,7},{6,4},{7,5},{8,10},{9,11},{10,... | collective-permute-start | bytes 1572872 | tf_op jit(solution)/shard_map/ppermute | solution.py:691
  149.1 5.2 %collective-permute-start.20 = (bf16[4,32,2176]{2,1,0:T(8,128)(2,1)S(1)}, bf16[4,32,2176]{2,1,0:T(8,128)(2,1)S(1)}, u32[]{:S(2)}, u32[]{:S(2)}) collective-permute-start(bf16[4,32,2176]{2,1,0:T(8,128)(2,1)S(1)} %pad_maximum_fusion.refs_0_), channel_id=1, source_target_pairs={{0,2},{1,3},{2,0},{3,1},{4,6},{5,7},{6,4},{7,5},{8,10},{9,11},{10,... | collective-permute-start | bytes 1671176 | tf_op jit(solution)/shard_map/ppermute | solution.py:691
  154.0 2.0 %collective-permute-start.21 = (bf16[4,32,2176]{2,1,0:T(8,128)(2,1)S(1)}, bf16[4,32,2176]{2,1,0:T(8,128)(2,1)S(1)}, u32[]{:S(2)}, u32[]{:S(2)}) collective-permute-start(bf16[4,32,2176]{2,1,0:T(8,128)(2,1)S(1)} %collective-permute-done.16.refs_1_), channel_id=1, source_target_pairs={{0,2},{1,3},{2,0},{3,1},{4,6},{5,7},{6,4},{7,5},{8,10},{9,11},{10,... | collective-permute-start | bytes 1671176 | tf_op jit(solution)/shard_map/ppermute | solution.py:691
  (2 other events, 2.4 us)

commit v6 on v5

--- a/solution.py
+++ b/solution.py
@@ -476,11 +476,8 @@
     )(*args)
 
 
-def layer_out_body(own, resid, oth, down, w_send, w_keep, vecs, *refs):
-    d = resid.shape[1]
-    half = w_send.shape[1]
-    out = mm(own[...], down[...])
-    out += mm(oth[:, 0:half], w_send[d : d + half, :]) + mm(oth[:, half:], w_keep[d : d + half, :])
+def layer_out_body(own, resid, oth, down, down_oth, vecs, *refs):
+    out = mm(own[...], down[...]) + mm(oth[...], down_oth[...])
     refs[-1][...] = (resid[...] + out + vecs[...].astype(F32)[7:8]).astype(BF)
 
 
@@ -732,19 +729,20 @@
     gated_own, dh2_own, own_keep, own_send, gub_own = ffn_own(
         core_s, vmem(h2), out_grad, up_weight, vecs, down_weight, rows=512
     )
-    w_send = hbm(after(w_send, own_send))
+    w_send = after(w_send, own_send)
     w_keep = swap(w_send, "core")
     own_recv = swap(own_send, "core")
     gated_oth, dattn, dctx, oth_keep, oth_send, gub_oth, gout, vec = ffn_other(
-        vmem(h2), out_grad, w_send, w_keep, vmem(dh2_own), hbm(resid), hbm(ctx), out_weight, vecs, rows=512
+        vmem(h2), out_grad, hbm(w_send), w_keep, vmem(dh2_own), hbm(resid), hbm(ctx), out_weight, vecs, rows=512
     )
     oth_recv = swap(oth_send, "core")
+    down_oth = jnp.concatenate([w[d : d + half] for w in lax.optimization_barrier((w_send, w_keep, oth_send))[:2]])
     blocks = t // 512
 
     def layer_out_part(first, count, before, *ready):
         return in_part(
             layer_out_body, 512, first, count, (hbm(gated_own), hbm(after(resid, *ready)), hbm(gated_oth)),
-            (down_weight, w_send, hbm(w_keep), vecs), before, 4 * half * d, "layer_out",
+            (down_weight, hbm(down_oth), vecs), before, 4 * half * d, "layer_out",
         )
 
     def in_grad_part(first, count, before, *ready):

time: 160 us -> 159 us (level)
  transfers between devices with their start and end apart: 22 -> 22, of which waited for: 11 -> 10; matrix products, arithmetic and copies ran while one was open for 0% -> 2% of each run, Pallas kernels for 62% -> 62%
where the time goes in v6:
time: 159 us; the launch traced here: 158 us
  Pallas kernels  104 us (65%)
  waiting for transfers between devices  25.1 us (16%)
  starting transfers between devices  24 us (15%)
  local copies, waits for them, and re-layouts  2.19 us (1%)
    ppermute x22, waiting for transfers between devices, swap(): return lax.ppermute(value, BOTH, pairs)  25.1 us
    ppermute x22, starting transfers between devices, swap(): return lax.ppermute(value, BOTH, pairs)  24 us
    pallas_call x1, Pallas kernels, ffn_other(): pl.pallas_call(ffn_other_body, grid_spec=pltpu.PrefetchScalarGridSpec(num...  23.2 us
    pallas_call x4, Pallas kernels, in_part(): pl.pallas_call(body, grid=(count,), in_specs=[spec(a.shape[1]) for a in s...  21.7 us
    pallas_call x1, Pallas kernels, ffn_own(): pl.pallas_call(ffn_own_body, grid_spec=pltpu.PrefetchScalarGridSpec(num_s...  17.2 us
    pallas_call x1, Pallas kernels, attn_fwd(): pl.pallas_call(attn_fwd_body, grid=(t // rows,), in_specs=[rows_spec(rows...  15 us
    pallas_call x1, Pallas kernels, attn_bwd(): pl.pallas_call(attn_bwd_body, grid_spec=pltpu.PrefetchScalarGridSpec(num_...  14.6 us
    pallas_call x6, Pallas kernels, on_chip(): pl.pallas_call(body, in_specs=[pl.BlockSpec(memory_space=pltpu.SMEM)] + [...  5.44 us
  transfers between devices with their start and end apart: 22, of which 10 were waited for; matrix products, arithmetic and copies ran while one was open for 2% of the time, Pallas kernels for 62%

profile of v6, /device:TPU:0, one launch (start us, length us, event | category | flops | bytes accessed | tf_op | source)
XLA Modules:
  0.0 158.4 jit_solution(9388277126776343547)
XLA Ops:
  1.5 1.3 fetch.1
  2.7 3.0 %collective-permute-start = (bf16[1040,512]{1,0:T(8,128)(2,1)S(1)}, bf16[1040,512]{1,0:T(8,128)(2,1)}, u32[]{:S(2)}, u32[]{:S(2)}) collective-permute-start(bf16[1040,512]{1,0:T(8,128)(2,1)S(1)} %fetch.1), channel_id=1, source_target_pairs={{0,1},{1,0},{2,3},{3,2},{4,5},{5,4},{6,7},{7,6},{8,9},{9,8},{10,11... | collective-permute-start | bytes 3194888 | tf_op jit(solution)/shard_map/ppermute | solution.py:688
  6.0 15.0 %attn_fwd.1 = (bf16[2048,1536]{1,0:T(8,128)(2,1)}, bf16[2048,512]{1,0:T(8,128)(2,1)}, f32[2048,512]{1,0:T(8,128)}, bf16[2048,512]{1,0:T(8,128)(2,1)S(1)}, bf16[5...) custom-call(bf16[2048,512]{1,0:T(8,128)(2,1)} %tok.5, s32[4,4,128]{2,1,0:T(4,128)S(1)} %bitcast.18, ...), custom_call_target="tpu_custom_call" | custom-call | flops 51539607552 | bytes 1 | tf_op jit(solution)/shard_map/attn_fwd/pallas_call | solution.py:135
  21.0 17.2 %ffn_own.1 = (bf16[2048,1024]{1,0:T(8,128)(2,1)}, f32[2048,512]{1,0:T(8,128)S(1)}, bf16[4,256,512]{2,1,0:T(8,128)(2,1)S(1)}, bf16[4,256,512]{2,1,0:T(8,128)(2,1)}, f32[2,512]{1,0:T(2,128)S(1)}) custom-call(s32[1]{0:T(128)} %bitcast.core, bf16[2048,512]{1,0:T(8,128)(2,1)S(1)} %get-tuple-element.82.h2, bf16[2048,512]{1,0:T(8,128)(2,1)} %g.3, ...), custom_call_target="tpu_custom_call" | custom-call | flops 85899345920 | bytes 1 | tf_op jit(solution)/shard_map/ffn_own/pallas_call | solution.py:255
  38.8 2.4 %collective-permute-done.1.w_keep = bf16[1040,512]{1,0:T(8,128)(2,1)S(1)} collective-permute-done((bf16[1040,512]{1,0:T(8,128)(2,1)}, bf16[1040,512]{1,0:T(8,128)(2,1)S(1)}, u32[]{:S(2)}, u32[]{:S(2)}) %collective-permute-start.1) | collective-permute-done | bytes 1064992 | tf_op jit(solution)/shard_map/ppermute | solution.py:688
  41.1 23.2 %ffn_other.1 = (bf16[2048,1024]{1,0:T(8,128)(2,1)}, bf16[2048,512]{1,0:T(8,128)(2,1)}, bf16[2048,512]{1,0:T(8,128)(2,1)}, bf16[4,256,512]{2,1,0:T(8,128)(2,1)S(1...) custom-call(bf16[2048,512]{1,0:T(8,128)(2,1)S(1)} %get-tuple-element.8, ...), custom_call_target="tpu_custom_call" | custom-call | flops 103079215104 | bytes 1 | tf_op jit(solution)/shard_map/ffn_other/pallas_call | solution.py:315
  64.7 2.7 %collective-permute-done.3.oth_b = bf16[4,256,512]{2,1,0:T(8,128)(2,1)} collective-permute-done((bf16[4,256,512]{2,1,0:T(8,128)(2,1)}, bf16[4,256,512]{2,1,0:T(8,128)(2,1)}, u32[]{:S(2)}, u32[]{:S(2)}) %collective-permute-start.3) | collective-permute-done | bytes 1048608 | tf_op jit(solution)/shard_map/ppermute | solution.py:688
  67.4 1.9 %split.1 = (bf16[4,256,512]{2,1,0:T(8,128)(2,1)S(1)}, bf16[4,256,512]{2,1,0:T(8,128)(2,1)S(1)}) custom-call(s32[14]{0:T(128)S(1)} %stack.82.at, bf16[4,256,512]{2,1,0:T(8,128)(2,1)S(1)} %get-tuple-element.91.own_a, bf16[4,256,512]{2,1,0:T(8,128)(2,1)S(1)} %collective-permute-done.2.own_b, bf16[4,256,512]{2,1,0:T(8,128)(2,1)S(1)} %get-tuple-element.92.oth_a, ...), custom_call_target="tpu_custom_call" | custom-call | bytes 1 | tf_op jit(solution)/shard_map/split/pallas_call | solution.py:485
  69.3 1.6 collective-permute-start.5
  70.9 14.6 %attn_bwd.1 = (bf16[2048,1536]{1,0:T(8,128)(2,1)S(1)}, bf16[8,32,2176]{2,1,0:T(8,128)(2,1)S(1)}, bf16[8,32,2176]{2,1,0:T(8,128)(2,1)S(1)}) custom-call(s32[2]{0:T(128)S(1)} %pad_add_fusion.place, bf16[2048,1536]{1,0:T(8,128)(2,1)} %get-tuple-element.85.joined, bf16[2048,512]{1,0:T(8,128)(2,1)} %get-tuple-element.95.dc, ...), custom_call_target="tpu_custom_call" | custom-call | flops 103079215104 | bytes 1 | tf_op jit(solution)/shard_map/attn_bwd/pallas_call | solution.py:431
  87.0 4.7 %in_grad.2.refs_0_ = bf16[2048,512]{1,0:T(8,128)(2,1)} custom-call(bf16[2048,1536]{1,0:T(8,128)(2,1)S(1)} %get-tuple-element.104.dj, bf16[2048,512]{1,0:T(8,128)(2,1)} %tok.5, bf16[2048,512]{1,0:T(8,128)(2,1)} %get-tuple-element.114.dattn, bf16[512,1536]{1,0:T(8,128)(2,1)S(1)} %copy-done.1, bf16[16,512]{1,0:T(8,128)(2,1)S(1)} %concatenate.16.vecs), custom_call_target="tpu_custom_call" | custom-call | flops 12884901888 | bytes 1 | tf_op jit(solution)/shard_map/in_grad/pallas_call | solution.py:464
  92.5 1.6 collective-permute-start.6
  94.1 4.7 %in_grad.3 = bf16[2048,512]{1,0:T(8,128)(2,1)} custom-call(bf16[2048,1536]{1,0:T(8,128)(2,1)S(1)} %get-tuple-element.104.dj, bf16[2048,512]{1,0:T(8,128)(2,1)} %tok.5, bf16[2048,512]{1,0:T(8,128)(2,1)} %get-tuple-element.114.dattn, bf16[512,1536]{1,0:T(8,128)(2,1)S(1)} %copy-done.1, ...), custom_call_target="tpu_custom_call", output_to_operand_aliasing={{}: (5, {})} | custom-call | flops 12884901888 | bytes 1 | tf_op jit(solution)/shard_map/in_grad/pallas_call | solution.py:464
  99.5 1.6 %collective-permute-start.9 = (bf16[1,256,512]{2,1,0:T(8,128)(2,1)S(1)}, bf16[1,256,512]{2,1,0:T(8,128)(2,1)S(1)}, u32[]{:S(2)}, u32[]{:S(2)}) collective-permute-start(bf16[1,256,512]{2,1,0:T(8,128)(2,1)S(1)} %get-tuple-element.120), channel_id=1, source_target_pairs={{0,8},{1,9},{2,6},{3,7},{4,12},{5,13},{6,2},{7,3},{8,0},{9,1},{10,... | collective-permute-start | bytes 786440 | tf_op jit(solution)/shard_map/ppermute | solution.py:688
  101.1 1.1 slice.9
  102.9 1.5 collective-permute-start.8
  104.4 1.0 pad_maximum_fusion.down_oth
  106.0 2.6 %collective-permute-start.12 = (bf16[1,256,512]{2,1,0:T(8,128)(2,1)S(1)}, bf16[1,256,512]{2,1,0:T(8,128)(2,1)S(1)}, u32[]{:S(2)}, u32[]{:S(2)}) collective-permute-start(bf16[1,256,512]{2,1,0:T(8,128)(2,1)S(1)} %add_convert_fusion.1), channel_id=1, source_target_pairs={{0,16},{1,17},{2,18},{3,19},{4,20},{5,21},{6,22},{7,23},{8,24},{9,... | collective-permute-start | bytes 786440 | tf_op jit(solution)/shard_map/ppermute | solution.py:688
  108.6 1.4 collective-permute-done.8.b
  110.7 1.3 collective-permute-start.10
  112.0 6.1 %layer_out.2.refs_0_ = bf16[2048,512]{1,0:T(8,128)(2,1)} custom-call(bf16[2048,1024]{1,0:T(8,128)(2,1)} %get-tuple-element.83.own, f32[2048,512]{1,0:T(8,128)} %get-tuple-element.135.resid, bf16[2048,1024]{1,0:T(8,128)(2,1)} %get-tuple-element.126.oth, bf16[1024,512]{1,0:T(8,128)(2,1)} %down.7, bf16[1024,512]{1,0:T(8,128)(2,1)} %pad_maximum_fusion.down_oth, ...), custom_call_target="tpu_custom_call" | custom-call | flops 17179869184 | bytes 1 | tf_op jit(solution)/shard_map/layer_out/pallas_call | solution.py:464
  118.2 4.8 %collective-permute-start.11 = (bf16[1,32,2176]{2,1,0:T(8,128)(2,1)S(1)}, bf16[1,32,2176]{2,1,0:T(8,128)(2,1)S(1)}, u32[]{:S(2)}, u32[]{:S(2)}) collective-permute-start(bf16[1,32,2176]{2,1,0:T(8,128)(2,1)S(1)} %add_convert_fusion.3), channel_id=1, source_target_pairs={{0,16},{1,17},{2,18},{3,19},{4,20},{5,21},{6,22},{7,23},{8,24},{9,... | collective-permute-start | bytes 417800 | tf_op jit(solution)/shard_map/ppermute | solution.py:688
  124.0 3.6 %collective-permute-done.11 = bf16[1,32,2176]{2,1,0:T(8,128)(2,1)S(1)} collective-permute-done((bf16[1,32,2176]{2,1,0:T(8,128)(2,1)S(1)}, bf16[1,32,2176]{2,1,0:T(8,128)(2,1)S(1)}, u32[]{:S(2)}, u32[]{:S(2)}) %collective-permute-start.11) | collective-permute-done | bytes 139296 | tf_op jit(solution)/shard_map/ppermute | solution.py:688
  128.1 2.9 %collective-permute-done.14 = bf16[1,256,512]{2,1,0:T(8,128)(2,1)S(1)} collective-permute-done((bf16[1,256,512]{2,1,0:T(8,128)(2,1)S(1)}, bf16[1,256,512]{2,1,0:T(8,128)(2,1)S(1)}, u32[]{:S(2)}, u32[]{:S(2)}) %collective-permute-start.14) | collective-permute-done | bytes 262176 | tf_op jit(solution)/shard_map/ppermute | solution.py:688
  131.1 1.7 %collective-permute-done.13 = bf16[1,32,2176]{2,1,0:T(8,128)(2,1)S(1)} collective-permute-done((bf16[1,32,2176]{2,1,0:T(8,128)(2,1)S(1)}, bf16[1,32,2176]{2,1,0:T(8,128)(2,1)S(1)}, u32[]{:S(2)}, u32[]{:S(2)}) %collective-permute-start.13) | collective-permute-done | bytes 139296 | tf_op jit(solution)/shard_map/ppermute | solution.py:688
  133.3 7.0 %collective-permute-done.15 = bf16[2,32,2176]{2,1,0:T(8,128)(2,1)S(1)} collective-permute-done((bf16[2,32,2176]{2,1,0:T(8,128)(2,1)S(1)}, bf16[2,32,2176]{2,1,0:T(8,128)(2,1)S(1)}, u32[]{:S(2)}, u32[]{:S(2)}) %collective-permute-start.15) | collective-permute-done | bytes 278560 | tf_op jit(solution)/shard_map/ppermute | solution.py:688
  140.4 1.7 %collective-permute-start.16 = (bf16[4,32,2176]{2,1,0:T(8,128)(2,1)S(1)}, bf16[4,32,2176]{2,1,0:T(8,128)(2,1)S(1)}, u32[]{:S(2)}, u32[]{:S(2)}) collective-permute-start(bf16[4,32,2176]{2,1,0:T(8,128)(2,1)S(1)} %pad_maximum_fusion.1.refs_0_), channel_id=1, source_target_pairs={{0,1},{1,0},{2,6},{3,7},{4,5},{5,4},{6,2},{7,3},{8,9},{9,8},{10,14... | collective-permute-start | bytes 1671176 | tf_op jit(solution)/shard_map/ppermute | solution.py:688
  142.1 6.1 %layer_out.3 = bf16[2048,512]{1,0:T(8,128)(2,1)} custom-call(bf16[2048,1024]{1,0:T(8,128)(2,1)} %get-tuple-element.83.own, f32[2048,512]{1,0:T(8,128)} %get-tuple-element.135.resid, bf16[2048,1024]{1,0:T(8,128)(2,1)} %get-tuple-element.126.oth, bf16[1024,512]{1,0:T(8,128)(2,1)} %down.7, ...), custom_call_target="tpu_custom_call", output_to_operand_aliasing={{}: (6, {})} | custom-call | flops 17179869184 | bytes 1 | tf_op jit(solution)/shard_map/layer_out/pallas_call | solution.py:464
  148.8 1.4 collective-permute-done.19.refs_3_
  150.2 3.0 %finish_ffn.1 = (f32[512,1024]{1,0:T(8,128)}, f32[1024,512]{1,0:T(8,128)}) custom-call(s32[14]{0:T(128)S(1)} %stack.82.at, bf16[2,256,512]{2,1,0:T(8,128)(2,1)S(1)} %pad_maximum_fusion.2.refs_0_, bf16[2,256,512]{2,1,0:T(8,128)(2,1)S(1)} %collective-permute-done.17.refs_1_, bf16[2,256,512]{2,1,0:T(8,128)(2,1)S(1)} %collective-permute-done.18.refs_2_, ...), custom_call_target="tpu_custom_call" | custom-call | bytes 1 | tf_op jit(solution)/shard_map/finish_ffn/pallas_call | solution.py:559
  153.6 1.6 %collective-permute-done.21.refs_3_ = bf16[4,32,2176]{2,1,0:T(8,128)(2,1)S(1)} collective-permute-done((bf16[4,32,2176]{2,1,0:T(8,128)(2,1)S(1)}, bf16[4,32,2176]{2,1,0:T(8,128)(2,1)S(1)}, u32[]{:S(2)}, u32[]{:S(2)}) %collective-permute-start.21) | collective-permute-done | bytes 557088 | tf_op jit(solution)/shard_map/ppermute | solution.py:688
  155.2 3.1 %finish_rest.1 = (f32[512,1536]{1,0:T(8,128)}, f32[2,512]{1,0:T(2,128)}, f32[512,512]{1,0:T(8,128)}, f32[1,512]{1,0:T(1,128)}, f32[1,512]{1,0:T(1,128)}, /*index...) custom-call(s32[14]{0:T(128)S(1)} %stack.82.at, ...), custom_call_target="tpu_custom_call" | custom-call | bytes 1 | tf_op jit(solution)/shard_map/finish_rest/pallas_call | solution.py:631
  (79 shorter events, 9.7 us)
Async XLA Ops:
  0.6 5.1 %copy-start.5 = (bf16[512]{0:T(512)(128)(2,1)S(1)}, bf16[512]{0:T(512)(128)(2,1)}, u32[]{:S(2)}) copy-start(bf16[512]{0:T(512)(128)(2,1)} %param.17) | copy-start | bytes 3076
  0.7 5.1 %copy-start.3 = (bf16[512]{0:T(512)(128)(2,1)S(1)}, bf16[512]{0:T(512)(128)(2,1)}, u32[]{:S(2)}) copy-start(bf16[512]{0:T(512)(128)(2,1)} %param.18) | copy-start | bytes 3076
  0.7 5.1 %copy-start.8 = (bf16[512]{0:T(512)(128)(2,1)S(1)}, bf16[512]{0:T(512)(128)(2,1)}, u32[]{:S(2)}) copy-start(bf16[512]{0:T(512)(128)(2,1)} %param.22) | copy-start | bytes 3076
  0.7 5.1 %copy-start.9 = (bf16[512]{0:T(512)(128)(2,1)S(1)}, bf16[512]{0:T(512)(128)(2,1)}, u32[]{:S(2)}) copy-start(bf16[512]{0:T(512)(128)(2,1)} %param.23) | copy-start | bytes 3076
  0.7 5.2 %copy-start.10 = (bf16[512]{0:T(512)(128)(2,1)S(1)}, bf16[512]{0:T(512)(128)(2,1)}, u32[]{:S(2)}) copy-start(bf16[512]{0:T(512)(128)(2,1)} %param.24) | copy-start | bytes 3076
  0.7 5.2 %copy-start.11 = (bf16[512]{0:T(512)(128)(2,1)S(1)}, bf16[512]{0:T(512)(128)(2,1)}, u32[]{:S(2)}) copy-start(bf16[512]{0:T(512)(128)(2,1)} %param.28) | copy-start | bytes 3076
  0.7 5.2 %copy-start.7 = (bf16[2,512]{1,0:T(2,128)(2,1)S(1)}, bf16[2,512]{1,0:T(2,128)(2,1)}, u32[]{:S(2)}) copy-start(bf16[2,512]{1,0:T(2,128)(2,1)} %param.20) | copy-start | bytes 6148
  0.7 5.2 %copy-start.2 = (s32[16,128]{1,0:T(8,128)S(1)}, s32[16,128]{1,0:T(8,128)}, u32[]{:S(2)}) copy-start(s32[16,128]{1,0:T(8,128)} %param.16) | copy-start | bytes 24580
  2.7 35.4 %collective-permute-start = (bf16[1040,512]{1,0:T(8,128)(2,1)S(1)}, bf16[1040,512]{1,0:T(8,128)(2,1)}, u32[]{:S(2)}, u32[]{:S(2)}) collective-permute-start(bf16[1040,512]{1,0:T(8,128)(2,1)S(1)} %fetch.1), channel_id=1, source_target_pairs={{0,1},{1,0},{2,3},{3,2},{4,5},{5,4},{6,7},{7,6},{8,9},{9,8},{10,11... | collective-permute-start | bytes 3194888 | tf_op jit(solution)/shard_map/ppermute | solution.py:688
  38.2 3.0 %collective-permute-start.1 = (bf16[1040,512]{1,0:T(8,128)(2,1)}, bf16[1040,512]{1,0:T(8,128)(2,1)S(1)}, u32[]{:S(2)}, u32[]{:S(2)}) collective-permute-start(bf16[1040,512]{1,0:T(8,128)(2,1)} %collective-permute-done.w_send), channel_id=1, source_target_pairs={{0,2},{1,3},{2,0},{3,1},{4,6},{5,7},{6,4},{7,5},{8,10},{9,11},{10,... | collective-permute-start | bytes 3194888 | tf_op jit(solution)/shard_map/ppermute | solution.py:688
  38.3 26.5 %collective-permute-start.2 = (bf16[4,256,512]{2,1,0:T(8,128)(2,1)}, bf16[4,256,512]{2,1,0:T(8,128)(2,1)S(1)}, u32[]{:S(2)}, u32[]{:S(2)}) collective-permute-start(bf16[4,256,512]{2,1,0:T(8,128)(2,1)} %get-tuple-element.86), channel_id=1, source_target_pairs={{0,2},{1,3},{2,0},{3,1},{4,6},{5,7},{6,4},{7,5},{8,10},{9,11},{10,... | collective-permute-start | bytes 3145736 | tf_op jit(solution)/shard_map/ppermute | solution.py:688
  41.1 23.2 %copy-start = (bf16[1040,512]{1,0:T(8,128)(2,1)}, bf16[1040,512]{1,0:T(8,128)(2,1)S(1)}, u32[]{:S(2)}) copy-start(bf16[1040,512]{1,0:T(8,128)(2,1)S(1)} %collective-permute-done.1.w_keep) | copy-start | bytes 3194884
  64.4 3.1 %collective-permute-start.3 = (bf16[4,256,512]{2,1,0:T(8,128)(2,1)}, bf16[4,256,512]{2,1,0:T(8,128)(2,1)}, u32[]{:S(2)}, u32[]{:S(2)}) collective-permute-start(bf16[4,256,512]{2,1,0:T(8,128)(2,1)} %get-tuple-element.93), channel_id=1, source_target_pairs={{0,2},{1,3},{2,0},{3,1},{4,6},{5,7},{6,4},{7,5},{8,10},{9,11},{10,... | collective-permute-start | bytes 3145736 | tf_op jit(solution)/shard_map/ppermute | solution.py:688
  69.3 16.3 %collective-permute-start.5 = (bf16[4,256,512]{2,1,0:T(8,128)(2,1)S(1)}, bf16[4,256,512]{2,1,0:T(8,128)(2,1)S(1)}, u32[]{:S(2)}, u32[]{:S(2)}) collective-permute-start(bf16[4,256,512]{2,1,0:T(8,128)(2,1)S(1)} %get-tuple-element.106), channel_id=1, source_target_pairs={{0,4},{1,5},{2,3},{3,2},{4,0},{5,1},{6,7},{7,6},{8,12},{9,13},{10,... | collective-permute-start | bytes 3145736 | tf_op jit(solution)/shard_map/ppermute | solution.py:688
  85.6 6.2 %collective-permute-start.4 = (bf16[8,32,2176]{2,1,0:T(8,128)(2,1)S(1)}, bf16[8,32,2176]{2,1,0:T(8,128)(2,1)S(1)}, u32[]{:S(2)}, u32[]{:S(2)}) collective-permute-start(bf16[8,32,2176]{2,1,0:T(8,128)(2,1)S(1)} %get-tuple-element.103), channel_id=1, source_target_pairs={{0,2},{1,3},{2,0},{3,1},{4,6},{5,7},{6,4},{7,5},{8,10},{9,11},{10,... | collective-permute-start | bytes 3342344 | tf_op jit(solution)/shard_map/ppermute | solution.py:688
  86.4 12.4 %collective-permute-start.7 = (bf16[2,256,512]{2,1,0:T(8,128)(2,1)S(1)}, bf16[2,256,512]{2,1,0:T(8,128)(2,1)S(1)}, u32[]{:S(2)}, u32[]{:S(2)}) collective-permute-start(bf16[2,256,512]{2,1,0:T(8,128)(2,1)S(1)} %get-tuple-element.113), channel_id=1, source_target_pairs={{0,1},{1,0},{2,10},{3,11},{4,5},{5,4},{6,14},{7,15},{8,9},{9,8},{1... | collective-permute-start | bytes 1572872 | tf_op jit(solution)/shard_map/ppermute | solution.py:688
  92.5 9.7 %collective-permute-start.6 = (bf16[4,32,2176]{2,1,0:T(8,128)(2,1)S(1)}, bf16[4,32,2176]{2,1,0:T(8,128)(2,1)S(1)}, u32[]{:S(2)}, u32[]{:S(2)}) collective-permute-start(bf16[4,32,2176]{2,1,0:T(8,128)(2,1)S(1)} %get-tuple-element.112), channel_id=1, source_target_pairs={{0,1},{1,0},{2,6},{3,7},{4,5},{5,4},{6,2},{7,3},{8,9},{9,8},{10,14... | collective-permute-start | bytes 1671176 | tf_op jit(solution)/shard_map/ppermute | solution.py:688
  98.8 5.6 %slice-start = ((bf16[1040,512]{1,0:T(8,128)(2,1)}), bf16[512,512]{1,0:T(8,128)(2,1)S(1)}, s32[]{:S(2)}) async-start(bf16[1040,512]{1,0:T(8,128)(2,1)} %copy-done), calls=%async_computation | async-start | bytes 1048576 | tf_op jit(solution)/shard_map/slice | solution.py:739
  99.5 6.4 %collective-permute-start.9 = (bf16[1,256,512]{2,1,0:T(8,128)(2,1)S(1)}, bf16[1,256,512]{2,1,0:T(8,128)(2,1)S(1)}, u32[]{:S(2)}, u32[]{:S(2)}) collective-permute-start(bf16[1,256,512]{2,1,0:T(8,128)(2,1)S(1)} %get-tuple-element.120), channel_id=1, source_target_pairs={{0,8},{1,9},{2,6},{3,7},{4,12},{5,13},{6,2},{7,3},{8,0},{9,1},{10,... | collective-permute-start | bytes 786440 | tf_op jit(solution)/shard_map/ppermute | solution.py:688
  102.9 7.1 %collective-permute-start.8 = (bf16[2,32,2176]{2,1,0:T(8,128)(2,1)S(1)}, bf16[2,32,2176]{2,1,0:T(8,128)(2,1)S(1)}, u32[]{:S(2)}, u32[]{:S(2)}) collective-permute-start(bf16[2,32,2176]{2,1,0:T(8,128)(2,1)S(1)} %get-tuple-element.119), channel_id=1, source_target_pairs={{0,8},{1,9},{2,3},{3,2},{4,12},{5,13},{6,7},{7,6},{8,0},{9,1},{10,... | collective-permute-start | bytes 835592 | tf_op jit(solution)/shard_map/ppermute | solution.py:688
  106.0 16.9 %collective-permute-start.12 = (bf16[1,256,512]{2,1,0:T(8,128)(2,1)S(1)}, bf16[1,256,512]{2,1,0:T(8,128)(2,1)S(1)}, u32[]{:S(2)}, u32[]{:S(2)}) collective-permute-start(bf16[1,256,512]{2,1,0:T(8,128)(2,1)S(1)} %add_convert_fusion.1), channel_id=1, source_target_pairs={{0,16},{1,17},{2,18},{3,19},{4,20},{5,21},{6,22},{7,23},{8,24},{9,... | collective-permute-start | bytes 786440 | tf_op jit(solution)/shard_map/ppermute | solution.py:688
  110.7 7.4 %collective-permute-start.10 = (bf16[1,32,2176]{2,1,0:T(8,128)(2,1)S(1)}, bf16[1,32,2176]{2,1,0:T(8,128)(2,1)S(1)}, u32[]{:S(2)}, u32[]{:S(2)}) collective-permute-start(bf16[1,32,2176]{2,1,0:T(8,128)(2,1)S(1)} %get-tuple-element.124), channel_id=1, source_target_pairs={{0,4},{1,5},{2,10},{3,11},{4,0},{5,1},{6,14},{7,15},{8,12},{9,13},... | collective-permute-start | bytes 417800 | tf_op jit(solution)/shard_map/ppermute | solution.py:688
  118.2 9.4 %collective-permute-start.11 = (bf16[1,32,2176]{2,1,0:T(8,128)(2,1)S(1)}, bf16[1,32,2176]{2,1,0:T(8,128)(2,1)S(1)}, u32[]{:S(2)}, u32[]{:S(2)}) collective-permute-start(bf16[1,32,2176]{2,1,0:T(8,128)(2,1)S(1)} %add_convert_fusion.3), channel_id=1, source_target_pairs={{0,16},{1,17},{2,18},{3,19},{4,20},{5,21},{6,22},{7,23},{8,24},{9,... | collective-permute-start | bytes 417800 | tf_op jit(solution)/shard_map/ppermute | solution.py:688
  123.0 8.0 %collective-permute-start.14 = (bf16[1,256,512]{2,1,0:T(8,128)(2,1)S(1)}, bf16[1,256,512]{2,1,0:T(8,128)(2,1)S(1)}, u32[]{:S(2)}, u32[]{:S(2)}) collective-permute-start(bf16[1,256,512]{2,1,0:T(8,128)(2,1)S(1)} %add_convert_fusion), channel_id=1, source_target_pairs={{0,8},{1,9},{2,6},{3,7},{4,12},{5,13},{6,2},{7,3},{8,0},{9,1},{10,... | collective-permute-start | bytes 786440 | tf_op jit(solution)/shard_map/ppermute | solution.py:688
  127.6 5.1 %collective-permute-start.13 = (bf16[1,32,2176]{2,1,0:T(8,128)(2,1)S(1)}, bf16[1,32,2176]{2,1,0:T(8,128)(2,1)S(1)}, u32[]{:S(2)}, u32[]{:S(2)}) collective-permute-start(bf16[1,32,2176]{2,1,0:T(8,128)(2,1)S(1)} %add_convert_fusion.2), channel_id=1, source_target_pairs={{0,4},{1,5},{2,10},{3,11},{4,0},{5,1},{6,14},{7,15},{8,12},{9,13},... | collective-permute-start | bytes 417800 | tf_op jit(solution)/shard_map/ppermute | solution.py:688
  132.8 7.6 %collective-permute-start.15 = (bf16[2,32,2176]{2,1,0:T(8,128)(2,1)S(1)}, bf16[2,32,2176]{2,1,0:T(8,128)(2,1)S(1)}, u32[]{:S(2)}, u32[]{:S(2)}) collective-permute-start(bf16[2,32,2176]{2,1,0:T(8,128)(2,1)S(1)} %pad_maximum_fusion.3), channel_id=1, source_target_pairs={{0,8},{1,9},{2,3},{3,2},{4,12},{5,13},{6,7},{7,6},{8,0},{9,1},{10,... | collective-permute-start | bytes 835592 | tf_op jit(solution)/shard_map/ppermute | solution.py:688
  132.8 15.4 %collective-permute-start.17 = (bf16[2,256,512]{2,1,0:T(8,128)(2,1)S(1)}, bf16[2,256,512]{2,1,0:T(8,128)(2,1)S(1)}, u32[]{:S(2)}, u32[]{:S(2)}) collective-permute-start(bf16[2,256,512]{2,1,0:T(8,128)(2,1)S(1)} %pad_maximum_fusion.2.refs_0_), channel_id=1, source_target_pairs={{0,4},{1,5},{2,10},{3,11},{4,0},{5,1},{6,14},{7,15},{8,12},{9,13},... | collective-permute-start | bytes 1572872 | tf_op jit(solution)/shard_map/ppermute | solution.py:688
  133.3 15.5 %collective-permute-start.18 = (bf16[2,256,512]{2,1,0:T(8,128)(2,1)S(1)}, bf16[2,256,512]{2,1,0:T(8,128)(2,1)S(1)}, u32[]{:S(2)}, u32[]{:S(2)}) collective-permute-start(bf16[2,256,512]{2,1,0:T(8,128)(2,1)S(1)} %pad_maximum_fusion.2.refs_0_), channel_id=1, source_target_pairs={{0,2},{1,3},{2,0},{3,1},{4,6},{5,7},{6,4},{7,5},{8,10},{9,11},{10,... | collective-permute-start | bytes 1572872 | tf_op jit(solution)/shard_map/ppermute | solution.py:688
  140.4 12.8 %collective-permute-start.16 = (bf16[4,32,2176]{2,1,0:T(8,128)(2,1)S(1)}, bf16[4,32,2176]{2,1,0:T(8,128)(2,1)S(1)}, u32[]{:S(2)}, u32[]{:S(2)}) collective-permute-start(bf16[4,32,2176]{2,1,0:T(8,128)(2,1)S(1)} %pad_maximum_fusion.1.refs_0_), channel_id=1, source_target_pairs={{0,1},{1,0},{2,6},{3,7},{4,5},{5,4},{6,2},{7,3},{8,9},{9,8},{10,14... | collective-permute-start | bytes 1671176 | tf_op jit(solution)/shard_map/ppermute | solution.py:688
  148.3 2.0 %collective-permute-start.19 = (bf16[2,256,512]{2,1,0:T(8,128)(2,1)S(1)}, bf16[2,256,512]{2,1,0:T(8,128)(2,1)S(1)}, u32[]{:S(2)}, u32[]{:S(2)}) collective-permute-start(bf16[2,256,512]{2,1,0:T(8,128)(2,1)S(1)} %collective-permute-done.17.refs_1_), channel_id=1, source_target_pairs={{0,2},{1,3},{2,0},{3,1},{4,6},{5,7},{6,4},{7,5},{8,10},{9,11},{10,... | collective-permute-start | bytes 1572872 | tf_op jit(solution)/shard_map/ppermute | solution.py:688
  148.3 5.2 %collective-permute-start.20 = (bf16[4,32,2176]{2,1,0:T(8,128)(2,1)S(1)}, bf16[4,32,2176]{2,1,0:T(8,128)(2,1)S(1)}, u32[]{:S(2)}, u32[]{:S(2)}) collective-permute-start(bf16[4,32,2176]{2,1,0:T(8,128)(2,1)S(1)} %pad_maximum_fusion.1.refs_0_), channel_id=1, source_target_pairs={{0,2},{1,3},{2,0},{3,1},{4,6},{5,7},{6,4},{7,5},{8,10},{9,11},{10,... | collective-permute-start | bytes 1671176 | tf_op jit(solution)/shard_map/ppermute | solution.py:688
  153.2 2.0 %collective-permute-start.21 = (bf16[4,32,2176]{2,1,0:T(8,128)(2,1)S(1)}, bf16[4,32,2176]{2,1,0:T(8,128)(2,1)S(1)}, u32[]{:S(2)}, u32[]{:S(2)}) collective-permute-start(bf16[4,32,2176]{2,1,0:T(8,128)(2,1)S(1)} %collective-permute-done.16.refs_1_), channel_id=1, source_target_pairs={{0,2},{1,3},{2,0},{3,1},{4,6},{5,7},{6,4},{7,5},{8,10},{9,11},{10,... | collective-permute-start | bytes 1671176 | tf_op jit(solution)/shard_map/ppermute | solution.py:688
  (3 other events, 11.7 us)

commit v7 on v6

--- a/solution.py
+++ b/solution.py
@@ -696,7 +696,7 @@
     u0 = [0, "y"] + list(range(1, up_dims))
     u1 = ["y", 1, 0] + list(range(2, up_dims))
     q0 = ["y", 1, 0, 2] + list(range(3, up_dims))
-    q1 = [0, "y", 1, 2] + list(range(3, up_dims))
+    q1 = [0, "y", 2, 1] + list(range(3, up_dims))
     at = jnp.stack(
         [core, bit(0), by_core(0, bit(u1[1]))]
         + [by_core(bit(u0[0]), bit(u1[1])), by_core(bit(u0[2]), bit(u1[2]))]

time: 159 us -> 158 us (level)
  waiting for transfers between devices: 25.1 us -> 22.3 us
  starting transfers between devices: 24 us -> 26.3 us
    ppermute x22, waiting for transfers between devices: 25.1 us -> 22.3 us  [swap(): return lax.ppermute(value, BOTH, pairs)]
    ppermute x22, starting transfers between devices: 24 us -> 26.3 us  [swap(): return lax.ppermute(value, BOTH, pairs)]
where the time goes in v7:
time: 158 us
  Pallas kernels  104 us (66%)
  starting transfers between devices  26.3 us (17%)
  waiting for transfers between devices  22.3 us (14%)
  local copies, waits for them, and re-layouts  2.19 us (1%)
    ppermute x22, starting transfers between devices, swap(): return lax.ppermute(value, BOTH, pairs)  26.3 us
    pallas_call x1, Pallas kernels, ffn_other(): pl.pallas_call(ffn_other_body, grid_spec=pltpu.PrefetchScalarGridSpec(num...  23.2 us
    ppermute x22, waiting for transfers between devices, swap(): return lax.ppermute(value, BOTH, pairs)  22.3 us
    pallas_call x4, Pallas kernels, in_part(): pl.pallas_call(body, grid=(count,), in_specs=[spec(a.shape[1]) for a in s...  21.7 us
    pallas_call x1, Pallas kernels, ffn_own(): pl.pallas_call(ffn_own_body, grid_spec=pltpu.PrefetchScalarGridSpec(num_s...  17.2 us
    pallas_call x1, Pallas kernels, attn_fwd(): pl.pallas_call(attn_fwd_body, grid=(t // rows,), in_specs=[rows_spec(rows...  15 us
    pallas_call x1, Pallas kernels, attn_bwd(): pl.pallas_call(attn_bwd_body, grid_spec=pltpu.PrefetchScalarGridSpec(num_...  14.6 us
    pallas_call x6, Pallas kernels, on_chip(): pl.pallas_call(body, in_specs=[pl.BlockSpec(memory_space=pltpu.SMEM)] + [...  5.44 us
  transfers between devices with their start and end apart: 22, of which 10 were waited for; matrix products, arithmetic and copies ran while one was open for 2% of the time, Pallas kernels for 62%

profile of v7, /device:TPU:0, one launch (start us, length us, event | category | flops | bytes accessed | tf_op | source)
XLA Modules:
  0.0 157.8 jit_solution(8065434082719175527)
XLA Ops:
  1.5 1.3 fetch.1
  2.7 3.0 %collective-permute-start = (bf16[1040,512]{1,0:T(8,128)(2,1)S(1)}, bf16[1040,512]{1,0:T(8,128)(2,1)}, u32[]{:S(2)}, u32[]{:S(2)}) collective-permute-start(bf16[1040,512]{1,0:T(8,128)(2,1)S(1)} %fetch.1), channel_id=1, source_target_pairs={{0,1},{1,0},{2,3},{3,2},{4,5},{5,4},{6,7},{7,6},{8,9},{9,8},{10,11... | collective-permute-start | bytes 3194888 | tf_op jit(solution)/shard_map/ppermute | solution.py:688
  6.0 15.0 %attn_fwd.1 = (bf16[2048,1536]{1,0:T(8,128)(2,1)}, bf16[2048,512]{1,0:T(8,128)(2,1)}, f32[2048,512]{1,0:T(8,128)}, bf16[2048,512]{1,0:T(8,128)(2,1)S(1)}, bf16[5...) custom-call(bf16[2048,512]{1,0:T(8,128)(2,1)} %tok.5, s32[4,4,128]{2,1,0:T(4,128)S(1)} %bitcast.20, ...), custom_call_target="tpu_custom_call" | custom-call | flops 51539607552 | bytes 1 | tf_op jit(solution)/shard_map/attn_fwd/pallas_call | solution.py:135
  21.0 17.2 %ffn_own.1 = (bf16[2048,1024]{1,0:T(8,128)(2,1)}, f32[2048,512]{1,0:T(8,128)S(1)}, bf16[4,256,512]{2,1,0:T(8,128)(2,1)S(1)}, bf16[4,256,512]{2,1,0:T(8,128)(2,1)}, f32[2,512]{1,0:T(2,128)S(1)}) custom-call(s32[1]{0:T(128)} %bitcast.core, bf16[2048,512]{1,0:T(8,128)(2,1)S(1)} %get-tuple-element.82.h2, bf16[2048,512]{1,0:T(8,128)(2,1)} %g.3, ...), custom_call_target="tpu_custom_call" | custom-call | flops 85899345920 | bytes 1 | tf_op jit(solution)/shard_map/ffn_own/pallas_call | solution.py:255
  38.8 2.4 %collective-permute-done.1.w_keep = bf16[1040,512]{1,0:T(8,128)(2,1)S(1)} collective-permute-done((bf16[1040,512]{1,0:T(8,128)(2,1)}, bf16[1040,512]{1,0:T(8,128)(2,1)S(1)}, u32[]{:S(2)}, u32[]{:S(2)}) %collective-permute-start.1) | collective-permute-done | bytes 1064992 | tf_op jit(solution)/shard_map/ppermute | solution.py:688
  41.1 23.2 %ffn_other.1 = (bf16[2048,1024]{1,0:T(8,128)(2,1)}, bf16[2048,512]{1,0:T(8,128)(2,1)}, bf16[2048,512]{1,0:T(8,128)(2,1)}, bf16[4,256,512]{2,1,0:T(8,128)(2,1)S(1...) custom-call(bf16[2048,512]{1,0:T(8,128)(2,1)S(1)} %get-tuple-element.8, ...), custom_call_target="tpu_custom_call" | custom-call | flops 103079215104 | bytes 1 | tf_op jit(solution)/shard_map/ffn_other/pallas_call | solution.py:315
  64.7 2.7 %collective-permute-done.3.oth_b = bf16[4,256,512]{2,1,0:T(8,128)(2,1)} collective-permute-done((bf16[4,256,512]{2,1,0:T(8,128)(2,1)}, bf16[4,256,512]{2,1,0:T(8,128)(2,1)}, u32[]{:S(2)}, u32[]{:S(2)}) %collective-permute-start.3) | collective-permute-done | bytes 1048608 | tf_op jit(solution)/shard_map/ppermute | solution.py:688
  67.4 1.9 %split.1 = (bf16[4,256,512]{2,1,0:T(8,128)(2,1)S(1)}, bf16[4,256,512]{2,1,0:T(8,128)(2,1)S(1)}) custom-call(s32[14]{0:T(128)S(1)} %stack.88.at, bf16[4,256,512]{2,1,0:T(8,128)(2,1)S(1)} %get-tuple-element.91.own_a, bf16[4,256,512]{2,1,0:T(8,128)(2,1)S(1)} %collective-permute-done.2.own_b, bf16[4,256,512]{2,1,0:T(8,128)(2,1)S(1)} %get-tuple-element.92.oth_a, ...), custom_call_target="tpu_custom_call" | custom-call | bytes 1 | tf_op jit(solution)/shard_map/split/pallas_call | solution.py:485
  69.3 1.6 %collective-permute-start.5 = (bf16[4,256,512]{2,1,0:T(8,128)(2,1)S(1)}, bf16[4,256,512]{2,1,0:T(8,128)(2,1)S(1)}, u32[]{:S(2)}, u32[]{:S(2)}) collective-permute-start(bf16[4,256,512]{2,1,0:T(8,128)(2,1)S(1)} %get-tuple-element.106), channel_id=1, source_target_pairs={{0,4},{1,5},{2,3},{3,2},{4,0},{5,1},{6,7},{7,6},{8,12},{9,13},{10,... | collective-permute-start | bytes 3145736 | tf_op jit(solution)/shard_map/ppermute | solution.py:688
  70.9 14.6 %attn_bwd.1 = (bf16[2048,1536]{1,0:T(8,128)(2,1)S(1)}, bf16[8,32,2176]{2,1,0:T(8,128)(2,1)S(1)}, bf16[8,32,2176]{2,1,0:T(8,128)(2,1)S(1)}) custom-call(s32[2]{0:T(128)S(1)} %pad_add_fusion.place, bf16[2048,1536]{1,0:T(8,128)(2,1)} %get-tuple-element.85.joined, bf16[2048,512]{1,0:T(8,128)(2,1)} %get-tuple-element.95.dc, ...), custom_call_target="tpu_custom_call" | custom-call | flops 103079215104 | bytes 1 | tf_op jit(solution)/shard_map/attn_bwd/pallas_call | solution.py:431
  87.0 4.7 %in_grad.2.refs_0_ = bf16[2048,512]{1,0:T(8,128)(2,1)} custom-call(bf16[2048,1536]{1,0:T(8,128)(2,1)S(1)} %get-tuple-element.104.dj, bf16[2048,512]{1,0:T(8,128)(2,1)} %tok.5, bf16[2048,512]{1,0:T(8,128)(2,1)} %get-tuple-element.114.dattn, bf16[512,1536]{1,0:T(8,128)(2,1)S(1)} %copy-done.1, bf16[16,512]{1,0:T(8,128)(2,1)S(1)} %concatenate.16.vecs), custom_call_target="tpu_custom_call" | custom-call | flops 12884901888 | bytes 1 | tf_op jit(solution)/shard_map/in_grad/pallas_call | solution.py:464
  92.5 1.6 %collective-permute-start.6 = (bf16[4,32,2176]{2,1,0:T(8,128)(2,1)S(1)}, bf16[4,32,2176]{2,1,0:T(8,128)(2,1)S(1)}, u32[]{:S(2)}, u32[]{:S(2)}) collective-permute-start(bf16[4,32,2176]{2,1,0:T(8,128)(2,1)S(1)} %get-tuple-element.112), channel_id=1, source_target_pairs={{0,1},{1,0},{2,6},{3,7},{4,5},{5,4},{6,2},{7,3},{8,9},{9,8},{10,14... | collective-permute-start | bytes 1671176 | tf_op jit(solution)/shard_map/ppermute | solution.py:688
  94.1 4.7 %in_grad.3 = bf16[2048,512]{1,0:T(8,128)(2,1)} custom-call(bf16[2048,1536]{1,0:T(8,128)(2,1)S(1)} %get-tuple-element.104.dj, bf16[2048,512]{1,0:T(8,128)(2,1)} %tok.5, bf16[2048,512]{1,0:T(8,128)(2,1)} %get-tuple-element.114.dattn, bf16[512,1536]{1,0:T(8,128)(2,1)S(1)} %copy-done.1, ...), custom_call_target="tpu_custom_call", output_to_operand_aliasing={{}: (5, {})} | custom-call | flops 12884901888 | bytes 1 | tf_op jit(solution)/shard_map/in_grad/pallas_call | solution.py:464
  99.5 1.6 %collective-permute-start.9 = (bf16[1,256,512]{2,1,0:T(8,128)(2,1)S(1)}, bf16[1,256,512]{2,1,0:T(8,128)(2,1)S(1)}, u32[]{:S(2)}, u32[]{:S(2)}) collective-permute-start(bf16[1,256,512]{2,1,0:T(8,128)(2,1)S(1)} %get-tuple-element.120), channel_id=1, source_target_pairs={{0,8},{1,9},{2,6},{3,7},{4,12},{5,13},{6,2},{7,3},{8,0},{9,1},{10,... | collective-permute-start | bytes 786440 | tf_op jit(solution)/shard_map/ppermute | solution.py:688
  101.1 1.1 slice.9
  102.9 1.5 collective-permute-start.8
  106.0 2.6 %collective-permute-start.12 = (bf16[1,256,512]{2,1,0:T(8,128)(2,1)S(1)}, bf16[1,256,512]{2,1,0:T(8,128)(2,1)S(1)}, u32[]{:S(2)}, u32[]{:S(2)}) collective-permute-start(bf16[1,256,512]{2,1,0:T(8,128)(2,1)S(1)} %add_convert_fusion.1), channel_id=1, source_target_pairs={{0,16},{1,17},{2,18},{3,19},{4,20},{5,21},{6,22},{7,23},{8,24},{9,... | collective-permute-start | bytes 786440 | tf_op jit(solution)/shard_map/ppermute | solution.py:688
  108.6 1.4 collective-permute-done.8.b
  110.7 1.3 collective-permute-start.10
  112.0 6.1 %layer_out.2.refs_0_ = bf16[2048,512]{1,0:T(8,128)(2,1)} custom-call(bf16[2048,1024]{1,0:T(8,128)(2,1)} %get-tuple-element.83.own, f32[2048,512]{1,0:T(8,128)} %get-tuple-element.135.resid, bf16[2048,1024]{1,0:T(8,128)(2,1)} %get-tuple-element.126.oth, bf16[1024,512]{1,0:T(8,128)(2,1)} %down.7, bf16[1024,512]{1,0:T(8,128)(2,1)} %pad_maximum_fusion.down_oth, ...), custom_call_target="tpu_custom_call" | custom-call | flops 17179869184 | bytes 1 | tf_op jit(solution)/shard_map/layer_out/pallas_call | solution.py:464
  118.2 4.7 %collective-permute-start.11 = (bf16[1,32,2176]{2,1,0:T(8,128)(2,1)S(1)}, bf16[1,32,2176]{2,1,0:T(8,128)(2,1)S(1)}, u32[]{:S(2)}, u32[]{:S(2)}) collective-permute-start(bf16[1,32,2176]{2,1,0:T(8,128)(2,1)S(1)} %add_convert_fusion.3), channel_id=1, source_target_pairs={{0,16},{1,17},{2,10},{3,11},{4,20},{5,21},{6,14},{7,15},{8,24},{9,... | collective-permute-start | bytes 417800 | tf_op jit(solution)/shard_map/ppermute | solution.py:688
  123.5 3.9 %collective-permute-done.11 = bf16[1,32,2176]{2,1,0:T(8,128)(2,1)S(1)} collective-permute-done((bf16[1,32,2176]{2,1,0:T(8,128)(2,1)S(1)}, bf16[1,32,2176]{2,1,0:T(8,128)(2,1)S(1)}, u32[]{:S(2)}, u32[]{:S(2)}) %collective-permute-start.11) | collective-permute-done | bytes 139296 | tf_op jit(solution)/shard_map/ppermute | solution.py:688
  128.1 3.3 %collective-permute-done.14 = bf16[1,256,512]{2,1,0:T(8,128)(2,1)S(1)} collective-permute-done((bf16[1,256,512]{2,1,0:T(8,128)(2,1)S(1)}, bf16[1,256,512]{2,1,0:T(8,128)(2,1)S(1)}, u32[]{:S(2)}, u32[]{:S(2)}) %collective-permute-start.14) | collective-permute-done | bytes 262176 | tf_op jit(solution)/shard_map/ppermute | solution.py:688
  131.4 1.2 collective-permute-done.13
  133.3 2.6 %collective-permute-start.18 = (bf16[2,256,512]{2,1,0:T(8,128)(2,1)S(1)}, bf16[2,256,512]{2,1,0:T(8,128)(2,1)S(1)}, u32[]{:S(2)}, u32[]{:S(2)}) collective-permute-start(bf16[2,256,512]{2,1,0:T(8,128)(2,1)S(1)} %pad_maximum_fusion.2.refs_0_), channel_id=1, source_target_pairs={{0,2},{1,3},{2,0},{3,1},{4,6},{5,7},{6,4},{7,5},{8,10},{9,11},{10,... | collective-permute-start | bytes 1572872 | tf_op jit(solution)/shard_map/ppermute | solution.py:688
  135.9 4.1 %collective-permute-done.15 = bf16[2,32,2176]{2,1,0:T(8,128)(2,1)S(1)} collective-permute-done((bf16[2,32,2176]{2,1,0:T(8,128)(2,1)S(1)}, bf16[2,32,2176]{2,1,0:T(8,128)(2,1)S(1)}, u32[]{:S(2)}, u32[]{:S(2)}) %collective-permute-start.15) | collective-permute-done | bytes 278560 | tf_op jit(solution)/shard_map/ppermute | solution.py:688
  140.8 6.1 %layer_out.3 = bf16[2048,512]{1,0:T(8,128)(2,1)} custom-call(bf16[2048,1024]{1,0:T(8,128)(2,1)} %get-tuple-element.83.own, f32[2048,512]{1,0:T(8,128)} %get-tuple-element.135.resid, bf16[2048,1024]{1,0:T(8,128)(2,1)} %get-tuple-element.126.oth, bf16[1024,512]{1,0:T(8,128)(2,1)} %down.7, ...), custom_call_target="tpu_custom_call", output_to_operand_aliasing={{}: (6, {})} | custom-call | flops 17179869184 | bytes 1 | tf_op jit(solution)/shard_map/layer_out/pallas_call | solution.py:464
  147.0 1.2 collective-permute-start.19
  148.2 1.5 collective-permute-done.19.refs_3_
  149.7 3.0 %finish_ffn.1 = (f32[512,1024]{1,0:T(8,128)}, f32[1024,512]{1,0:T(8,128)}) custom-call(s32[14]{0:T(128)S(1)} %stack.88.at, bf16[2,256,512]{2,1,0:T(8,128)(2,1)S(1)} %pad_maximum_fusion.2.refs_0_, bf16[2,256,512]{2,1,0:T(8,128)(2,1)S(1)} %collective-permute-done.17.refs_1_, bf16[2,256,512]{2,1,0:T(8,128)(2,1)S(1)} %collective-permute-done.18.refs_2_, ...), custom_call_target="tpu_custom_call" | custom-call | bytes 1 | tf_op jit(solution)/shard_map/finish_ffn/pallas_call | solution.py:559
  153.3 1.4 collective-permute-done.21.refs_3_
  154.6 3.1 %finish_rest.1 = (f32[512,1536]{1,0:T(8,128)}, f32[2,512]{1,0:T(2,128)}, f32[512,512]{1,0:T(8,128)}, f32[1,512]{1,0:T(1,128)}, f32[1,512]{1,0:T(1,128)}, /*index...) custom-call(s32[14]{0:T(128)S(1)} %stack.88.at, ...), custom_call_target="tpu_custom_call" | custom-call | bytes 1 | tf_op jit(solution)/shard_map/finish_rest/pallas_call | solution.py:631
  (79 shorter events, 11.0 us)
Async XLA Ops:
  0.6 5.1 %copy-start.5 = (bf16[512]{0:T(512)(128)(2,1)S(1)}, bf16[512]{0:T(512)(128)(2,1)}, u32[]{:S(2)}) copy-start(bf16[512]{0:T(512)(128)(2,1)} %param.17) | copy-start | bytes 3076
  0.7 5.1 %copy-start.9 = (bf16[512]{0:T(512)(128)(2,1)S(1)}, bf16[512]{0:T(512)(128)(2,1)}, u32[]{:S(2)}) copy-start(bf16[512]{0:T(512)(128)(2,1)} %param.23) | copy-start | bytes 3076
  0.7 5.2 %copy-start.10 = (bf16[512]{0:T(512)(128)(2,1)S(1)}, bf16[512]{0:T(512)(128)(2,1)}, u32[]{:S(2)}) copy-start(bf16[512]{0:T(512)(128)(2,1)} %param.24) | copy-start | bytes 3076
  0.7 5.2 %copy-start.11 = (bf16[512]{0:T(512)(128)(2,1)S(1)}, bf16[512]{0:T(512)(128)(2,1)}, u32[]{:S(2)}) copy-start(bf16[512]{0:T(512)(128)(2,1)} %param.28) | copy-start | bytes 3076
  0.7 5.2 %copy-start.7 = (bf16[2,512]{1,0:T(2,128)(2,1)S(1)}, bf16[2,512]{1,0:T(2,128)(2,1)}, u32[]{:S(2)}) copy-start(bf16[2,512]{1,0:T(2,128)(2,1)} %param.20) | copy-start | bytes 6148
  0.7 5.2 %copy-start.2 = (s32[16,128]{1,0:T(8,128)S(1)}, s32[16,128]{1,0:T(8,128)}, u32[]{:S(2)}) copy-start(s32[16,128]{1,0:T(8,128)} %param.16) | copy-start | bytes 24580
  2.7 35.4 %collective-permute-start = (bf16[1040,512]{1,0:T(8,128)(2,1)S(1)}, bf16[1040,512]{1,0:T(8,128)(2,1)}, u32[]{:S(2)}, u32[]{:S(2)}) collective-permute-start(bf16[1040,512]{1,0:T(8,128)(2,1)S(1)} %fetch.1), channel_id=1, source_target_pairs={{0,1},{1,0},{2,3},{3,2},{4,5},{5,4},{6,7},{7,6},{8,9},{9,8},{10,11... | collective-permute-start | bytes 3194888 | tf_op jit(solution)/shard_map/ppermute | solution.py:688
  38.2 3.0 %collective-permute-start.1 = (bf16[1040,512]{1,0:T(8,128)(2,1)}, bf16[1040,512]{1,0:T(8,128)(2,1)S(1)}, u32[]{:S(2)}, u32[]{:S(2)}) collective-permute-start(bf16[1040,512]{1,0:T(8,128)(2,1)} %collective-permute-done.w_send), channel_id=1, source_target_pairs={{0,2},{1,3},{2,0},{3,1},{4,6},{5,7},{6,4},{7,5},{8,10},{9,11},{10,... | collective-permute-start | bytes 3194888 | tf_op jit(solution)/shard_map/ppermute | solution.py:688
  38.3 26.5 %collective-permute-start.2 = (bf16[4,256,512]{2,1,0:T(8,128)(2,1)}, bf16[4,256,512]{2,1,0:T(8,128)(2,1)S(1)}, u32[]{:S(2)}, u32[]{:S(2)}) collective-permute-start(bf16[4,256,512]{2,1,0:T(8,128)(2,1)} %get-tuple-element.86), channel_id=1, source_target_pairs={{0,2},{1,3},{2,0},{3,1},{4,6},{5,7},{6,4},{7,5},{8,10},{9,11},{10,... | collective-permute-start | bytes 3145736 | tf_op jit(solution)/shard_map/ppermute | solution.py:688
  41.1 23.2 %copy-start = (bf16[1040,512]{1,0:T(8,128)(2,1)}, bf16[1040,512]{1,0:T(8,128)(2,1)S(1)}, u32[]{:S(2)}) copy-start(bf16[1040,512]{1,0:T(8,128)(2,1)S(1)} %collective-permute-done.1.w_keep) | copy-start | bytes 3194884
  64.4 3.1 %collective-permute-start.3 = (bf16[4,256,512]{2,1,0:T(8,128)(2,1)}, bf16[4,256,512]{2,1,0:T(8,128)(2,1)}, u32[]{:S(2)}, u32[]{:S(2)}) collective-permute-start(bf16[4,256,512]{2,1,0:T(8,128)(2,1)} %get-tuple-element.93), channel_id=1, source_target_pairs={{0,2},{1,3},{2,0},{3,1},{4,6},{5,7},{6,4},{7,5},{8,10},{9,11},{10,... | collective-permute-start | bytes 3145736 | tf_op jit(solution)/shard_map/ppermute | solution.py:688
  69.3 16.3 %collective-permute-start.5 = (bf16[4,256,512]{2,1,0:T(8,128)(2,1)S(1)}, bf16[4,256,512]{2,1,0:T(8,128)(2,1)S(1)}, u32[]{:S(2)}, u32[]{:S(2)}) collective-permute-start(bf16[4,256,512]{2,1,0:T(8,128)(2,1)S(1)} %get-tuple-element.106), channel_id=1, source_target_pairs={{0,4},{1,5},{2,3},{3,2},{4,0},{5,1},{6,7},{7,6},{8,12},{9,13},{10,... | collective-permute-start | bytes 3145736 | tf_op jit(solution)/shard_map/ppermute | solution.py:688
  85.5 6.2 %collective-permute-start.4 = (bf16[8,32,2176]{2,1,0:T(8,128)(2,1)S(1)}, bf16[8,32,2176]{2,1,0:T(8,128)(2,1)S(1)}, u32[]{:S(2)}, u32[]{:S(2)}) collective-permute-start(bf16[8,32,2176]{2,1,0:T(8,128)(2,1)S(1)} %get-tuple-element.103), channel_id=1, source_target_pairs={{0,2},{1,3},{2,0},{3,1},{4,6},{5,7},{6,4},{7,5},{8,10},{9,11},{10,... | collective-permute-start | bytes 3342344 | tf_op jit(solution)/shard_map/ppermute | solution.py:688
  86.4 12.4 %collective-permute-start.7 = (bf16[2,256,512]{2,1,0:T(8,128)(2,1)S(1)}, bf16[2,256,512]{2,1,0:T(8,128)(2,1)S(1)}, u32[]{:S(2)}, u32[]{:S(2)}) collective-permute-start(bf16[2,256,512]{2,1,0:T(8,128)(2,1)S(1)} %get-tuple-element.113), channel_id=1, source_target_pairs={{0,1},{1,0},{2,10},{3,11},{4,5},{5,4},{6,14},{7,15},{8,9},{9,8},{1... | collective-permute-start | bytes 1572872 | tf_op jit(solution)/shard_map/ppermute | solution.py:688
  92.5 9.7 %collective-permute-start.6 = (bf16[4,32,2176]{2,1,0:T(8,128)(2,1)S(1)}, bf16[4,32,2176]{2,1,0:T(8,128)(2,1)S(1)}, u32[]{:S(2)}, u32[]{:S(2)}) collective-permute-start(bf16[4,32,2176]{2,1,0:T(8,128)(2,1)S(1)} %get-tuple-element.112), channel_id=1, source_target_pairs={{0,1},{1,0},{2,6},{3,7},{4,5},{5,4},{6,2},{7,3},{8,9},{9,8},{10,14... | collective-permute-start | bytes 1671176 | tf_op jit(solution)/shard_map/ppermute | solution.py:688
  98.8 5.6 %slice-start = ((bf16[1040,512]{1,0:T(8,128)(2,1)}), bf16[512,512]{1,0:T(8,128)(2,1)S(1)}, s32[]{:S(2)}) async-start(bf16[1040,512]{1,0:T(8,128)(2,1)} %copy-done), calls=%async_computation | async-start | bytes 1048576 | tf_op jit(solution)/shard_map/slice | solution.py:739
  99.5 6.4 %collective-permute-start.9 = (bf16[1,256,512]{2,1,0:T(8,128)(2,1)S(1)}, bf16[1,256,512]{2,1,0:T(8,128)(2,1)S(1)}, u32[]{:S(2)}, u32[]{:S(2)}) collective-permute-start(bf16[1,256,512]{2,1,0:T(8,128)(2,1)S(1)} %get-tuple-element.120), channel_id=1, source_target_pairs={{0,8},{1,9},{2,6},{3,7},{4,12},{5,13},{6,2},{7,3},{8,0},{9,1},{10,... | collective-permute-start | bytes 786440 | tf_op jit(solution)/shard_map/ppermute | solution.py:688
  102.9 7.1 %collective-permute-start.8 = (bf16[2,32,2176]{2,1,0:T(8,128)(2,1)S(1)}, bf16[2,32,2176]{2,1,0:T(8,128)(2,1)S(1)}, u32[]{:S(2)}, u32[]{:S(2)}) collective-permute-start(bf16[2,32,2176]{2,1,0:T(8,128)(2,1)S(1)} %get-tuple-element.119), channel_id=1, source_target_pairs={{0,8},{1,9},{2,3},{3,2},{4,12},{5,13},{6,7},{7,6},{8,0},{9,1},{10,... | collective-permute-start | bytes 835592 | tf_op jit(solution)/shard_map/ppermute | solution.py:688
  106.0 16.9 %collective-permute-start.12 = (bf16[1,256,512]{2,1,0:T(8,128)(2,1)S(1)}, bf16[1,256,512]{2,1,0:T(8,128)(2,1)S(1)}, u32[]{:S(2)}, u32[]{:S(2)}) collective-permute-start(bf16[1,256,512]{2,1,0:T(8,128)(2,1)S(1)} %add_convert_fusion.1), channel_id=1, source_target_pairs={{0,16},{1,17},{2,18},{3,19},{4,20},{5,21},{6,22},{7,23},{8,24},{9,... | collective-permute-start | bytes 786440 | tf_op jit(solution)/shard_map/ppermute | solution.py:688
  110.7 7.5 %collective-permute-start.10 = (bf16[1,32,2176]{2,1,0:T(8,128)(2,1)S(1)}, bf16[1,32,2176]{2,1,0:T(8,128)(2,1)S(1)}, u32[]{:S(2)}, u32[]{:S(2)}) collective-permute-start(bf16[1,32,2176]{2,1,0:T(8,128)(2,1)S(1)} %get-tuple-element.124), channel_id=1, source_target_pairs={{0,4},{1,5},{2,18},{3,19},{4,0},{5,1},{6,22},{7,23},{8,12},{9,13},... | collective-permute-start | bytes 417800 | tf_op jit(solution)/shard_map/ppermute | solution.py:688
  118.2 9.3 %collective-permute-start.11 = (bf16[1,32,2176]{2,1,0:T(8,128)(2,1)S(1)}, bf16[1,32,2176]{2,1,0:T(8,128)(2,1)S(1)}, u32[]{:S(2)}, u32[]{:S(2)}) collective-permute-start(bf16[1,32,2176]{2,1,0:T(8,128)(2,1)S(1)} %add_convert_fusion.3), channel_id=1, source_target_pairs={{0,16},{1,17},{2,10},{3,11},{4,20},{5,21},{6,14},{7,15},{8,24},{9,... | collective-permute-start | bytes 417800 | tf_op jit(solution)/shard_map/ppermute | solution.py:688
  123.0 8.4 %collective-permute-start.14 = (bf16[1,256,512]{2,1,0:T(8,128)(2,1)S(1)}, bf16[1,256,512]{2,1,0:T(8,128)(2,1)S(1)}, u32[]{:S(2)}, u32[]{:S(2)}) collective-permute-start(bf16[1,256,512]{2,1,0:T(8,128)(2,1)S(1)} %add_convert_fusion), channel_id=1, source_target_pairs={{0,8},{1,9},{2,6},{3,7},{4,12},{5,13},{6,2},{7,3},{8,0},{9,1},{10,... | collective-permute-start | bytes 786440 | tf_op jit(solution)/shard_map/ppermute | solution.py:688
  127.5 5.1 %collective-permute-start.13 = (bf16[1,32,2176]{2,1,0:T(8,128)(2,1)S(1)}, bf16[1,32,2176]{2,1,0:T(8,128)(2,1)S(1)}, u32[]{:S(2)}, u32[]{:S(2)}) collective-permute-start(bf16[1,32,2176]{2,1,0:T(8,128)(2,1)S(1)} %add_convert_fusion.2), channel_id=1, source_target_pairs={{0,4},{1,5},{2,18},{3,19},{4,0},{5,1},{6,22},{7,23},{8,12},{9,13},... | collective-permute-start | bytes 417800 | tf_op jit(solution)/shard_map/ppermute | solution.py:688
  132.6 7.3 %collective-permute-start.15 = (bf16[2,32,2176]{2,1,0:T(8,128)(2,1)S(1)}, bf16[2,32,2176]{2,1,0:T(8,128)(2,1)S(1)}, u32[]{:S(2)}, u32[]{:S(2)}) collective-permute-start(bf16[2,32,2176]{2,1,0:T(8,128)(2,1)S(1)} %pad_maximum_fusion.3), channel_id=1, source_target_pairs={{0,8},{1,9},{2,3},{3,2},{4,12},{5,13},{6,7},{7,6},{8,0},{9,1},{10,... | collective-permute-start | bytes 835592 | tf_op jit(solution)/shard_map/ppermute | solution.py:688
  132.7 14.2 %collective-permute-start.17 = (bf16[2,256,512]{2,1,0:T(8,128)(2,1)S(1)}, bf16[2,256,512]{2,1,0:T(8,128)(2,1)S(1)}, u32[]{:S(2)}, u32[]{:S(2)}) collective-permute-start(bf16[2,256,512]{2,1,0:T(8,128)(2,1)S(1)} %pad_maximum_fusion.2.refs_0_), channel_id=1, source_target_pairs={{0,4},{1,5},{2,10},{3,11},{4,0},{5,1},{6,14},{7,15},{8,12},{9,13},... | collective-permute-start | bytes 1572872 | tf_op jit(solution)/shard_map/ppermute | solution.py:688
  133.3 14.9 %collective-permute-start.18 = (bf16[2,256,512]{2,1,0:T(8,128)(2,1)S(1)}, bf16[2,256,512]{2,1,0:T(8,128)(2,1)S(1)}, u32[]{:S(2)}, u32[]{:S(2)}) collective-permute-start(bf16[2,256,512]{2,1,0:T(8,128)(2,1)S(1)} %pad_maximum_fusion.2.refs_0_), channel_id=1, source_target_pairs={{0,2},{1,3},{2,0},{3,1},{4,6},{5,7},{6,4},{7,5},{8,10},{9,11},{10,... | collective-permute-start | bytes 1572872 | tf_op jit(solution)/shard_map/ppermute | solution.py:688
  140.0 12.6 %collective-permute-start.16 = (bf16[4,32,2176]{2,1,0:T(8,128)(2,1)S(1)}, bf16[4,32,2176]{2,1,0:T(8,128)(2,1)S(1)}, u32[]{:S(2)}, u32[]{:S(2)}) collective-permute-start(bf16[4,32,2176]{2,1,0:T(8,128)(2,1)S(1)} %pad_maximum_fusion.1.refs_0_), channel_id=1, source_target_pairs={{0,1},{1,0},{2,6},{3,7},{4,5},{5,4},{6,2},{7,3},{8,9},{9,8},{10,14... | collective-permute-start | bytes 1671176 | tf_op jit(solution)/shard_map/ppermute | solution.py:688
  146.9 6.1 %copy-start.4 = (bf16[512]{0:T(512)(128)(2,1)S(1)}, bf16[512]{0:T(512)(128)(2,1)}, u32[]{:S(2)}) copy-start(bf16[512]{0:T(512)(128)(2,1)} %param.18) | copy-start | bytes 3076
  146.9 6.1 %copy-start.6 = (bf16[512]{0:T(512)(128)(2,1)S(1)}, bf16[512]{0:T(512)(128)(2,1)}, u32[]{:S(2)}) copy-start(bf16[512]{0:T(512)(128)(2,1)} %param.17) | copy-start | bytes 3076
  147.0 2.7 %collective-permute-start.19 = (bf16[2,256,512]{2,1,0:T(8,128)(2,1)S(1)}, bf16[2,256,512]{2,1,0:T(8,128)(2,1)S(1)}, u32[]{:S(2)}, u32[]{:S(2)}) collective-permute-start(bf16[2,256,512]{2,1,0:T(8,128)(2,1)S(1)} %collective-permute-done.17.refs_1_), channel_id=1, source_target_pairs={{0,2},{1,3},{2,0},{3,1},{4,6},{5,7},{6,4},{7,5},{8,10},{9,11},{10,... | collective-permute-start | bytes 1572872 | tf_op jit(solution)/shard_map/ppermute | solution.py:688
  148.2 5.1 %collective-permute-start.20 = (bf16[4,32,2176]{2,1,0:T(8,128)(2,1)S(1)}, bf16[4,32,2176]{2,1,0:T(8,128)(2,1)S(1)}, u32[]{:S(2)}, u32[]{:S(2)}) collective-permute-start(bf16[4,32,2176]{2,1,0:T(8,128)(2,1)S(1)} %pad_maximum_fusion.1.refs_0_), channel_id=1, source_target_pairs={{0,2},{1,3},{2,0},{3,1},{4,6},{5,7},{6,4},{7,5},{8,10},{9,11},{10,... | collective-permute-start | bytes 1671176 | tf_op jit(solution)/shard_map/ppermute | solution.py:688
  152.7 2.0 %collective-permute-start.21 = (bf16[4,32,2176]{2,1,0:T(8,128)(2,1)S(1)}, bf16[4,32,2176]{2,1,0:T(8,128)(2,1)S(1)}, u32[]{:S(2)}, u32[]{:S(2)}) collective-permute-start(bf16[4,32,2176]{2,1,0:T(8,128)(2,1)S(1)} %collective-permute-done.16.refs_1_), channel_id=1, source_target_pairs={{0,2},{1,3},{2,0},{3,1},{4,6},{5,7},{6,4},{7,5},{8,10},{9,11},{10,... | collective-permute-start | bytes 1671176 | tf_op jit(solution)/shard_map/ppermute | solution.py:688
  (3 other events, 11.7 us)
